TPU v7x, 32 devices: a whole 2x2x4 slice. The times are simulated.
32 devices in a mesh: depth: 8 (over y, x, core), freq: 4 (over z).
Axes of the slice: x: 2, y: 2, z: 4, core: 2. Of those that a mesh axis runs over, the one named last changes fastest.
Arguments:
- source_field: float32 [4, 2, 64, 2048], P('freq'), may hold values from -6 to 6
- receiver_data: float32 [4, 2, 64, 2048], P('freq'), may hold values from -6 to 6
- propagator: bfloat16 [4, 8, 16, 6, 2, 128, 128], P('freq', 'depth'), may hold values from -0.102062073 to 0.102062073
- block_columns: int32 [8, 16, 6], P('depth'), may hold values from 0 to 15, as said below
- image_pairs: int32 [8, 8, 2], P('depth'), may hold values from 0 to 15, as said below
Outputs:
- image: float32 [8, 8, 128, 128], P('depth', 'freq')
Inputs may be any that keep to these rules, and one draw needn't show every extreme that they name: `block_columns`: each block row lists 6 distinct block columns, its own among them. `image_pairs`: the two block indices of a pair differ by at most one.
All inputs are finite; a program needn't handle non-finite values.
Results may differ from a plain program's by a relative error of at most 0.0003.
Values sent between devices are 32-bit elements; how exact they have to be, the bound alone decides.
No kernel may reach another device: no remote copies, remote signals or barrier semaphores. Data moves between devices by JAX's collectives and lax.ppermute only.
A program may use at most 64 MiB of HBM per device.

v0:
```python
import math

import jax
import jax.numpy as jnp
from jax import lax
from jax.sharding import PartitionSpec as P

NG = 8


def passed_along(value, axis, steps):
    count = lax.axis_size(axis)
    initial, last = (max(0, -steps), min(count, count - steps))
    return lax.ppermute(value, axis, [(source, source + steps) for source in range(initial, last)])


def edge_taper(lateral):
    position = jnp.arange(lateral, dtype=jnp.int32)
    distance = jnp.minimum(position, lateral - 1 - position).astype(jnp.float32)
    edge_cells = lateral // 32
    edge_ramp = jnp.maximum(0.0, 1.0 - distance / edge_cells)
    return 1.0 - 0.3 * edge_ramp * edge_ramp


def propagate(field, level_operator, level_columns, taper_row):
    lane_count, shot_count, lateral = field.shape
    block_rows = level_columns.shape[0]
    blocks = field.reshape(lane_count, shot_count, block_rows, lateral // block_rows)
    picked = jnp.take(blocks, level_columns, axis=2)
    operator_real = level_operator[:, :, 0].astype(jnp.float32)
    operator_imag = level_operator[:, :, 1].astype(jnp.float32)
    real_part = jnp.einsum(
        "cbrjk,rjkm->cbrm", picked, operator_real, precision=lax.Precision.HIGHEST
    )
    imag_part = jnp.einsum(
        "cbrjk,rjkm->cbrm", picked, operator_imag, precision=lax.Precision.HIGHEST
    )
    source_real = real_part[0] - imag_part[1]
    source_imag = real_part[1] + imag_part[0]
    receiver_real = real_part[2] + imag_part[3]
    receiver_imag = real_part[3] - imag_part[2]
    combined = jnp.stack([source_real, source_imag, receiver_real, receiver_imag])
    return combined.reshape(lane_count, shot_count, lateral) * taper_row


def image_level(field, level_pairs, block_size):
    lane_count, shot_count, lateral = field.shape
    blocks = field.reshape(lane_count, shot_count, lateral // block_size, block_size)
    source_blocks = jnp.take(blocks[0:2], level_pairs[:, 0], axis=2)
    receiver_blocks = jnp.take(blocks[2:4], level_pairs[:, 1], axis=2)
    return jnp.einsum(
        "csik,csim->ikm", source_blocks, receiver_blocks, precision=lax.Precision.HIGHEST
    )


def shards(source_field, receiver_data, propagator, block_columns, image_pairs):
    depth_count = lax.axis_size("depth")
    depth_index = lax.axis_index("depth")
    freq_count = lax.axis_size("freq")
    shots_all = source_field.shape[2]
    lateral = source_field.shape[3]
    levels_here = block_columns.shape[0]
    pair_count = image_pairs.shape[1]
    block_size = propagator.shape[-1]
    group_shots = shots_all // NG
    turns = depth_count + NG - 1
    taper_row = edge_taper(lateral)
    image_scale = 1.0 / math.sqrt(2.0 * shots_all * freq_count)

    def advance(field):
        field = propagate(field, propagator[0, 0], block_columns[0], taper_row)
        level_images = [image_level(field, image_pairs[0], block_size)]
        return (field, jnp.stack(level_images))

    def spare_turn(field):
        return (
            jnp.zeros_like(field),
            jnp.zeros((levels_here, pair_count, block_size, block_size), jnp.float32),
        )

    def one_turn(turn_index, loop_state):
        incoming, images = loop_state
        group_index = turn_index - depth_index
        active = jnp.logical_and(group_index >= 0, group_index < NG)
        shot_start = jnp.clip(group_index, 0, NG - 1) * group_shots

        def surface_group():
            source_part = lax.dynamic_slice_in_dim(source_field[0], shot_start, group_shots, 1)
            receiver_part = lax.dynamic_slice_in_dim(receiver_data[0], shot_start, group_shots, 1)
            return jnp.concatenate([source_part, receiver_part], axis=0)

        def from_above():
            return incoming

        entering = lax.cond(depth_index == 0, surface_group, from_above)
        leaving, fresh_images = lax.cond(active, advance, spare_turn, entering)
        passed = passed_along(leaving, "depth", 1)
        return (passed, images + fresh_images)

    initial = (
        jnp.zeros((4, group_shots, lateral), jnp.float32),
        jnp.zeros((levels_here, pair_count, block_size, block_size), jnp.float32),
    )
    unused, images = lax.fori_loop(0, turns, one_turn, initial)
    return lax.psum_scatter(images * image_scale, "freq", scatter_dimension=1, tiled=True)


def solution(mesh):
    placed = (
        P("freq", None, None, None),
        P("freq", None, None, None),
        P("freq", "depth", None, None, None, None, None),
        P("depth", None, None),
        P("depth", None, None),
    )
    return jax.shard_map(
        shards,
        mesh=mesh,
        in_specs=placed,
        out_specs=P("depth", "freq", None, None),
        check_vma=False,
    )
```

profile of v0, /device:TPU:0, one launch (start us, length us, event | category | flops | bytes accessed | tf_op | source)
XLA Modules:
  0.0 323.8 jit_solution(3420622824151670975)
XLA Ops:
  6.5 8.1 %copy.15 = bf16[1,1,16,6,2,128,128]{6,5,3,2,4,1,0:T(8,128)(2,1)} copy(bf16[1,1,16,6,2,128,128]{6,5,4,3,2,1,0:T(8,128)(2,1)} %param.15) | data formatting | bytes 12582912
  14.7 247.6 %while.20 = (s32[]{:T(128)}, f32[4,8,2048]{2,1,0:T(8,128)S(1)}, f32[1,8,128,128]{3,2,1,0:T(8,128)S(1)}, s32[]{:T(128)}, pred[]{:T(512)}, /*index=5*/f32[1,2,64,2...) while((s32[]{:T(128)}, f32[4,8,2048]{2,1,0:T(8,128)S(1)}, ...), condition=%wide.region_5.7_spmd.clone, body=%wide.region_0.6_spmd.clone.sunk | while | flops 1234622464 | bytes 19587604 | solution.py:104
  15.8 11.8 %conditional.7 = (f32[4,8,2048]{2,1,0:T(8,128)}, f32[1,8,128,128]{3,2,1,0:T(8,128)S(1)}) conditional(s32[]{:T(128)} %convert_element_type.43, () %tuple.81, (s32[1,16,6]{1,2,0:T(8,128)S(1)}, f32[4,8,2048]{2,1,0:T(8,128)S(1)}, bf16[1,1,16,6,2,128,128]{6,5,3,2,4,1,0:T(8,128)(2,1)}, f32[]{:T(128)}, s32[1,8,2]{1,2,0:T(2,128)S(1)}, ...), branch_computations={%region_3.3_spmd, %region_4.5_spmd.clone} | conditional | flops 1234282496 | bytes 15909012 | solution.py:96
  16.9 3.4 %fusion.11 = f32[4,8,16,128]{3,1,0,2:T(8,128)S(1)} fusion(bf16[16,6,2,128,128]{4,3,1,0,2:T(8,128)(2,1)} %bitcast.110, f32[16,6,4,8,128]{4,3,2,1,0:T(8,128)S(1)} %bitcast.108, pred[16,6]{1,0:T(8,128)(4,1)S(1)} %copy.21), kind=kOutput, calls=%fused_computation.17 | convolution fusion | flops 604372992 | bytes 4980832 | tf_op jit(solution)/shard_map/while/body/eval_jaxpr/cond/branch_1_fun/cbrjk,rjkm->cbrm/dot_general | solution.py:35
  20.2 3.4 %fusion.8 = f32[4,8,16,128]{3,1,0,2:T(8,128)S(1)} fusion(bf16[16,6,2,128,128]{4,3,1,0,2:T(8,128)(2,1)} %bitcast.111, f32[16,6,4,8,128]{4,3,2,1,0:T(8,128)S(1)} %bitcast.109, pred[16,6]{1,0:T(8,128)(4,1)S(1)} %copy.21), kind=kOutput, calls=%fused_computation.16 | convolution fusion | flops 604372992 | bytes 4980832 | tf_op jit(solution)/shard_map/while/body/eval_jaxpr/cond/branch_1_fun/cbrjk,rjkm->cbrm/dot_general | solution.py:32
  26.5 1.1 convolution_bitcast_fusion
  27.6 1.3 collective-permute-start
  29.1 1.2 collective-permute-done
  31.3 11.8 %conditional.7 = (f32[4,8,2048]{2,1,0:T(8,128)}, f32[1,8,128,128]{3,2,1,0:T(8,128)S(1)}) conditional(s32[]{:T(128)} %convert_element_type.43, () %tuple.81, (s32[1,16,6]{1,2,0:T(8,128)S(1)}, f32[4,8,2048]{2,1,0:T(8,128)S(1)}, bf16[1,1,16,6,2,128,128]{6,5,3,2,4,1,0:T(8,128)(2,1)}, f32[]{:T(128)}, s32[1,8,2]{1,2,0:T(2,128)S(1)}, ...), branch_computations={%region_3.3_spmd, %region_4.5_spmd.clone} | conditional | flops 1234282496 | bytes 15909012 | solution.py:96
  32.4 3.4 %fusion.11 = f32[4,8,16,128]{3,1,0,2:T(8,128)S(1)} fusion(bf16[16,6,2,128,128]{4,3,1,0,2:T(8,128)(2,1)} %bitcast.110, f32[16,6,4,8,128]{4,3,2,1,0:T(8,128)S(1)} %bitcast.108, pred[16,6]{1,0:T(8,128)(4,1)S(1)} %copy.21), kind=kOutput, calls=%fused_computation.17 | convolution fusion | flops 604372992 | bytes 4980832 | tf_op jit(solution)/shard_map/while/body/eval_jaxpr/cond/branch_1_fun/cbrjk,rjkm->cbrm/dot_general | solution.py:35
  35.7 3.4 %fusion.8 = f32[4,8,16,128]{3,1,0,2:T(8,128)S(1)} fusion(bf16[16,6,2,128,128]{4,3,1,0,2:T(8,128)(2,1)} %bitcast.111, f32[16,6,4,8,128]{4,3,2,1,0:T(8,128)S(1)} %bitcast.109, pred[16,6]{1,0:T(8,128)(4,1)S(1)} %copy.21), kind=kOutput, calls=%fused_computation.16 | convolution fusion | flops 604372992 | bytes 4980832 | tf_op jit(solution)/shard_map/while/body/eval_jaxpr/cond/branch_1_fun/cbrjk,rjkm->cbrm/dot_general | solution.py:32
  42.0 1.1 convolution_bitcast_fusion
  43.1 1.3 collective-permute-start
  44.6 1.2 collective-permute-done
  46.8 11.8 %conditional.7 = (f32[4,8,2048]{2,1,0:T(8,128)}, f32[1,8,128,128]{3,2,1,0:T(8,128)S(1)}) conditional(s32[]{:T(128)} %convert_element_type.43, () %tuple.81, (s32[1,16,6]{1,2,0:T(8,128)S(1)}, f32[4,8,2048]{2,1,0:T(8,128)S(1)}, bf16[1,1,16,6,2,128,128]{6,5,3,2,4,1,0:T(8,128)(2,1)}, f32[]{:T(128)}, s32[1,8,2]{1,2,0:T(2,128)S(1)}, ...), branch_computations={%region_3.3_spmd, %region_4.5_spmd.clone} | conditional | flops 1234282496 | bytes 15909012 | solution.py:96
  47.9 3.4 %fusion.11 = f32[4,8,16,128]{3,1,0,2:T(8,128)S(1)} fusion(bf16[16,6,2,128,128]{4,3,1,0,2:T(8,128)(2,1)} %bitcast.110, f32[16,6,4,8,128]{4,3,2,1,0:T(8,128)S(1)} %bitcast.108, pred[16,6]{1,0:T(8,128)(4,1)S(1)} %copy.21), kind=kOutput, calls=%fused_computation.17 | convolution fusion | flops 604372992 | bytes 4980832 | tf_op jit(solution)/shard_map/while/body/eval_jaxpr/cond/branch_1_fun/cbrjk,rjkm->cbrm/dot_general | solution.py:35
  51.2 3.4 %fusion.8 = f32[4,8,16,128]{3,1,0,2:T(8,128)S(1)} fusion(bf16[16,6,2,128,128]{4,3,1,0,2:T(8,128)(2,1)} %bitcast.111, f32[16,6,4,8,128]{4,3,2,1,0:T(8,128)S(1)} %bitcast.109, pred[16,6]{1,0:T(8,128)(4,1)S(1)} %copy.21), kind=kOutput, calls=%fused_computation.16 | convolution fusion | flops 604372992 | bytes 4980832 | tf_op jit(solution)/shard_map/while/body/eval_jaxpr/cond/branch_1_fun/cbrjk,rjkm->cbrm/dot_general | solution.py:32
  57.5 1.1 convolution_bitcast_fusion
  58.6 3.1 collective-permute-start
  61.9 1.2 collective-permute-done
  64.1 11.8 %conditional.7 = (f32[4,8,2048]{2,1,0:T(8,128)}, f32[1,8,128,128]{3,2,1,0:T(8,128)S(1)}) conditional(s32[]{:T(128)} %convert_element_type.43, () %tuple.81, (s32[1,16,6]{1,2,0:T(8,128)S(1)}, f32[4,8,2048]{2,1,0:T(8,128)S(1)}, bf16[1,1,16,6,2,128,128]{6,5,3,2,4,1,0:T(8,128)(2,1)}, f32[]{:T(128)}, s32[1,8,2]{1,2,0:T(2,128)S(1)}, ...), branch_computations={%region_3.3_spmd, %region_4.5_spmd.clone} | conditional | flops 1234282496 | bytes 15909012 | solution.py:96
  65.2 3.4 %fusion.11 = f32[4,8,16,128]{3,1,0,2:T(8,128)S(1)} fusion(bf16[16,6,2,128,128]{4,3,1,0,2:T(8,128)(2,1)} %bitcast.110, f32[16,6,4,8,128]{4,3,2,1,0:T(8,128)S(1)} %bitcast.108, pred[16,6]{1,0:T(8,128)(4,1)S(1)} %copy.21), kind=kOutput, calls=%fused_computation.17 | convolution fusion | flops 604372992 | bytes 4980832 | tf_op jit(solution)/shard_map/while/body/eval_jaxpr/cond/branch_1_fun/cbrjk,rjkm->cbrm/dot_general | solution.py:35
  68.5 3.4 %fusion.8 = f32[4,8,16,128]{3,1,0,2:T(8,128)S(1)} fusion(bf16[16,6,2,128,128]{4,3,1,0,2:T(8,128)(2,1)} %bitcast.111, f32[16,6,4,8,128]{4,3,2,1,0:T(8,128)S(1)} %bitcast.109, pred[16,6]{1,0:T(8,128)(4,1)S(1)} %copy.21), kind=kOutput, calls=%fused_computation.16 | convolution fusion | flops 604372992 | bytes 4980832 | tf_op jit(solution)/shard_map/while/body/eval_jaxpr/cond/branch_1_fun/cbrjk,rjkm->cbrm/dot_general | solution.py:32
  74.8 1.1 convolution_bitcast_fusion
  75.9 5.5 %collective-permute-start = (f32[4,8,2048]{2,1,0:T(8,128)}, f32[4,8,2048]{2,1,0:T(8,128)S(1)}, u32[]{:S(2)}, u32[]{:S(2)}) collective-permute-start(f32[4,8,2048]{2,1,0:T(8,128)} %get-tuple-element.450), channel_id=1, source_target_pairs={{0,4},{4,8},{8,12},{12,16},{16,20},{20,24},{24,28},{1,5},{5,9},{9,... | collective-permute-start | bytes 786440 | tf_op jit(solution)/shard_map/while/body/eval_jaxpr/ppermute | solution.py:14
  81.6 1.2 collective-permute-done
  83.8 11.8 %conditional.7 = (f32[4,8,2048]{2,1,0:T(8,128)}, f32[1,8,128,128]{3,2,1,0:T(8,128)S(1)}) conditional(s32[]{:T(128)} %convert_element_type.43, () %tuple.81, (s32[1,16,6]{1,2,0:T(8,128)S(1)}, f32[4,8,2048]{2,1,0:T(8,128)S(1)}, bf16[1,1,16,6,2,128,128]{6,5,3,2,4,1,0:T(8,128)(2,1)}, f32[]{:T(128)}, s32[1,8,2]{1,2,0:T(2,128)S(1)}, ...), branch_computations={%region_3.3_spmd, %region_4.5_spmd.clone} | conditional | flops 1234282496 | bytes 15909012 | solution.py:96
  84.9 3.4 %fusion.11 = f32[4,8,16,128]{3,1,0,2:T(8,128)S(1)} fusion(bf16[16,6,2,128,128]{4,3,1,0,2:T(8,128)(2,1)} %bitcast.110, f32[16,6,4,8,128]{4,3,2,1,0:T(8,128)S(1)} %bitcast.108, pred[16,6]{1,0:T(8,128)(4,1)S(1)} %copy.21), kind=kOutput, calls=%fused_computation.17 | convolution fusion | flops 604372992 | bytes 4980832 | tf_op jit(solution)/shard_map/while/body/eval_jaxpr/cond/branch_1_fun/cbrjk,rjkm->cbrm/dot_general | solution.py:35
  88.2 3.4 %fusion.8 = f32[4,8,16,128]{3,1,0,2:T(8,128)S(1)} fusion(bf16[16,6,2,128,128]{4,3,1,0,2:T(8,128)(2,1)} %bitcast.111, f32[16,6,4,8,128]{4,3,2,1,0:T(8,128)S(1)} %bitcast.109, pred[16,6]{1,0:T(8,128)(4,1)S(1)} %copy.21), kind=kOutput, calls=%fused_computation.16 | convolution fusion | flops 604372992 | bytes 4980832 | tf_op jit(solution)/shard_map/while/body/eval_jaxpr/cond/branch_1_fun/cbrjk,rjkm->cbrm/dot_general | solution.py:32
  94.5 1.1 convolution_bitcast_fusion
  95.6 5.5 %collective-permute-start = (f32[4,8,2048]{2,1,0:T(8,128)}, f32[4,8,2048]{2,1,0:T(8,128)S(1)}, u32[]{:S(2)}, u32[]{:S(2)}) collective-permute-start(f32[4,8,2048]{2,1,0:T(8,128)} %get-tuple-element.450), channel_id=1, source_target_pairs={{0,4},{4,8},{8,12},{12,16},{16,20},{20,24},{24,28},{1,5},{5,9},{9,... | collective-permute-start | bytes 786440 | tf_op jit(solution)/shard_map/while/body/eval_jaxpr/ppermute | solution.py:14
  101.3 1.2 collective-permute-done
  103.5 11.8 %conditional.7 = (f32[4,8,2048]{2,1,0:T(8,128)}, f32[1,8,128,128]{3,2,1,0:T(8,128)S(1)}) conditional(s32[]{:T(128)} %convert_element_type.43, () %tuple.81, (s32[1,16,6]{1,2,0:T(8,128)S(1)}, f32[4,8,2048]{2,1,0:T(8,128)S(1)}, bf16[1,1,16,6,2,128,128]{6,5,3,2,4,1,0:T(8,128)(2,1)}, f32[]{:T(128)}, s32[1,8,2]{1,2,0:T(2,128)S(1)}, ...), branch_computations={%region_3.3_spmd, %region_4.5_spmd.clone} | conditional | flops 1234282496 | bytes 15909012 | solution.py:96
  104.6 3.4 %fusion.11 = f32[4,8,16,128]{3,1,0,2:T(8,128)S(1)} fusion(bf16[16,6,2,128,128]{4,3,1,0,2:T(8,128)(2,1)} %bitcast.110, f32[16,6,4,8,128]{4,3,2,1,0:T(8,128)S(1)} %bitcast.108, pred[16,6]{1,0:T(8,128)(4,1)S(1)} %copy.21), kind=kOutput, calls=%fused_computation.17 | convolution fusion | flops 604372992 | bytes 4980832 | tf_op jit(solution)/shard_map/while/body/eval_jaxpr/cond/branch_1_fun/cbrjk,rjkm->cbrm/dot_general | solution.py:35
  107.9 3.4 %fusion.8 = f32[4,8,16,128]{3,1,0,2:T(8,128)S(1)} fusion(bf16[16,6,2,128,128]{4,3,1,0,2:T(8,128)(2,1)} %bitcast.111, f32[16,6,4,8,128]{4,3,2,1,0:T(8,128)S(1)} %bitcast.109, pred[16,6]{1,0:T(8,128)(4,1)S(1)} %copy.21), kind=kOutput, calls=%fused_computation.16 | convolution fusion | flops 604372992 | bytes 4980832 | tf_op jit(solution)/shard_map/while/body/eval_jaxpr/cond/branch_1_fun/cbrjk,rjkm->cbrm/dot_general | solution.py:32
  114.2 1.1 convolution_bitcast_fusion
  115.3 5.5 %collective-permute-start = (f32[4,8,2048]{2,1,0:T(8,128)}, f32[4,8,2048]{2,1,0:T(8,128)S(1)}, u32[]{:S(2)}, u32[]{:S(2)}) collective-permute-start(f32[4,8,2048]{2,1,0:T(8,128)} %get-tuple-element.450), channel_id=1, source_target_pairs={{0,4},{4,8},{8,12},{12,16},{16,20},{20,24},{24,28},{1,5},{5,9},{9,... | collective-permute-start | bytes 786440 | tf_op jit(solution)/shard_map/while/body/eval_jaxpr/ppermute | solution.py:14
  121.0 1.2 collective-permute-done
  123.2 11.8 %conditional.7 = (f32[4,8,2048]{2,1,0:T(8,128)}, f32[1,8,128,128]{3,2,1,0:T(8,128)S(1)}) conditional(s32[]{:T(128)} %convert_element_type.43, () %tuple.81, (s32[1,16,6]{1,2,0:T(8,128)S(1)}, f32[4,8,2048]{2,1,0:T(8,128)S(1)}, bf16[1,1,16,6,2,128,128]{6,5,3,2,4,1,0:T(8,128)(2,1)}, f32[]{:T(128)}, s32[1,8,2]{1,2,0:T(2,128)S(1)}, ...), branch_computations={%region_3.3_spmd, %region_4.5_spmd.clone} | conditional | flops 1234282496 | bytes 15909012 | solution.py:96
  124.3 3.4 %fusion.11 = f32[4,8,16,128]{3,1,0,2:T(8,128)S(1)} fusion(bf16[16,6,2,128,128]{4,3,1,0,2:T(8,128)(2,1)} %bitcast.110, f32[16,6,4,8,128]{4,3,2,1,0:T(8,128)S(1)} %bitcast.108, pred[16,6]{1,0:T(8,128)(4,1)S(1)} %copy.21), kind=kOutput, calls=%fused_computation.17 | convolution fusion | flops 604372992 | bytes 4980832 | tf_op jit(solution)/shard_map/while/body/eval_jaxpr/cond/branch_1_fun/cbrjk,rjkm->cbrm/dot_general | solution.py:35
  127.7 3.4 %fusion.8 = f32[4,8,16,128]{3,1,0,2:T(8,128)S(1)} fusion(bf16[16,6,2,128,128]{4,3,1,0,2:T(8,128)(2,1)} %bitcast.111, f32[16,6,4,8,128]{4,3,2,1,0:T(8,128)S(1)} %bitcast.109, pred[16,6]{1,0:T(8,128)(4,1)S(1)} %copy.21), kind=kOutput, calls=%fused_computation.16 | convolution fusion | flops 604372992 | bytes 4980832 | tf_op jit(solution)/shard_map/while/body/eval_jaxpr/cond/branch_1_fun/cbrjk,rjkm->cbrm/dot_general | solution.py:32
  133.9 1.1 convolution_bitcast_fusion
  135.0 5.5 %collective-permute-start = (f32[4,8,2048]{2,1,0:T(8,128)}, f32[4,8,2048]{2,1,0:T(8,128)S(1)}, u32[]{:S(2)}, u32[]{:S(2)}) collective-permute-start(f32[4,8,2048]{2,1,0:T(8,128)} %get-tuple-element.450), channel_id=1, source_target_pairs={{0,4},{4,8},{8,12},{12,16},{16,20},{20,24},{24,28},{1,5},{5,9},{9,... | collective-permute-start | bytes 786440 | tf_op jit(solution)/shard_map/while/body/eval_jaxpr/ppermute | solution.py:14
  140.7 1.2 collective-permute-done
  142.9 11.8 %conditional.7 = (f32[4,8,2048]{2,1,0:T(8,128)}, f32[1,8,128,128]{3,2,1,0:T(8,128)S(1)}) conditional(s32[]{:T(128)} %convert_element_type.43, () %tuple.81, (s32[1,16,6]{1,2,0:T(8,128)S(1)}, f32[4,8,2048]{2,1,0:T(8,128)S(1)}, bf16[1,1,16,6,2,128,128]{6,5,3,2,4,1,0:T(8,128)(2,1)}, f32[]{:T(128)}, s32[1,8,2]{1,2,0:T(2,128)S(1)}, ...), branch_computations={%region_3.3_spmd, %region_4.5_spmd.clone} | conditional | flops 1234282496 | bytes 15909012 | solution.py:96
  144.0 3.4 %fusion.11 = f32[4,8,16,128]{3,1,0,2:T(8,128)S(1)} fusion(bf16[16,6,2,128,128]{4,3,1,0,2:T(8,128)(2,1)} %bitcast.110, f32[16,6,4,8,128]{4,3,2,1,0:T(8,128)S(1)} %bitcast.108, pred[16,6]{1,0:T(8,128)(4,1)S(1)} %copy.21), kind=kOutput, calls=%fused_computation.17 | convolution fusion | flops 604372992 | bytes 4980832 | tf_op jit(solution)/shard_map/while/body/eval_jaxpr/cond/branch_1_fun/cbrjk,rjkm->cbrm/dot_general | solution.py:35
  147.4 3.4 %fusion.8 = f32[4,8,16,128]{3,1,0,2:T(8,128)S(1)} fusion(bf16[16,6,2,128,128]{4,3,1,0,2:T(8,128)(2,1)} %bitcast.111, f32[16,6,4,8,128]{4,3,2,1,0:T(8,128)S(1)} %bitcast.109, pred[16,6]{1,0:T(8,128)(4,1)S(1)} %copy.21), kind=kOutput, calls=%fused_computation.16 | convolution fusion | flops 604372992 | bytes 4980832 | tf_op jit(solution)/shard_map/while/body/eval_jaxpr/cond/branch_1_fun/cbrjk,rjkm->cbrm/dot_general | solution.py:32
  154.7 5.5 %collective-permute-start = (f32[4,8,2048]{2,1,0:T(8,128)}, f32[4,8,2048]{2,1,0:T(8,128)S(1)}, u32[]{:S(2)}, u32[]{:S(2)}) collective-permute-start(f32[4,8,2048]{2,1,0:T(8,128)} %get-tuple-element.450), channel_id=1, source_target_pairs={{0,4},{4,8},{8,12},{12,16},{16,20},{20,24},{24,28},{1,5},{5,9},{9,... | collective-permute-start | bytes 786440 | tf_op jit(solution)/shard_map/while/body/eval_jaxpr/ppermute | solution.py:14
  160.4 1.2 collective-permute-done
  163.4 16.6 %collective-permute-start = (f32[4,8,2048]{2,1,0:T(8,128)}, f32[4,8,2048]{2,1,0:T(8,128)S(1)}, u32[]{:S(2)}, u32[]{:S(2)}) collective-permute-start(f32[4,8,2048]{2,1,0:T(8,128)} %get-tuple-element.450), channel_id=1, source_target_pairs={{0,4},{4,8},{8,12},{12,16},{16,20},{20,24},{24,28},{1,5},{5,9},{9,... | collective-permute-start | bytes 786440 | tf_op jit(solution)/shard_map/while/body/eval_jaxpr/ppermute | solution.py:14
  180.1 1.2 collective-permute-done
  183.1 5.5 %collective-permute-start = (f32[4,8,2048]{2,1,0:T(8,128)}, f32[4,8,2048]{2,1,0:T(8,128)S(1)}, u32[]{:S(2)}, u32[]{:S(2)}) collective-permute-start(f32[4,8,2048]{2,1,0:T(8,128)} %get-tuple-element.450), channel_id=1, source_target_pairs={{0,4},{4,8},{8,12},{12,16},{16,20},{20,24},{24,28},{1,5},{5,9},{9,... | collective-permute-start | bytes 786440 | tf_op jit(solution)/shard_map/while/body/eval_jaxpr/ppermute | solution.py:14
  188.8 1.2 collective-permute-done
  191.7 16.6 %collective-permute-start = (f32[4,8,2048]{2,1,0:T(8,128)}, f32[4,8,2048]{2,1,0:T(8,128)S(1)}, u32[]{:S(2)}, u32[]{:S(2)}) collective-permute-start(f32[4,8,2048]{2,1,0:T(8,128)} %get-tuple-element.450), channel_id=1, source_target_pairs={{0,4},{4,8},{8,12},{12,16},{16,20},{20,24},{24,28},{1,5},{5,9},{9,... | collective-permute-start | bytes 786440 | tf_op jit(solution)/shard_map/while/body/eval_jaxpr/ppermute | solution.py:14
  208.5 1.2 collective-permute-done
  211.5 5.5 %collective-permute-start = (f32[4,8,2048]{2,1,0:T(8,128)}, f32[4,8,2048]{2,1,0:T(8,128)S(1)}, u32[]{:S(2)}, u32[]{:S(2)}) collective-permute-start(f32[4,8,2048]{2,1,0:T(8,128)} %get-tuple-element.450), channel_id=1, source_target_pairs={{0,4},{4,8},{8,12},{12,16},{16,20},{20,24},{24,28},{1,5},{5,9},{9,... | collective-permute-start | bytes 786440 | tf_op jit(solution)/shard_map/while/body/eval_jaxpr/ppermute | solution.py:14
  217.2 1.2 collective-permute-done
  220.1 10.7 %collective-permute-start = (f32[4,8,2048]{2,1,0:T(8,128)}, f32[4,8,2048]{2,1,0:T(8,128)S(1)}, u32[]{:S(2)}, u32[]{:S(2)}) collective-permute-start(f32[4,8,2048]{2,1,0:T(8,128)} %get-tuple-element.450), channel_id=1, source_target_pairs={{0,4},{4,8},{8,12},{12,16},{16,20},{20,24},{24,28},{1,5},{5,9},{9,... | collective-permute-start | bytes 786440 | tf_op jit(solution)/shard_map/while/body/eval_jaxpr/ppermute | solution.py:14
  231.0 1.2 collective-permute-done
  234.0 6.4 %collective-permute-start = (f32[4,8,2048]{2,1,0:T(8,128)}, f32[4,8,2048]{2,1,0:T(8,128)S(1)}, u32[]{:S(2)}, u32[]{:S(2)}) collective-permute-start(f32[4,8,2048]{2,1,0:T(8,128)} %get-tuple-element.450), channel_id=1, source_target_pairs={{0,4},{4,8},{8,12},{12,16},{16,20},{20,24},{24,28},{1,5},{5,9},{9,... | collective-permute-start | bytes 786440 | tf_op jit(solution)/shard_map/while/body/eval_jaxpr/ppermute | solution.py:14
  240.5 1.2 collective-permute-done
  243.5 17.5 %collective-permute-start = (f32[4,8,2048]{2,1,0:T(8,128)}, f32[4,8,2048]{2,1,0:T(8,128)S(1)}, u32[]{:S(2)}, u32[]{:S(2)}) collective-permute-start(f32[4,8,2048]{2,1,0:T(8,128)} %get-tuple-element.450), channel_id=1, source_target_pairs={{0,4},{4,8},{8,12},{12,16},{16,20},{20,24},{24,28},{1,5},{5,9},{9,... | collective-permute-start | bytes 786440 | tf_op jit(solution)/shard_map/while/body/eval_jaxpr/ppermute | solution.py:14
  261.1 1.2 collective-permute-done
  263.2 53.8 %reduce-scatter.2.cloned.1.call-done = f32[1,2,128,128]{3,2,1,0:T(8,128)} async-done(((f32[1,8,128,128]{3,2,1,0:T(8,128)}), f32[1,2,128,128]{3,2,1,0:T(8,128)}) %reduce-scatter.2.cloned.1.call-update) | async-done | bytes 131088 | tf_op jit(solution)/shard_map/reduce_scatter | solution.py:105
  (227 shorter events, 76.7 us)
Async XLA Ops:
  6.5 310.4 %reduce-scatter.2.cloned.1.call-start = ((), (), s32[]{:S(2)}) async-start(), calls=%async_computation.1 | async-start | bytes 655360 | tf_op jit(solution)/shard_map/reduce_scatter | solution.py:105
  6.5 8.1 %copy-start.1 = (s32[1,16,6]{1,0,2:T(1,128)S(1)}, s32[1,16,6]{1,0,2:T(1,128)}, u32[]{:S(2)}) copy-start(s32[1,16,6]{1,0,2:T(1,128)} %param.16) | copy-start | bytes 1156
  6.5 8.1 %copy-start = (s32[1,8,2]{1,2,0:T(2,128)S(1)}, s32[1,8,2]{1,2,0:T(2,128)}, u32[]{:S(2)}) copy-start(s32[1,8,2]{1,2,0:T(2,128)} %param.17) | copy-start | bytes 196
  27.6 2.7 collective-permute-start
  43.1 2.7 collective-permute-start
  58.6 4.4 %collective-permute-start = (f32[4,8,2048]{2,1,0:T(8,128)}, f32[4,8,2048]{2,1,0:T(8,128)S(1)}, u32[]{:S(2)}, u32[]{:S(2)}) collective-permute-start(f32[4,8,2048]{2,1,0:T(8,128)} %get-tuple-element.450), channel_id=1, source_target_pairs={{0,4},{4,8},{8,12},{12,16},{16,20},{20,24},{24,28},{1,5},{5,9},{9,... | collective-permute-start | bytes 786440 | tf_op jit(solution)/shard_map/while/body/eval_jaxpr/ppermute | solution.py:14
  75.9 6.9 %collective-permute-start = (f32[4,8,2048]{2,1,0:T(8,128)}, f32[4,8,2048]{2,1,0:T(8,128)S(1)}, u32[]{:S(2)}, u32[]{:S(2)}) collective-permute-start(f32[4,8,2048]{2,1,0:T(8,128)} %get-tuple-element.450), channel_id=1, source_target_pairs={{0,4},{4,8},{8,12},{12,16},{16,20},{20,24},{24,28},{1,5},{5,9},{9,... | collective-permute-start | bytes 786440 | tf_op jit(solution)/shard_map/while/body/eval_jaxpr/ppermute | solution.py:14
  95.6 6.9 %collective-permute-start = (f32[4,8,2048]{2,1,0:T(8,128)}, f32[4,8,2048]{2,1,0:T(8,128)S(1)}, u32[]{:S(2)}, u32[]{:S(2)}) collective-permute-start(f32[4,8,2048]{2,1,0:T(8,128)} %get-tuple-element.450), channel_id=1, source_target_pairs={{0,4},{4,8},{8,12},{12,16},{16,20},{20,24},{24,28},{1,5},{5,9},{9,... | collective-permute-start | bytes 786440 | tf_op jit(solution)/shard_map/while/body/eval_jaxpr/ppermute | solution.py:14
  115.3 6.9 %collective-permute-start = (f32[4,8,2048]{2,1,0:T(8,128)}, f32[4,8,2048]{2,1,0:T(8,128)S(1)}, u32[]{:S(2)}, u32[]{:S(2)}) collective-permute-start(f32[4,8,2048]{2,1,0:T(8,128)} %get-tuple-element.450), channel_id=1, source_target_pairs={{0,4},{4,8},{8,12},{12,16},{16,20},{20,24},{24,28},{1,5},{5,9},{9,... | collective-permute-start | bytes 786440 | tf_op jit(solution)/shard_map/while/body/eval_jaxpr/ppermute | solution.py:14
  135.0 6.9 %collective-permute-start = (f32[4,8,2048]{2,1,0:T(8,128)}, f32[4,8,2048]{2,1,0:T(8,128)S(1)}, u32[]{:S(2)}, u32[]{:S(2)}) collective-permute-start(f32[4,8,2048]{2,1,0:T(8,128)} %get-tuple-element.450), channel_id=1, source_target_pairs={{0,4},{4,8},{8,12},{12,16},{16,20},{20,24},{24,28},{1,5},{5,9},{9,... | collective-permute-start | bytes 786440 | tf_op jit(solution)/shard_map/while/body/eval_jaxpr/ppermute | solution.py:14
  154.7 6.9 %collective-permute-start = (f32[4,8,2048]{2,1,0:T(8,128)}, f32[4,8,2048]{2,1,0:T(8,128)S(1)}, u32[]{:S(2)}, u32[]{:S(2)}) collective-permute-start(f32[4,8,2048]{2,1,0:T(8,128)} %get-tuple-element.450), channel_id=1, source_target_pairs={{0,4},{4,8},{8,12},{12,16},{16,20},{20,24},{24,28},{1,5},{5,9},{9,... | collective-permute-start | bytes 786440 | tf_op jit(solution)/shard_map/while/body/eval_jaxpr/ppermute | solution.py:14
  163.4 17.9 %collective-permute-start = (f32[4,8,2048]{2,1,0:T(8,128)}, f32[4,8,2048]{2,1,0:T(8,128)S(1)}, u32[]{:S(2)}, u32[]{:S(2)}) collective-permute-start(f32[4,8,2048]{2,1,0:T(8,128)} %get-tuple-element.450), channel_id=1, source_target_pairs={{0,4},{4,8},{8,12},{12,16},{16,20},{20,24},{24,28},{1,5},{5,9},{9,... | collective-permute-start | bytes 786440 | tf_op jit(solution)/shard_map/while/body/eval_jaxpr/ppermute | solution.py:14
  183.1 6.9 %collective-permute-start = (f32[4,8,2048]{2,1,0:T(8,128)}, f32[4,8,2048]{2,1,0:T(8,128)S(1)}, u32[]{:S(2)}, u32[]{:S(2)}) collective-permute-start(f32[4,8,2048]{2,1,0:T(8,128)} %get-tuple-element.450), channel_id=1, source_target_pairs={{0,4},{4,8},{8,12},{12,16},{16,20},{20,24},{24,28},{1,5},{5,9},{9,... | collective-permute-start | bytes 786440 | tf_op jit(solution)/shard_map/while/body/eval_jaxpr/ppermute | solution.py:14
  191.7 17.9 %collective-permute-start = (f32[4,8,2048]{2,1,0:T(8,128)}, f32[4,8,2048]{2,1,0:T(8,128)S(1)}, u32[]{:S(2)}, u32[]{:S(2)}) collective-permute-start(f32[4,8,2048]{2,1,0:T(8,128)} %get-tuple-element.450), channel_id=1, source_target_pairs={{0,4},{4,8},{8,12},{12,16},{16,20},{20,24},{24,28},{1,5},{5,9},{9,... | collective-permute-start | bytes 786440 | tf_op jit(solution)/shard_map/while/body/eval_jaxpr/ppermute | solution.py:14
  211.5 6.9 %collective-permute-start = (f32[4,8,2048]{2,1,0:T(8,128)}, f32[4,8,2048]{2,1,0:T(8,128)S(1)}, u32[]{:S(2)}, u32[]{:S(2)}) collective-permute-start(f32[4,8,2048]{2,1,0:T(8,128)} %get-tuple-element.450), channel_id=1, source_target_pairs={{0,4},{4,8},{8,12},{12,16},{16,20},{20,24},{24,28},{1,5},{5,9},{9,... | collective-permute-start | bytes 786440 | tf_op jit(solution)/shard_map/while/body/eval_jaxpr/ppermute | solution.py:14
  220.1 12.0 %collective-permute-start = (f32[4,8,2048]{2,1,0:T(8,128)}, f32[4,8,2048]{2,1,0:T(8,128)S(1)}, u32[]{:S(2)}, u32[]{:S(2)}) collective-permute-start(f32[4,8,2048]{2,1,0:T(8,128)} %get-tuple-element.450), channel_id=1, source_target_pairs={{0,4},{4,8},{8,12},{12,16},{16,20},{20,24},{24,28},{1,5},{5,9},{9,... | collective-permute-start | bytes 786440 | tf_op jit(solution)/shard_map/while/body/eval_jaxpr/ppermute | solution.py:14
  234.0 7.8 %collective-permute-start = (f32[4,8,2048]{2,1,0:T(8,128)}, f32[4,8,2048]{2,1,0:T(8,128)S(1)}, u32[]{:S(2)}, u32[]{:S(2)}) collective-permute-start(f32[4,8,2048]{2,1,0:T(8,128)} %get-tuple-element.450), channel_id=1, source_target_pairs={{0,4},{4,8},{8,12},{12,16},{16,20},{20,24},{24,28},{1,5},{5,9},{9,... | collective-permute-start | bytes 786440 | tf_op jit(solution)/shard_map/while/body/eval_jaxpr/ppermute | solution.py:14
  243.5 18.8 %collective-permute-start = (f32[4,8,2048]{2,1,0:T(8,128)}, f32[4,8,2048]{2,1,0:T(8,128)S(1)}, u32[]{:S(2)}, u32[]{:S(2)}) collective-permute-start(f32[4,8,2048]{2,1,0:T(8,128)} %get-tuple-element.450), channel_id=1, source_target_pairs={{0,4},{4,8},{8,12},{12,16},{16,20},{20,24},{24,28},{1,5},{5,9},{9,... | collective-permute-start | bytes 786440 | tf_op jit(solution)/shard_map/while/body/eval_jaxpr/ppermute | solution.py:14
Sparse Core Ops, SparseCore 0:
  263.3 53.5 reduce-scatter.1
where the time goes:
time: 325 us; the launch traced here: 324 us
  starting transfers between devices  112 us (34%)
  waiting for transfers between devices  71.2 us (22%)
  matrix products  62.3 us (19%)
  local copies, waits for them, and re-layouts  53.1 us (16%)
  between operations  13.4 us (4%)
  other arithmetic  10.1 us (3%)
    ppermute x15, starting transfers between devices, passed_along(): lax.ppermute(value, axis, [(source, source + steps) for source in range(i...  112 us
    reduce_scatter x1, waiting for transfers between devices, shards(): lax.psum_scatter(images * image_scale, 'freq', scatter_dimension=1, tiled...  53.8 us
    dot_general x8, matrix products, propagate(): jnp.einsum('cbrjk,rjkm->cbrm', picked, operator_real, precision=lax.Preci...  26.9 us
    dot_general x8, matrix products, propagate(): jnp.einsum('cbrjk,rjkm->cbrm', picked, operator_imag, precision=lax.Preci...  26.9 us
    ppermute x15, waiting for transfers between devices, passed_along(): lax.ppermute(value, axis, [(source, source + steps) for source in range(i...  17.4 us
    dynamic_slice x15, local copies, waits for them, and re-layouts, surface_group(): lax.dynamic_slice_in_dim(receiver_data[0], shot_start, group_shots, 1)  14.8 us
    dot_general x8, matrix products, image_level(): jnp.einsum('csik,csim->ikm', source_blocks, receiver_blocks, precision=la...  8.54 us
    unnamed x6, local copies, waits for them, and re-layouts  8.11 us
  transfers between devices with their start and end apart: 16, of which 16 were waited for; matrix products, arithmetic and copies ran while one was open for 1% of the time, Pallas kernels for 0%

commit v1 on v0

v1 whole, which is shorter than its diff:
```python
import functools
import math

import jax
import jax.numpy as jnp
from jax import lax
from jax.experimental import pallas as pl
from jax.experimental.pallas import tpu as pltpu
from jax.sharding import PartitionSpec as P

GROUPS = 4
NEAR_DELAY = 1
FAR_DELAY = 2
UNROLL = 16
SMEM = pl.BlockSpec(memory_space=pltpu.SMEM)
VMEM = pl.BlockSpec(memory_space=pltpu.VMEM)
HBM = pl.BlockSpec(memory_space=pltpu.HBM)


def edge_taper(lateral):
    position = jnp.arange(lateral, dtype=jnp.int32)
    distance = jnp.minimum(position, lateral - 1 - position).astype(jnp.float32)
    edge_cells = lateral // 32
    edge_ramp = jnp.maximum(0.0, 1.0 - distance / edge_cells)
    return 1.0 - 0.3 * edge_ramp * edge_ramp


def split_halves(value):
    high = value.astype(jnp.bfloat16)
    low = (value - high.astype(jnp.float32)).astype(jnp.bfloat16)
    return high, low


def load_kernel(columns, pairs, taper, operator, out, semaphore):
    copy = pltpu.make_async_copy(operator.at[0, 0], out, semaphore)
    copy.start()
    copy.wait()


def entry_turn(depth):
    return (depth + 1) // 2 * NEAR_DELAY + depth // 2 * FAR_DELAY


def propagate_kernel(*refs, turn, first_shot, near_in, far_in, surface_in):
    refs = list(refs)
    columns, operator, taper, kept_in = refs[:4]
    del refs[:4]
    depth = lax.axis_index("depth")
    group = turn - entry_turn(depth)
    active = jnp.logical_and(group >= 0, group < GROUPS)
    odd = lax.rem(depth, 2) == 1
    near = refs.pop(0) if near_in else None
    far = refs.pop(0) if far_in else None
    surface = [refs.pop(0), refs.pop(0)] if surface_in else None
    out, kept, split = refs[:3]
    block_rows, nnz = operator.shape[0], operator.shape[1]
    width = operator.shape[-1]
    rows = out.shape[2]
    shots = rows // 2

    def put(block, part, value):
        high, low = split_halves(value)
        split[block, part * rows:(part + 1) * rows, :] = high
        split[block, (2 + part) * rows:(3 + part) * rows, :] = low

    def take(field):
        for block in range(block_rows):
            for part in range(2):
                put(block, part, field[block, part])

    if surface_in:
        drawn, semaphores = refs[3:5]

        @pl.when(jnp.logical_and(active, depth == 0))
        def _():
            copies = [
                pltpu.make_async_copy(
                    surface[k].at[0, :, pl.ds(first_shot, shots), :],
                    drawn.at[k], semaphores.at[k])
                for k in range(2)
            ]
            for copy in copies:
                copy.start()
            for copy in copies:
                copy.wait()
            for block in range(block_rows):
                lanes = slice(block * width, (block + 1) * width)
                for part in range(2):
                    receiver = drawn[1, part, :, lanes]
                    if part == 1:
                        receiver = -receiver
                    put(block, part, jnp.concatenate([drawn[0, part, :, lanes], receiver], axis=0))

    if near_in:
        @pl.when(jnp.logical_and(active, odd))
        def _():
            take(near)

    if far_in:
        @pl.when(jnp.logical_and(active, jnp.logical_and(depth > 0, jnp.logical_not(odd))))
        def _():
            take(far)

    @pl.when(active)
    def _():
        def one_row(r, carry):
            picked = jnp.concatenate(
                [split[columns[r * nnz + j]] for j in range(nnz)], axis=1
            )
            real = operator[r, :, 0].reshape(nnz * width, width)
            imag = operator[r, :, 1].reshape(nnz * width, width)
            weights = jnp.concatenate([real, imag], axis=1)
            product = jnp.dot(picked, weights, preferred_element_type=jnp.float32)
            product = product[: 2 * rows] + product[2 * rows:]
            scale = taper[pl.ds(r, 1), :]
            real_out = (product[:rows, :width] - product[rows:, width:]) * scale
            imag_out = (product[rows:, :width] + product[:rows, width:]) * scale
            out[r, 0] = real_out
            out[r, 1] = imag_out
            kept[group, r, 0] = real_out
            kept[group, r, 1] = imag_out
            return carry

        lax.fori_loop(0, block_rows, one_row, 0, unroll=UNROLL)


def image_block(pairs, index, kept, groups, scale):
    shots = kept.shape[3] // 2
    a = pairs[2 * index]
    b = pairs[2 * index + 1]
    left = jnp.concatenate(
        [kept[g, a, part, :shots, :] for g in groups for part in range(2)], axis=0
    ) * scale
    right = jnp.concatenate(
        [kept[g, b, part, shots:, :] * (1.0 - 2.0 * part) for g in groups for part in range(2)],
        axis=0,
    )
    left_high, left_low = split_halves(left)
    right_high, right_low = split_halves(right)
    lhs = jnp.concatenate([left_high, left_high, left_low], axis=0)
    rhs = jnp.concatenate([right_high, right_low, right_high], axis=0)
    return lax.dot_general(
        lhs, rhs, (((0,), (0,)), ((), ())), preferred_element_type=jnp.float32
    )


def early_kernel(pairs, kept_in, kept, out, *, groups, scale):
    for index in range(out.shape[0]):
        out[index] = image_block(pairs, index, kept_in, groups, scale)


def last_kernel(pairs, early, kept, *outs, groups, scale):
    share = outs[0].shape[0]
    parts = len(outs)
    own = lax.axis_index("freq")
    for step in range(parts):
        owner = lax.rem(own + step, parts)
        for index in range(share):
            pair = owner * share + index
            outs[step][index] = early[pair] + image_block(pairs, pair, kept, groups, scale)


def shards(source_field, receiver_data, propagator, block_columns, image_pairs):
    depth_count = lax.axis_size("depth")
    freq_count = lax.axis_size("freq")
    shots_all, lateral = source_field.shape[2:]
    block_rows, nnz = propagator.shape[2:4]
    width = propagator.shape[-1]
    pair_count = image_pairs.shape[1]
    shots = shots_all // GROUPS
    rows = 2 * shots
    taper = edge_taper(lateral).reshape(block_rows, width)
    scale = 1.0 / math.sqrt(2.0 * shots_all * freq_count)
    columns = block_columns[0].reshape(-1)
    pairs = image_pairs[0].reshape(-1)
    field_type = pltpu.VMEM((block_rows, 2, rows, width), jnp.float32)
    kept_type = pltpu.VMEM((GROUPS, block_rows, 2, rows, width), jnp.float32)
    params = pltpu.CompilerParams(vmem_limit_bytes=16 * 1024 * 1024)

    turns = GROUPS + entry_turn(depth_count - 1)

    operator = pl.pallas_call(
        load_kernel,
        out_shape=pltpu.VMEM(propagator.shape[2:], propagator.dtype),
        in_specs=[SMEM, SMEM, VMEM, HBM],
        out_specs=VMEM,
        scratch_shapes=[pltpu.SemaphoreType.DMA],
        compiler_params=params,
    )(columns, pairs, taper, propagator)

    def active(d, turn):
        return 0 <= turn - entry_turn(d) < GROUPS

    def steps(turn, odd):
        return [(d, d + 1) for d in range(depth_count - 1)
                if d % 2 == odd and active(d, turn)]

    kept = None
    early = None
    near_sent = {}
    far_sent = {}
    for turn in range(turns):
        near = near_sent.pop(turn - NEAR_DELAY, None)
        far = far_sent.pop(turn - FAR_DELAY, None)
        surface_in = turn < GROUPS
        operands = [columns, operator, taper]
        specs = [SMEM, VMEM, VMEM]
        if kept is None:
            kept = pl.pallas_call(
                lambda out: None, out_shape=kept_type, out_specs=VMEM, compiler_params=params)()
        operands.append(kept)
        specs.append(VMEM)
        for value in (near, far):
            if value is not None:
                operands.append(value)
                specs.append(VMEM)
        scratch = [pltpu.VMEM((block_rows, 4 * rows, width), jnp.bfloat16)]
        if surface_in:
            operands += [source_field, receiver_data]
            specs += [HBM, HBM]
            scratch += [pltpu.VMEM((2, 2, shots, lateral), jnp.float32),
                        pltpu.SemaphoreType.DMA((2,))]
        field, kept = pl.pallas_call(
            functools.partial(
                propagate_kernel, turn=turn, first_shot=min(turn, GROUPS - 1) * shots,
                near_in=near is not None, far_in=far is not None, surface_in=surface_in),
            out_shape=(field_type, kept_type),
            in_specs=specs,
            out_specs=(VMEM, VMEM),
            input_output_aliases={3: 1},
            scratch_shapes=scratch,
            compiler_params=params,
            cost_estimate=pl.CostEstimate(
                flops=2 * 4 * rows * block_rows * nnz * 2 * width * width,
                bytes_accessed=block_rows * nnz * 4 * width * width, transcendentals=0),
        )(*operands)
        near_steps = steps(turn, 0)
        far_steps = steps(turn, 1)
        if near_steps:
            near_sent[turn] = lax.ppermute(field, "depth", near_steps)
        if far_steps:
            far_sent[turn] = lax.ppermute(field, "depth", far_steps)
        if turn == turns - 2:
            image_type = jax.ShapeDtypeStruct((pair_count, width, width), jnp.float32)
            kept, early = pl.pallas_call(
                functools.partial(early_kernel, groups=list(range(GROUPS - 1)), scale=scale),
                out_shape=(kept_type, image_type),
                in_specs=[SMEM, VMEM],
                out_specs=(VMEM, VMEM),
                input_output_aliases={1: 0},
                compiler_params=params,
            )(pairs, kept)

    share = pair_count // freq_count
    share_type = jax.ShapeDtypeStruct((share, width, width), jnp.float32)
    shares = pl.pallas_call(
        functools.partial(last_kernel, groups=[GROUPS - 1], scale=scale),
        out_shape=(share_type,) * freq_count,
        in_specs=[SMEM, VMEM, VMEM],
        out_specs=(VMEM,) * freq_count,
        compiler_params=params,
    )(pairs, early, kept)
    total = shares[0]
    for step in range(1, freq_count):
        total += lax.ppermute(
            shares[step], "freq", [(f, (f + step) % freq_count) for f in range(freq_count)])
    return total[None]


def solution(mesh):
    placed = (
        P("freq", None, None, None),
        P("freq", None, None, None),
        P("freq", "depth", None, None, None, None, None),
        P("depth", None, None),
        P("depth", None, None),
    )
    return jax.shard_map(
        shards,
        mesh=mesh,
        in_specs=placed,
        out_specs=P("depth", "freq", None, None),
        check_vma=False,
    )
```

time: 325 us -> 101 us (0.31)
  the two profiles are of different devices: /device:TPU:0 before, /device:TPU:15 now
where the time goes in v1:
time: 101 us
  waiting for transfers between devices  55.5 us (55%)
  starting transfers between devices  22.2 us (22%)
  Pallas kernels  17.5 us (17%)
  local copies, waits for them, and re-layouts  4.33 us (4%)
    ppermute x13, waiting for transfers between devices, shards(): near_sent[turn] = lax.ppermute(field, 'depth', near_steps)  45.6 us
    pallas_call x14, Pallas kernels, shards(): pl.pallas_call(functools.partial(propagate_kernel, turn=turn, first_shot=...  14.8 us
    ppermute x13, starting transfers between devices, shards(): near_sent[turn] = lax.ppermute(field, 'depth', near_steps)  11.4 us
    ppermute x3, waiting for transfers between devices, shards(): lax.ppermute(shares[step], 'freq', [(f, (f + step) % freq_count) for f in...  9.91 us
    ppermute x10, starting transfers between devices, shards(): far_sent[turn] = lax.ppermute(field, 'depth', far_steps)  6.94 us
    unnamed x12, local copies, waits for them, and re-layouts  4.16 us
    ppermute x3, starting transfers between devices, shards(): lax.ppermute(shares[step], 'freq', [(f, (f + step) % freq_count) for f in...  3.83 us
  transfers between devices with their start and end apart: 26, of which 7 were waited for; matrix products, arithmetic and copies ran while one was open for 0% of the time, Pallas kernels for 10%

profile of v1, /device:TPU:15, one launch (start us, length us, event | category | flops | bytes accessed | tf_op | source)
XLA Modules:
  0.0 100.8 jit_solution(14464756236165611410)
XLA Ops:
  0.0 0.7 copy-done.4
  0.7 0.1 copy.23
  0.8 0.1 reshape_squeeze.6.pairs
  0.8 0.1 copy.24
  0.9 0.1 reshape_squeeze.7.columns.refs_0_
  1.0 0.0 copy-start.2
  1.0 2.8 %copy-done.2 = bf16[1,1,16,6,2,128,128]{6,5,4,3,2,1,0:T(8,128)(2,1)S(1)} copy-done((bf16[1,1,16,6,2,128,128]{6,5,4,3,2,1,0:T(8,128)(2,1)S(1)}, bf16[1,1,16,6,2,128,128]{6,5,4,3,2,1,0:T(8,128)(2,1)}, u32[]{:S(2)}) %copy-start.2) | copy-done | bytes 6291480
  3.8 1.0 shard_map.55.refs_1_
  4.8 0.2 copy-done
  5.0 0.3 copy-done.1
  5.4 0.6 shard_map.57
  5.9 0.7 collective-permute-start
  6.7 0.6 shard_map.58
  7.3 0.7 collective-permute-start.1
  8.0 0.7 collective-permute-start.3
  8.7 0.6 shard_map.59
  9.3 0.7 collective-permute-start.2
  10.0 0.7 collective-permute-start.5
  10.7 0.6 shard_map.60
  11.3 0.7 collective-permute-start.4
  12.0 0.7 collective-permute-start.7
  12.7 0.0 collective-permute-done.4.refs_4_
  12.7 0.6 shard_map.61
  13.3 0.7 collective-permute-start.6
  14.0 0.7 collective-permute-start.9
  14.8 0.6 shard_map.62
  15.4 0.7 collective-permute-start.8
  16.1 0.7 collective-permute-start.11
  16.8 0.0 collective-permute-done.9.refs_5_
  16.8 0.6 shard_map.63
  17.4 0.7 collective-permute-start.10
  18.1 0.7 collective-permute-start.13
  18.8 0.0 collective-permute-done.11.refs_5_
  18.8 0.6 shard_map.64
  19.4 0.7 collective-permute-start.12
  20.1 0.7 collective-permute-start.15
  20.8 0.0 collective-permute-done.13.refs_5_
  20.8 0.8 shard_map.65
  21.6 0.7 collective-permute-start.14
  22.3 0.7 collective-permute-start.17
  23.0 0.6 shard_map.66
  23.6 1.3 %collective-permute-start.16 = (f32[16,2,32,128]{3,2,1,0:T(8,128)S(1)}, f32[16,2,32,128]{3,2,1,0:T(8,128)S(1)}, u32[]{:S(2)}, u32[]{:S(2)}) collective-permute-start(f32[16,2,32,128]{3,2,1,0:T(8,128)S(1)} %get-tuple-element.57), channel_id=1, source_target_pairs={{16,20},{24,28},{17,21},{25,29},{18,22},{26,30},{19,23},{27,31}} | collective-permute-start | bytes 1572872 | tf_op jit(solution)/shard_map/ppermute | solution.py:240
  24.9 0.7 collective-permute-start.19
  25.6 36.4 %collective-permute-done.16.refs_4_ = f32[16,2,32,128]{3,2,1,0:T(8,128)S(1)} collective-permute-done((f32[16,2,32,128]{3,2,1,0:T(8,128)S(1)}, f32[16,2,32,128]{3,2,1,0:T(8,128)S(1)}, u32[]{:S(2)}, u32[]{:S(2)}) %collective-permute-start.16) | collective-permute-done | bytes 524320 | tf_op jit(solution)/shard_map/ppermute | solution.py:240
  62.0 2.0 %shard_map.67 = (f32[16,2,32,128]{3,2,1,0:T(8,128)S(1)}, f32[4,16,2,32,128]{4,3,2,1,0:T(8,128)S(1)}) custom-call(s32[96]{0:T(128)S(1)} %reshape_squeeze.7.columns.refs_0_, bf16[16,6,2,128,128]{4,3,2,1,0:T(8,128)(2,1)S(1)} %shard_map.55.refs_1_, f32[16,128]{1,0:T(8,128)S(1)} %fusion.4.taper.refs_2_, ...), custom_call_target="tpu_custom_call", output_to_operand_aliasing={{1}: (3, {})} | custom-call | flops 805306368 | bytes 6291456 | tf_op jit(solution)/shard_map/pallas_call | solution.py:223
  64.0 1.3 %collective-permute-start.18 = (f32[16,2,32,128]{3,2,1,0:T(8,128)S(1)}, f32[16,2,32,128]{3,2,1,0:T(8,128)S(1)}, u32[]{:S(2)}, u32[]{:S(2)}) collective-permute-start(f32[16,2,32,128]{3,2,1,0:T(8,128)S(1)} %get-tuple-element.59), channel_id=1, source_target_pairs={{24,28},{25,29},{26,30},{27,31}} | collective-permute-start | bytes 1572872 | tf_op jit(solution)/shard_map/ppermute | solution.py:240
  65.3 0.7 collective-permute-start.21
  66.0 2.0 %collective-permute-done.18.refs_4_ = f32[16,2,32,128]{3,2,1,0:T(8,128)S(1)} collective-permute-done((f32[16,2,32,128]{3,2,1,0:T(8,128)S(1)}, f32[16,2,32,128]{3,2,1,0:T(8,128)S(1)}, u32[]{:S(2)}, u32[]{:S(2)}) %collective-permute-start.18) | collective-permute-done | bytes 524320 | tf_op jit(solution)/shard_map/ppermute | solution.py:240
  68.0 2.0 %shard_map.68 = (f32[16,2,32,128]{3,2,1,0:T(8,128)S(1)}, f32[4,16,2,32,128]{4,3,2,1,0:T(8,128)S(1)}) custom-call(s32[96]{0:T(128)S(1)} %reshape_squeeze.7.columns.refs_0_, bf16[16,6,2,128,128]{4,3,2,1,0:T(8,128)(2,1)S(1)} %shard_map.55.refs_1_, f32[16,128]{1,0:T(8,128)S(1)} %fusion.4.taper.refs_2_, ...), custom_call_target="tpu_custom_call", output_to_operand_aliasing={{1}: (3, {})} | custom-call | flops 805306368 | bytes 6291456 | tf_op jit(solution)/shard_map/pallas_call | solution.py:223
  70.0 1.3 %collective-permute-start.20 = (f32[16,2,32,128]{3,2,1,0:T(8,128)S(1)}, f32[16,2,32,128]{3,2,1,0:T(8,128)S(1)}, u32[]{:S(2)}, u32[]{:S(2)}) collective-permute-start(f32[16,2,32,128]{3,2,1,0:T(8,128)S(1)} %get-tuple-element.61), channel_id=1, source_target_pairs={{24,28},{25,29},{26,30},{27,31}} | collective-permute-start | bytes 1572872 | tf_op jit(solution)/shard_map/ppermute | solution.py:240
  71.3 5.6 %collective-permute-done.20.refs_4_ = f32[16,2,32,128]{3,2,1,0:T(8,128)S(1)} collective-permute-done((f32[16,2,32,128]{3,2,1,0:T(8,128)S(1)}, f32[16,2,32,128]{3,2,1,0:T(8,128)S(1)}, u32[]{:S(2)}, u32[]{:S(2)}) %collective-permute-start.20) | collective-permute-done | bytes 524320 | tf_op jit(solution)/shard_map/ppermute | solution.py:240
  76.9 2.0 %shard_map.69 = (f32[16,2,32,128]{3,2,1,0:T(8,128)S(1)}, f32[4,16,2,32,128]{4,3,2,1,0:T(8,128)S(1)}) custom-call(s32[96]{0:T(128)S(1)} %reshape_squeeze.7.columns.refs_0_, bf16[16,6,2,128,128]{4,3,2,1,0:T(8,128)(2,1)S(1)} %shard_map.55.refs_1_, f32[16,128]{1,0:T(8,128)S(1)} %fusion.4.taper.refs_2_, ...), custom_call_target="tpu_custom_call", output_to_operand_aliasing={{1}: (3, {})} | custom-call | flops 805306368 | bytes 6291456 | tf_op jit(solution)/shard_map/pallas_call | solution.py:223
  78.9 1.3 %collective-permute-start.22 = (f32[16,2,32,128]{3,2,1,0:T(8,128)S(1)}, f32[16,2,32,128]{3,2,1,0:T(8,128)S(1)}, u32[]{:S(2)}, u32[]{:S(2)}) collective-permute-start(f32[16,2,32,128]{3,2,1,0:T(8,128)S(1)} %get-tuple-element.65), channel_id=1, source_target_pairs={{24,28},{25,29},{26,30},{27,31}} | collective-permute-start | bytes 1572872 | tf_op jit(solution)/shard_map/ppermute | solution.py:240
  80.2 1.0 shard_map.70
  81.2 1.5 %collective-permute-done.22.refs_4_ = f32[16,2,32,128]{3,2,1,0:T(8,128)S(1)} collective-permute-done((f32[16,2,32,128]{3,2,1,0:T(8,128)S(1)}, f32[16,2,32,128]{3,2,1,0:T(8,128)S(1)}, u32[]{:S(2)}, u32[]{:S(2)}) %collective-permute-start.22) | collective-permute-done | bytes 524320 | tf_op jit(solution)/shard_map/ppermute | solution.py:240
  82.7 2.8 %shard_map.71 = (f32[16,2,32,128]{3,2,1,0:T(8,128)}, f32[4,16,2,32,128]{4,3,2,1,0:T(8,128)S(1)}) custom-call(s32[96]{0:T(128)S(1)} %reshape_squeeze.7.columns.refs_0_, bf16[16,6,2,128,128]{4,3,2,1,0:T(8,128)(2,1)S(1)} %shard_map.55.refs_1_, f32[16,128]{1,0:T(8,128)S(1)} %fusion.4.taper.refs_2_, ...), custom_call_target="tpu_custom_call", output_to_operand_aliasing={{1}: (3, {})} | custom-call | flops 805306368 | bytes 6291456 | tf_op jit(solution)/shard_map/pallas_call | solution.py:223
  85.5 0.8 shard_map.72
  86.4 1.3 %collective-permute-start.23 = (f32[2,128,128]{2,1,0:T(8,128)S(1)}, f32[2,128,128]{2,1,0:T(8,128)S(1)}, u32[]{:S(2)}, u32[]{:S(2)}) collective-permute-start(f32[2,128,128]{2,1,0:T(8,128)S(1)} %get-tuple-element.68), channel_id=1, source_target_pairs={{0,1},{1,2},{2,3},{3,0},{4,5},{5,6},{6,7},{7,4},{8,9},{9,10},{10,1... | collective-permute-start | bytes 393224 | tf_op jit(solution)/shard_map/ppermute | solution.py:265
  87.7 1.1 %collective-permute-start.24 = (f32[2,128,128]{2,1,0:T(8,128)S(1)}, f32[2,128,128]{2,1,0:T(8,128)S(1)}, u32[]{:S(2)}, u32[]{:S(2)}) collective-permute-start(f32[2,128,128]{2,1,0:T(8,128)S(1)} %get-tuple-element.69), channel_id=1, source_target_pairs={{0,2},{1,3},{2,0},{3,1},{4,6},{5,7},{6,4},{7,5},{8,10},{9,11},{10,... | collective-permute-start | bytes 393224 | tf_op jit(solution)/shard_map/ppermute | solution.py:265
  88.8 1.4 %collective-permute-start.25 = (f32[2,128,128]{2,1,0:T(8,128)S(1)}, f32[2,128,128]{2,1,0:T(8,128)S(1)}, u32[]{:S(2)}, u32[]{:S(2)}) collective-permute-start(f32[2,128,128]{2,1,0:T(8,128)S(1)} %get-tuple-element.70), channel_id=1, source_target_pairs={{0,3},{1,0},{2,1},{3,2},{4,7},{5,4},{6,5},{7,6},{8,11},{9,8},{10,9... | collective-permute-start | bytes 393224 | tf_op jit(solution)/shard_map/ppermute | solution.py:265
  90.2 6.3 %collective-permute-done.23 = f32[2,128,128]{2,1,0:T(8,128)S(1)} collective-permute-done((f32[2,128,128]{2,1,0:T(8,128)S(1)}, f32[2,128,128]{2,1,0:T(8,128)S(1)}, u32[]{:S(2)}, u32[]{:S(2)}) %collective-permute-start.23) | collective-permute-done | bytes 131104 | tf_op jit(solution)/shard_map/ppermute | solution.py:265
  96.5 2.2 %collective-permute-done.24 = f32[2,128,128]{2,1,0:T(8,128)S(1)} collective-permute-done((f32[2,128,128]{2,1,0:T(8,128)S(1)}, f32[2,128,128]{2,1,0:T(8,128)S(1)}, u32[]{:S(2)}, u32[]{:S(2)}) %collective-permute-start.24) | collective-permute-done | bytes 131104 | tf_op jit(solution)/shard_map/ppermute | solution.py:265
  98.6 1.5 %collective-permute-done.25 = f32[2,128,128]{2,1,0:T(8,128)S(1)} collective-permute-done((f32[2,128,128]{2,1,0:T(8,128)S(1)}, f32[2,128,128]{2,1,0:T(8,128)S(1)}, u32[]{:S(2)}, u32[]{:S(2)}) %collective-permute-start.25) | collective-permute-done | bytes 131104 | tf_op jit(solution)/shard_map/ppermute | solution.py:265
  100.1 0.7 add_bitcast_fusion
  (22 shorter events, 0.1 us)
Async XLA Ops:
  0.0 0.7 copy-start.4
  0.0 0.8 copy-start.3
  1.0 2.8 %copy-start.2 = (bf16[1,1,16,6,2,128,128]{6,5,4,3,2,1,0:T(8,128)(2,1)S(1)}, bf16[1,1,16,6,2,128,128]{6,5,4,3,2,1,0:T(8,128)(2,1)}, u32[]{:S(2)}) copy-start(bf16[1,1,16,6,2,128,128]{6,5,4,3,2,1,0:T(8,128)(2,1)} %operator.1) | copy-start | bytes 18874372
  3.8 1.2 %copy-start = (f32[1,2,64,2048]{3,2,1,0:T(8,128)S(1)}, f32[1,2,64,2048]{3,2,1,0:T(8,128)}, u32[]{:S(2)}) copy-start(f32[1,2,64,2048]{3,2,1,0:T(8,128)} %refs_6_.5) | copy-start | bytes 3145732
  3.8 1.5 %copy-start.1 = (f32[1,2,64,2048]{3,2,1,0:T(8,128)S(1)}, f32[1,2,64,2048]{3,2,1,0:T(8,128)}, u32[]{:S(2)}) copy-start(f32[1,2,64,2048]{3,2,1,0:T(8,128)} %refs_7_.1) | copy-start | bytes 3145732
  5.9 0.7 collective-permute-start
  7.3 1.4 %collective-permute-start.1 = (f32[16,2,32,128]{3,2,1,0:T(8,128)S(1)}, f32[16,2,32,128]{3,2,1,0:T(8,128)S(1)}, u32[]{:S(2)}, u32[]{:S(2)}) collective-permute-start(f32[16,2,32,128]{3,2,1,0:T(8,128)S(1)} %get-tuple-element.41), channel_id=1, source_target_pairs={{0,4},{1,5},{2,6},{3,7}} | collective-permute-start | bytes 1572872 | tf_op jit(solution)/shard_map/ppermute | solution.py:240
  8.0 2.7 %collective-permute-start.3 = (f32[16,2,32,128]{3,2,1,0:T(8,128)S(1)}, f32[16,2,32,128]{3,2,1,0:T(8,128)S(1)}, u32[]{:S(2)}, u32[]{:S(2)}) collective-permute-start(f32[16,2,32,128]{3,2,1,0:T(8,128)S(1)} %get-tuple-element.41), channel_id=1, source_target_pairs={{4,8},{5,9},{6,10},{7,11}} | collective-permute-start | bytes 1572872 | tf_op jit(solution)/shard_map/ppermute | solution.py:242
  9.3 1.4 %collective-permute-start.2 = (f32[16,2,32,128]{3,2,1,0:T(8,128)S(1)}, f32[16,2,32,128]{3,2,1,0:T(8,128)S(1)}, u32[]{:S(2)}, u32[]{:S(2)}) collective-permute-start(f32[16,2,32,128]{3,2,1,0:T(8,128)S(1)} %get-tuple-element.43), channel_id=1, source_target_pairs={{0,4},{1,5},{2,6},{3,7}} | collective-permute-start | bytes 1572872 | tf_op jit(solution)/shard_map/ppermute | solution.py:240
  10.0 2.7 %collective-permute-start.5 = (f32[16,2,32,128]{3,2,1,0:T(8,128)S(1)}, f32[16,2,32,128]{3,2,1,0:T(8,128)S(1)}, u32[]{:S(2)}, u32[]{:S(2)}) collective-permute-start(f32[16,2,32,128]{3,2,1,0:T(8,128)S(1)} %get-tuple-element.43), channel_id=1, source_target_pairs={{4,8},{5,9},{6,10},{7,11}} | collective-permute-start | bytes 1572872 | tf_op jit(solution)/shard_map/ppermute | solution.py:242
  11.3 1.4 %collective-permute-start.4 = (f32[16,2,32,128]{3,2,1,0:T(8,128)S(1)}, f32[16,2,32,128]{3,2,1,0:T(8,128)S(1)}, u32[]{:S(2)}, u32[]{:S(2)}) collective-permute-start(f32[16,2,32,128]{3,2,1,0:T(8,128)S(1)} %get-tuple-element.45), channel_id=1, source_target_pairs={{0,4},{8,12},{1,5},{9,13},{2,6},{10,14},{3,7},{11,15}} | collective-permute-start | bytes 1572872 | tf_op jit(solution)/shard_map/ppermute | solution.py:240
  12.0 2.7 %collective-permute-start.7 = (f32[16,2,32,128]{3,2,1,0:T(8,128)S(1)}, f32[16,2,32,128]{3,2,1,0:T(8,128)S(1)}, u32[]{:S(2)}, u32[]{:S(2)}) collective-permute-start(f32[16,2,32,128]{3,2,1,0:T(8,128)S(1)} %get-tuple-element.45), channel_id=1, source_target_pairs={{4,8},{5,9},{6,10},{7,11}} | collective-permute-start | bytes 1572872 | tf_op jit(solution)/shard_map/ppermute | solution.py:242
  13.3 1.4 %collective-permute-start.6 = (f32[16,2,32,128]{3,2,1,0:T(8,128)S(1)}, f32[16,2,32,128]{3,2,1,0:T(8,128)S(1)}, u32[]{:S(2)}, u32[]{:S(2)}) collective-permute-start(f32[16,2,32,128]{3,2,1,0:T(8,128)S(1)} %get-tuple-element.47), channel_id=1, source_target_pairs={{8,12},{9,13},{10,14},{11,15}} | collective-permute-start | bytes 1572872 | tf_op jit(solution)/shard_map/ppermute | solution.py:240
  14.0 2.7 %collective-permute-start.9 = (f32[16,2,32,128]{3,2,1,0:T(8,128)S(1)}, f32[16,2,32,128]{3,2,1,0:T(8,128)S(1)}, u32[]{:S(2)}, u32[]{:S(2)}) collective-permute-start(f32[16,2,32,128]{3,2,1,0:T(8,128)S(1)} %get-tuple-element.47), channel_id=1, source_target_pairs={{4,8},{12,16},{5,9},{13,17},{6,10},{14,18},{7,11},{15,19}} | collective-permute-start | bytes 1572872 | tf_op jit(solution)/shard_map/ppermute | solution.py:242
  15.4 1.4 %collective-permute-start.8 = (f32[16,2,32,128]{3,2,1,0:T(8,128)S(1)}, f32[16,2,32,128]{3,2,1,0:T(8,128)S(1)}, u32[]{:S(2)}, u32[]{:S(2)}) collective-permute-start(f32[16,2,32,128]{3,2,1,0:T(8,128)S(1)} %get-tuple-element.49), channel_id=1, source_target_pairs={{8,12},{9,13},{10,14},{11,15}} | collective-permute-start | bytes 1572872 | tf_op jit(solution)/shard_map/ppermute | solution.py:240
  16.1 2.7 %collective-permute-start.11 = (f32[16,2,32,128]{3,2,1,0:T(8,128)S(1)}, f32[16,2,32,128]{3,2,1,0:T(8,128)S(1)}, u32[]{:S(2)}, u32[]{:S(2)}) collective-permute-start(f32[16,2,32,128]{3,2,1,0:T(8,128)S(1)} %get-tuple-element.49), channel_id=1, source_target_pairs={{12,16},{13,17},{14,18},{15,19}} | collective-permute-start | bytes 1572872 | tf_op jit(solution)/shard_map/ppermute | solution.py:242
  17.4 1.4 %collective-permute-start.10 = (f32[16,2,32,128]{3,2,1,0:T(8,128)S(1)}, f32[16,2,32,128]{3,2,1,0:T(8,128)S(1)}, u32[]{:S(2)}, u32[]{:S(2)}) collective-permute-start(f32[16,2,32,128]{3,2,1,0:T(8,128)S(1)} %get-tuple-element.51), channel_id=1, source_target_pairs={{8,12},{16,20},{9,13},{17,21},{10,14},{18,22},{11,15},{19,23}} | collective-permute-start | bytes 1572872 | tf_op jit(solution)/shard_map/ppermute | solution.py:240
  18.1 2.7 %collective-permute-start.13 = (f32[16,2,32,128]{3,2,1,0:T(8,128)S(1)}, f32[16,2,32,128]{3,2,1,0:T(8,128)S(1)}, u32[]{:S(2)}, u32[]{:S(2)}) collective-permute-start(f32[16,2,32,128]{3,2,1,0:T(8,128)S(1)} %get-tuple-element.51), channel_id=1, source_target_pairs={{12,16},{13,17},{14,18},{15,19}} | collective-permute-start | bytes 1572872 | tf_op jit(solution)/shard_map/ppermute | solution.py:242
  19.4 1.4 %collective-permute-start.12 = (f32[16,2,32,128]{3,2,1,0:T(8,128)S(1)}, f32[16,2,32,128]{3,2,1,0:T(8,128)S(1)}, u32[]{:S(2)}, u32[]{:S(2)}) collective-permute-start(f32[16,2,32,128]{3,2,1,0:T(8,128)S(1)} %get-tuple-element.53), channel_id=1, source_target_pairs={{16,20},{17,21},{18,22},{19,23}} | collective-permute-start | bytes 1572872 | tf_op jit(solution)/shard_map/ppermute | solution.py:240
  20.1 2.9 %collective-permute-start.15 = (f32[16,2,32,128]{3,2,1,0:T(8,128)S(1)}, f32[16,2,32,128]{3,2,1,0:T(8,128)S(1)}, u32[]{:S(2)}, u32[]{:S(2)}) collective-permute-start(f32[16,2,32,128]{3,2,1,0:T(8,128)S(1)} %get-tuple-element.53), channel_id=1, source_target_pairs={{12,16},{20,24},{13,17},{21,25},{14,18},{22,26},{15,19},{23,27}} | collective-permute-start | bytes 1572872 | tf_op jit(solution)/shard_map/ppermute | solution.py:242
  21.6 1.4 %collective-permute-start.14 = (f32[16,2,32,128]{3,2,1,0:T(8,128)S(1)}, f32[16,2,32,128]{3,2,1,0:T(8,128)S(1)}, u32[]{:S(2)}, u32[]{:S(2)}) collective-permute-start(f32[16,2,32,128]{3,2,1,0:T(8,128)S(1)} %get-tuple-element.55), channel_id=1, source_target_pairs={{16,20},{17,21},{18,22},{19,23}} | collective-permute-start | bytes 1572872 | tf_op jit(solution)/shard_map/ppermute | solution.py:240
  22.3 3.3 %collective-permute-start.17 = (f32[16,2,32,128]{3,2,1,0:T(8,128)S(1)}, f32[16,2,32,128]{3,2,1,0:T(8,128)S(1)}, u32[]{:S(2)}, u32[]{:S(2)}) collective-permute-start(f32[16,2,32,128]{3,2,1,0:T(8,128)S(1)} %get-tuple-element.55), channel_id=1, source_target_pairs={{20,24},{21,25},{22,26},{23,27}} | collective-permute-start | bytes 1572872 | tf_op jit(solution)/shard_map/ppermute | solution.py:242
  23.6 38.5 %collective-permute-start.16 = (f32[16,2,32,128]{3,2,1,0:T(8,128)S(1)}, f32[16,2,32,128]{3,2,1,0:T(8,128)S(1)}, u32[]{:S(2)}, u32[]{:S(2)}) collective-permute-start(f32[16,2,32,128]{3,2,1,0:T(8,128)S(1)} %get-tuple-element.57), channel_id=1, source_target_pairs={{16,20},{24,28},{17,21},{25,29},{18,22},{26,30},{19,23},{27,31}} | collective-permute-start | bytes 1572872 | tf_op jit(solution)/shard_map/ppermute | solution.py:240
  24.9 41.1 %collective-permute-start.19 = (f32[16,2,32,128]{3,2,1,0:T(8,128)S(1)}, f32[16,2,32,128]{3,2,1,0:T(8,128)S(1)}, u32[]{:S(2)}, u32[]{:S(2)}) collective-permute-start(f32[16,2,32,128]{3,2,1,0:T(8,128)S(1)} %get-tuple-element.57), channel_id=1, source_target_pairs={{20,24},{21,25},{22,26},{23,27}} | collective-permute-start | bytes 1572872 | tf_op jit(solution)/shard_map/ppermute | solution.py:242
  64.0 4.0 %collective-permute-start.18 = (f32[16,2,32,128]{3,2,1,0:T(8,128)S(1)}, f32[16,2,32,128]{3,2,1,0:T(8,128)S(1)}, u32[]{:S(2)}, u32[]{:S(2)}) collective-permute-start(f32[16,2,32,128]{3,2,1,0:T(8,128)S(1)} %get-tuple-element.59), channel_id=1, source_target_pairs={{24,28},{25,29},{26,30},{27,31}} | collective-permute-start | bytes 1572872 | tf_op jit(solution)/shard_map/ppermute | solution.py:240
  65.3 6.0 %collective-permute-start.21 = (f32[16,2,32,128]{3,2,1,0:T(8,128)S(1)}, f32[16,2,32,128]{3,2,1,0:T(8,128)S(1)}, u32[]{:S(2)}, u32[]{:S(2)}) collective-permute-start(f32[16,2,32,128]{3,2,1,0:T(8,128)S(1)} %get-tuple-element.59), channel_id=1, source_target_pairs={{20,24},{21,25},{22,26},{23,27}} | collective-permute-start | bytes 1572872 | tf_op jit(solution)/shard_map/ppermute | solution.py:242
  70.0 6.9 %collective-permute-start.20 = (f32[16,2,32,128]{3,2,1,0:T(8,128)S(1)}, f32[16,2,32,128]{3,2,1,0:T(8,128)S(1)}, u32[]{:S(2)}, u32[]{:S(2)}) collective-permute-start(f32[16,2,32,128]{3,2,1,0:T(8,128)S(1)} %get-tuple-element.61), channel_id=1, source_target_pairs={{24,28},{25,29},{26,30},{27,31}} | collective-permute-start | bytes 1572872 | tf_op jit(solution)/shard_map/ppermute | solution.py:240
  78.9 3.8 %collective-permute-start.22 = (f32[16,2,32,128]{3,2,1,0:T(8,128)S(1)}, f32[16,2,32,128]{3,2,1,0:T(8,128)S(1)}, u32[]{:S(2)}, u32[]{:S(2)}) collective-permute-start(f32[16,2,32,128]{3,2,1,0:T(8,128)S(1)} %get-tuple-element.65), channel_id=1, source_target_pairs={{24,28},{25,29},{26,30},{27,31}} | collective-permute-start | bytes 1572872 | tf_op jit(solution)/shard_map/ppermute | solution.py:240
  86.4 10.1 %collective-permute-start.23 = (f32[2,128,128]{2,1,0:T(8,128)S(1)}, f32[2,128,128]{2,1,0:T(8,128)S(1)}, u32[]{:S(2)}, u32[]{:S(2)}) collective-permute-start(f32[2,128,128]{2,1,0:T(8,128)S(1)} %get-tuple-element.68), channel_id=1, source_target_pairs={{0,1},{1,2},{2,3},{3,0},{4,5},{5,6},{6,7},{7,4},{8,9},{9,10},{10,1... | collective-permute-start | bytes 393224 | tf_op jit(solution)/shard_map/ppermute | solution.py:265
  87.7 10.9 %collective-permute-start.24 = (f32[2,128,128]{2,1,0:T(8,128)S(1)}, f32[2,128,128]{2,1,0:T(8,128)S(1)}, u32[]{:S(2)}, u32[]{:S(2)}) collective-permute-start(f32[2,128,128]{2,1,0:T(8,128)S(1)} %get-tuple-element.69), channel_id=1, source_target_pairs={{0,2},{1,3},{2,0},{3,1},{4,6},{5,7},{6,4},{7,5},{8,10},{9,11},{10,... | collective-permute-start | bytes 393224 | tf_op jit(solution)/shard_map/ppermute | solution.py:265
  88.8 11.3 %collective-permute-start.25 = (f32[2,128,128]{2,1,0:T(8,128)S(1)}, f32[2,128,128]{2,1,0:T(8,128)S(1)}, u32[]{:S(2)}, u32[]{:S(2)}) collective-permute-start(f32[2,128,128]{2,1,0:T(8,128)S(1)} %get-tuple-element.70), channel_id=1, source_target_pairs={{0,3},{1,0},{2,1},{3,2},{4,7},{5,4},{6,5},{7,6},{8,11},{9,8},{10,9... | collective-permute-start | bytes 393224 | tf_op jit(solution)/shard_map/ppermute | solution.py:265

commit v2 on v0

v2 whole, which is shorter than its diff:
```python
import functools
import math

import jax
import jax.numpy as jnp
from jax import lax
from jax.experimental import pallas as pl
from jax.experimental.pallas import tpu as pltpu
from jax.sharding import PartitionSpec as P

PARTS = (1, 1, 1, 1, 1, 1, 1, 1)
CHUNKS = 4
DELAY = 3
SMEM = pl.BlockSpec(memory_space=pltpu.SMEM)
VMEM = pl.BlockSpec(memory_space=pltpu.VMEM)
HBM = pl.BlockSpec(memory_space=pltpu.HBM)


def entry_turn(depth):
    return DELAY * depth


def taper_row(block, block_rows, width):
    lateral = block_rows * width
    position = block * width + lax.broadcasted_iota(jnp.int32, (1, width), 1)
    distance = jnp.minimum(position, lateral - 1 - position).astype(jnp.float32)
    edge_ramp = jnp.maximum(0.0, 1.0 - distance / (lateral // 32))
    return 1.0 - 0.3 * edge_ramp * edge_ramp


def split_halves(value):
    high = value.astype(jnp.bfloat16)
    low = (value - high.astype(jnp.float32)).astype(jnp.bfloat16)
    return high, low


def any_of(group, members):
    found = group == members[0]
    for member in members[1:]:
        found = jnp.logical_or(found, group == member)
    return found


def propagate_kernel(*refs, turn, sizes, offsets, classes, arrived, send):
    refs = list(refs)
    first = turn == 0
    if first:
        columns_in, pairs_in, propagator = refs[:3]
        del refs[:3]
    else:
        columns, operator, kept_in = refs[:3]
        del refs[:3]
    arrived = {c: refs.pop(0) for c in arrived}
    surface = [refs.pop(0), refs.pop(0)] if turn < len(sizes) else None
    if first:
        columns, pairs, operator = refs[:3]
        del refs[:3]
    kept = refs.pop(0)
    outs = {c: refs.pop(0) for c in send}
    splits = {c: refs.pop(0) for c in classes}
    if surface:
        drawn, surface_sems = refs[:2]
        del refs[:2]
    block_rows, nnz = operator.shape[:2]
    width = operator.shape[-1]
    depth = lax.axis_index("depth")
    group = turn - entry_turn(depth)

    def chunk(k):
        rows = pl.ds(k * (block_rows // CHUNKS), block_rows // CHUNKS)
        return pltpu.make_async_copy(
            propagator.at[0, 0, rows], operator.at[rows], refs[0].at[k])

    if surface:
        draws = [
            pltpu.make_async_copy(
                surface[k].at[0, :, pl.ds(offsets[turn], sizes[turn]), :],
                drawn.at[k], surface_sems.at[k])
            for k in range(2)
        ]

        @pl.when(depth == 0)
        def _():
            for copy in draws:
                copy.start()

    if first:
        for k in range(CHUNKS):
            chunk(k).start()
        tables = [pltpu.make_async_copy(columns_in, columns, refs[1].at[0]),
                  pltpu.make_async_copy(pairs_in, pairs, refs[1].at[1])]
        for copy in tables:
            copy.start()
        for copy in tables:
            copy.wait()

    def level(shots):
        rows = 2 * shots
        split = splits[shots]
        members = [g for g in range(len(sizes)) if sizes[g] == shots]

        def put(block, part, value):
            high, low = split_halves(value)
            split[block, part * rows:(part + 1) * rows, :] = high
            split[block, (2 + part) * rows:(3 + part) * rows, :] = low

        if surface and sizes[turn] == shots:
            @pl.when(depth == 0)
            def _():
                for copy in draws:
                    copy.wait()
                for block in range(block_rows):
                    lanes = slice(block * width, (block + 1) * width)
                    for part in range(2):
                        receiver = drawn[1, part, :, lanes]
                        if part == 1:
                            receiver = -receiver
                        put(block, part, jnp.concatenate(
                            [drawn[0, part, :, lanes], receiver], axis=0))

        if shots in arrived:
            @pl.when(depth > 0)
            def _():
                for block in range(block_rows):
                    for part in range(2):
                        put(block, part, arrived[shots][block, part])

        start = jnp.int32(0)
        for member in members:
            start = jnp.where(group == member, offsets[member], start)
        start = pl.multiple_of(start, 8)
        place = pl.ds(start, shots)

        for r in range(block_rows):
            if first and r % (block_rows // CHUNKS) == 0:
                chunk(r // (block_rows // CHUNKS)).wait()
            picked = jnp.concatenate(
                [split[columns[j, 0, r]] for j in range(nnz)], axis=1
            )
            real = operator[r, :, 0].reshape(nnz * width, width)
            imag = operator[r, :, 1].reshape(nnz * width, width)
            weights = jnp.concatenate([real, imag], axis=1)
            product = jnp.dot(picked, weights, preferred_element_type=jnp.float32)
            product = product[: 2 * rows] + product[2 * rows:]
            scale = taper_row(r, block_rows, width)
            real_out = (product[:rows, :width] - product[rows:, width:]) * scale
            imag_out = (product[rows:, :width] + product[:rows, width:]) * scale
            for part, value in ((0, real_out), (1, imag_out)):
                if shots in send:
                    outs[shots][r, part] = value
                kept[r, part, 0, place, :] = value[:shots]
                kept[r, part, 1, place, :] = value[shots:]

    for shots in classes:
        members = [g for g in range(len(sizes)) if sizes[g] == shots]
        pl.when(any_of(group, members))(functools.partial(level, shots))

    if first:
        @pl.when(depth > 0)
        def _():
            for k in range(CHUNKS):
                chunk(k).wait()


def image_block(pairs, index, kept, shots, scale):
    a = pairs[0, 0, index]
    b = pairs[0, 1, index]
    left = jnp.concatenate([kept[a, 0, 0, shots, :], kept[a, 1, 0, shots, :]], axis=0) * scale
    right = jnp.concatenate([kept[b, 0, 1, shots, :], -kept[b, 1, 1, shots, :]], axis=0)
    left_high, left_low = split_halves(left)
    right_high, right_low = split_halves(right)
    lhs = jnp.concatenate([left_high, left_high, left_low], axis=0)
    rhs = jnp.concatenate([right_high, right_low, right_high], axis=0)
    return lax.dot_general(
        lhs, rhs, (((0,), (0,)), ((), ())), preferred_element_type=jnp.float32
    )


def early_kernel(pairs, kept_in, kept, out, *, shots, scale):
    for index in range(out.shape[0]):
        out[index] = image_block(pairs, index, kept_in, shots, scale)


def last_kernel(pairs, early, kept, *outs, shots, scale):
    share = outs[0].shape[0]
    parts = len(outs)
    own = lax.axis_index("freq")
    for step in range(parts):
        owner = lax.rem(own + step, parts)
        for index in range(share):
            pair = owner * share + index
            outs[step][index] = early[pair] + image_block(pairs, pair, kept, shots, scale)


def shards(source_field, receiver_data, propagator, block_columns, image_pairs):
    depth_count = lax.axis_size("depth")
    freq_count = lax.axis_size("freq")
    shots_all, lateral = source_field.shape[2:]
    block_rows, nnz = propagator.shape[2:4]
    width = propagator.shape[-1]
    pair_count = image_pairs.shape[1]
    unit = shots_all // sum(PARTS)
    sizes = [unit * part for part in PARTS]
    offsets = [sum(sizes[:g]) for g in range(len(sizes))]
    groups = len(sizes)
    scale = 1.0 / math.sqrt(2.0 * shots_all * freq_count)
    kept_type = pltpu.VMEM((block_rows, 2, 2, shots_all, width), jnp.float32)
    params = pltpu.CompilerParams(vmem_limit_bytes=16 * 1024 * 1024)
    turns = groups + entry_turn(depth_count - 1)

    def hbm(value):
        return pltpu.with_memory_space_constraint(value, pltpu.HBM)

    source_field, receiver_data, propagator = map(hbm, (source_field, receiver_data, propagator))

    def size_of(d, turn):
        group = turn - entry_turn(d)
        return sizes[group] if 0 <= group < groups else None

    sent = {}
    for turn in range(turns):
        arrived = sent.pop(turn - DELAY, {})
        present = [size_of(d, turn) for d in range(depth_count)]
        classes = sorted({c for c in present if c})
        send = sorted({c for c in present[:-1] if c})
        if turn == 0:
            columns_in = hbm(block_columns.transpose(2, 0, 1))
            pairs_in = hbm(image_pairs.transpose(0, 2, 1))
            operands = [columns_in, pairs_in, propagator]
            specs = [HBM, HBM, HBM]
            out_shape = [pltpu.SMEM(columns_in.shape, jnp.int32),
                         pltpu.SMEM(pairs_in.shape, jnp.int32),
                         pltpu.VMEM(propagator.shape[2:], propagator.dtype),
                         kept_type]
            out_specs = [SMEM, SMEM, VMEM, VMEM]
            aliases = {}
        else:
            operands = [columns, operator, kept]
            specs = [SMEM, VMEM, VMEM]
            out_shape = [kept_type]
            out_specs = [VMEM]
            aliases = {2: 0}
        operands += list(arrived.values())
        specs += [VMEM] * len(arrived)
        out_shape += [pltpu.VMEM((block_rows, 2, 2 * c, width), jnp.float32) for c in send]
        out_specs += [VMEM] * len(send)
        scratch = [pltpu.VMEM((block_rows, 8 * c, width), jnp.bfloat16) for c in classes]
        if turn < groups:
            operands += [source_field, receiver_data]
            specs += [HBM, HBM]
            scratch += [pltpu.VMEM((2, 2, sizes[turn], lateral), jnp.float32),
                        pltpu.SemaphoreType.DMA((2,))]
        if turn == 0:
            scratch += [pltpu.SemaphoreType.DMA((CHUNKS,)), pltpu.SemaphoreType.DMA((2,))]
        results = pl.pallas_call(
            functools.partial(
                propagate_kernel, turn=turn, sizes=sizes, offsets=offsets, classes=classes,
                arrived=list(arrived), send=send),
            out_shape=out_shape,
            in_specs=specs,
            out_specs=out_specs,
            input_output_aliases=aliases,
            scratch_shapes=scratch,
            compiler_params=params,
            cost_estimate=pl.CostEstimate(flops=0, bytes_accessed=0, transcendentals=0),
        )(*operands)
        if turn == 0:
            columns, pairs, operator = results[:3]
            results = results[3:]
        kept = results[0]
        fields = dict(zip(send, results[1:]))
        sent[turn] = {
            c: lax.ppermute(fields[c], "depth", [
                (d, d + 1) for d in range(depth_count - 1) if size_of(d, turn) == c])
            for c in send
        }
        if turn == turns - 2:
            image_type = pltpu.VMEM((pair_count, width, width), jnp.float32)
            kept, early = pl.pallas_call(
                functools.partial(early_kernel, shots=slice(0, offsets[-1]), scale=scale),
                out_shape=(kept_type, image_type),
                in_specs=[SMEM, VMEM],
                out_specs=(VMEM, VMEM),
                input_output_aliases={1: 0},
                compiler_params=params,
            )(pairs, kept)

    share = pair_count // freq_count
    share_type = pltpu.VMEM((share, width, width), jnp.float32)
    shares = pl.pallas_call(
        functools.partial(last_kernel, shots=slice(offsets[-1], shots_all), scale=scale),
        out_shape=(share_type,) * freq_count,
        in_specs=[SMEM, VMEM, VMEM],
        out_specs=(VMEM,) * freq_count,
        compiler_params=params,
    )(pairs, early, kept)
    total = shares[0]
    for step in range(1, freq_count):
        total += lax.ppermute(
            shares[step], "freq", [(f, (f + step) % freq_count) for f in range(freq_count)])
    return total[None]


def solution(mesh):
    placed = (
        P("freq", None, None, None),
        P("freq", None, None, None),
        P("freq", "depth", None, None, None, None, None),
        P("depth", None, None),
        P("depth", None, None),
    )
    return jax.shard_map(
        shards,
        mesh=mesh,
        in_specs=placed,
        out_specs=P("depth", "freq", None, None),
        check_vma=False,
    )
```

time: 325 us -> 83.3 us (0.26)
  the two profiles are of different devices: /device:TPU:0 before, /device:TPU:15 now
where the time goes in v2:
time: 83.3 us; the launch traced here: 82.8 us
  waiting for transfers between devices  40.6 us (49%)
  starting transfers between devices  26.4 us (32%)
  Pallas kernels  14.5 us (17%)
    ppermute x26, waiting for transfers between devices, shards(): lax.ppermute(fields[c], 'depth', [(d, d + 1) for d in range(depth_count -...  30.6 us
    ppermute x26, starting transfers between devices, shards(): lax.ppermute(fields[c], 'depth', [(d, d + 1) for d in range(depth_count -...  22.5 us
    pallas_call x29, Pallas kernels, shards(): pl.pallas_call(functools.partial(propagate_kernel, turn=turn, sizes=sizes...  13.8 us
    ppermute x3, waiting for transfers between devices, shards(): lax.ppermute(shares[step], 'freq', [(f, (f + step) % freq_count) for f in...  10.1 us
    ppermute x3, starting transfers between devices, shards(): lax.ppermute(shares[step], 'freq', [(f, (f + step) % freq_count) for f in...  3.83 us
  transfers between devices with their start and end apart: 29, of which 10 were waited for; matrix products, arithmetic and copies ran while one was open for 0% of the time, Pallas kernels for 12%

profile of v2, /device:TPU:15, one launch (start us, length us, event | category | flops | bytes accessed | tf_op | source)
XLA Modules:
  0.0 82.8 jit_solution(15738175708708001425)
XLA Ops:
  0.0 2.9 %shard_map.55 = (s32[6,1,16]{2,1,0:T(1,128)S(4)}, s32[1,2,8]{2,1,0:T(2,128)S(4)}, bf16[16,6,2,128,128]{4,3,2,1,0:T(8,128)(2,1)S(1)}, f32[16,2,2,64,128]{4,3,2,1,0:T(8,128)S(1)}, f32[16,2,16,128]{3,2,1,0:T(8,128)S(1)}) custom-call(s32[6,1,16]{2,1,0:T(1,128)} %bitcast.4, s32[1,2,8]{2,1,0:T(2,128)} %bitcast.5, bf16[1,1,16,6,2,128,128]{6,5,4,3,2,1,0:T(8,128)(2,1)} %refs_2_.1, ...), custom_call_target="tpu_custom_call" | custom-call | tf_op jit(solution)/shard_map/pallas_call | solution.py:255
  2.9 0.7 collective-permute-start
  3.6 0.7 collective-permute-start.1
  4.4 0.7 collective-permute-start.2
  5.1 0.0 collective-permute-done.refs_3_
  5.1 0.7 collective-permute-start.3
  5.8 0.0 collective-permute-done.1.refs_3_
  5.9 0.7 collective-permute-start.4
  6.6 0.0 collective-permute-done.2.refs_3_
  6.6 0.7 collective-permute-start.5
  7.4 0.7 collective-permute-start.6
  8.1 0.7 collective-permute-start.7
  8.8 0.0 collective-permute-done.5.refs_3_
  8.9 0.7 collective-permute-start.8
  9.6 0.7 collective-permute-start.9
  10.3 0.0 collective-permute-done.7.refs_3_
  10.3 0.7 collective-permute-start.10
  11.0 0.2 shard_map.66
  11.2 0.7 collective-permute-start.11
  11.9 0.0 collective-permute-done.9.refs_3_
  11.9 0.7 collective-permute-start.12
  12.7 0.7 collective-permute-start.13
  13.4 0.0 collective-permute-done.11.refs_3_
  13.4 0.7 collective-permute-start.14
  14.1 0.7 collective-permute-start.15
  14.8 0.0 collective-permute-done.13.refs_3_
  14.9 0.7 collective-permute-start.16
  15.5 0.0 collective-permute-done.14.refs_3_
  15.6 0.7 collective-permute-start.17
  16.3 1.3 %collective-permute-start.18 = (f32[16,2,16,128]{3,2,1,0:T(8,128)S(1)}, f32[16,2,16,128]{3,2,1,0:T(8,128)S(1)}, u32[]{:S(2)}, u32[]{:S(2)}) collective-permute-start(f32[16,2,16,128]{3,2,1,0:T(8,128)S(1)} %get-tuple-element.108), channel_id=1, source_target_pairs={{16,20},{20,24},{24,28},{17,21},{21,25},{25,29},{18,22},{22,26},{2... | collective-permute-start | bytes 786440 | tf_op jit(solution)/shard_map/ppermute | solution.py:273
  17.6 0.0 collective-permute-done.16.refs_3_
  17.6 1.3 %collective-permute-start.19 = (f32[16,2,16,128]{3,2,1,0:T(8,128)S(1)}, f32[16,2,16,128]{3,2,1,0:T(8,128)S(1)}, u32[]{:S(2)}, u32[]{:S(2)}) collective-permute-start(f32[16,2,16,128]{3,2,1,0:T(8,128)S(1)} %get-tuple-element.110), channel_id=1, source_target_pairs={{16,20},{20,24},{24,28},{17,21},{21,25},{25,29},{18,22},{22,26},{2... | collective-permute-start | bytes 786440 | tf_op jit(solution)/shard_map/ppermute | solution.py:273
  18.9 0.0 collective-permute-done.17.refs_3_
  19.0 1.3 %collective-permute-start.20 = (f32[16,2,16,128]{3,2,1,0:T(8,128)S(1)}, f32[16,2,16,128]{3,2,1,0:T(8,128)S(1)}, u32[]{:S(2)}, u32[]{:S(2)}) collective-permute-start(f32[16,2,16,128]{3,2,1,0:T(8,128)S(1)} %get-tuple-element.112), channel_id=1, source_target_pairs={{20,24},{24,28},{21,25},{25,29},{22,26},{26,30},{23,27},{27,31}} | collective-permute-start | bytes 786440 | tf_op jit(solution)/shard_map/ppermute | solution.py:273
  20.3 23.8 %collective-permute-done.18.refs_3_ = f32[16,2,16,128]{3,2,1,0:T(8,128)S(1)} collective-permute-done((f32[16,2,16,128]{3,2,1,0:T(8,128)S(1)}, f32[16,2,16,128]{3,2,1,0:T(8,128)S(1)}, u32[]{:S(2)}, u32[]{:S(2)}) %collective-permute-start.18) | collective-permute-done | bytes 262176 | tf_op jit(solution)/shard_map/ppermute | solution.py:273
  44.1 1.2 %shard_map.76 = (f32[16,2,2,64,128]{4,3,2,1,0:T(8,128)S(1)}, f32[16,2,16,128]{3,2,1,0:T(8,128)S(1)}) custom-call(s32[6,1,16]{2,1,0:T(1,128)S(4)} %get-tuple-element.67.refs_0_, bf16[16,6,2,128,128]{4,3,2,1,0:T(8,128)(2,1)S(1)} %get-tuple-element.68.refs_1_, f32[16,2,2,64,128]{4,3,2,1,0:T(8,128)S(1)} %get-tuple-element.107.refs_2_, ...), custom_call_target="tpu_custom_call", output_to_operand_aliasing={{0}: (2, {})} | custom-call | tf_op jit(solution)/shard_map/pallas_call | solution.py:255
  45.3 1.3 %collective-permute-start.21 = (f32[16,2,16,128]{3,2,1,0:T(8,128)S(1)}, f32[16,2,16,128]{3,2,1,0:T(8,128)S(1)}, u32[]{:S(2)}, u32[]{:S(2)}) collective-permute-start(f32[16,2,16,128]{3,2,1,0:T(8,128)S(1)} %get-tuple-element.114), channel_id=1, source_target_pairs={{20,24},{24,28},{21,25},{25,29},{22,26},{26,30},{23,27},{27,31}} | collective-permute-start | bytes 786440 | tf_op jit(solution)/shard_map/ppermute | solution.py:273
  46.6 1.0 %collective-permute-done.19.refs_3_ = f32[16,2,16,128]{3,2,1,0:T(8,128)S(1)} collective-permute-done((f32[16,2,16,128]{3,2,1,0:T(8,128)S(1)}, f32[16,2,16,128]{3,2,1,0:T(8,128)S(1)}, u32[]{:S(2)}, u32[]{:S(2)}) %collective-permute-start.19) | collective-permute-done | bytes 262176 | tf_op jit(solution)/shard_map/ppermute | solution.py:273
  47.6 1.2 %shard_map.77 = (f32[16,2,2,64,128]{4,3,2,1,0:T(8,128)S(1)}, f32[16,2,16,128]{3,2,1,0:T(8,128)S(1)}) custom-call(s32[6,1,16]{2,1,0:T(1,128)S(4)} %get-tuple-element.67.refs_0_, bf16[16,6,2,128,128]{4,3,2,1,0:T(8,128)(2,1)S(1)} %get-tuple-element.68.refs_1_, f32[16,2,2,64,128]{4,3,2,1,0:T(8,128)S(1)} %get-tuple-element.109.refs_2_, ...), custom_call_target="tpu_custom_call", output_to_operand_aliasing={{0}: (2, {})} | custom-call | tf_op jit(solution)/shard_map/pallas_call | solution.py:255
  48.9 1.3 %collective-permute-start.22 = (f32[16,2,16,128]{3,2,1,0:T(8,128)S(1)}, f32[16,2,16,128]{3,2,1,0:T(8,128)S(1)}, u32[]{:S(2)}, u32[]{:S(2)}) collective-permute-start(f32[16,2,16,128]{3,2,1,0:T(8,128)S(1)} %get-tuple-element.116), channel_id=1, source_target_pairs={{20,24},{24,28},{21,25},{25,29},{22,26},{26,30},{23,27},{27,31}} | collective-permute-start | bytes 786440 | tf_op jit(solution)/shard_map/ppermute | solution.py:273
  50.2 1.2 %collective-permute-done.20.refs_3_ = f32[16,2,16,128]{3,2,1,0:T(8,128)S(1)} collective-permute-done((f32[16,2,16,128]{3,2,1,0:T(8,128)S(1)}, f32[16,2,16,128]{3,2,1,0:T(8,128)S(1)}, u32[]{:S(2)}, u32[]{:S(2)}) %collective-permute-start.20) | collective-permute-done | bytes 262176 | tf_op jit(solution)/shard_map/ppermute | solution.py:273
  51.3 1.2 %shard_map.78 = (f32[16,2,2,64,128]{4,3,2,1,0:T(8,128)S(1)}, f32[16,2,16,128]{3,2,1,0:T(8,128)S(1)}) custom-call(s32[6,1,16]{2,1,0:T(1,128)S(4)} %get-tuple-element.67.refs_0_, bf16[16,6,2,128,128]{4,3,2,1,0:T(8,128)(2,1)S(1)} %get-tuple-element.68.refs_1_, f32[16,2,2,64,128]{4,3,2,1,0:T(8,128)S(1)} %get-tuple-element.111.refs_2_, ...), custom_call_target="tpu_custom_call", output_to_operand_aliasing={{0}: (2, {})} | custom-call | tf_op jit(solution)/shard_map/pallas_call | solution.py:255
  52.6 1.3 %collective-permute-start.23 = (f32[16,2,16,128]{3,2,1,0:T(8,128)S(1)}, f32[16,2,16,128]{3,2,1,0:T(8,128)S(1)}, u32[]{:S(2)}, u32[]{:S(2)}) collective-permute-start(f32[16,2,16,128]{3,2,1,0:T(8,128)S(1)} %get-tuple-element.118), channel_id=1, source_target_pairs={{24,28},{25,29},{26,30},{27,31}} | collective-permute-start | bytes 786440 | tf_op jit(solution)/shard_map/ppermute | solution.py:273
  53.9 0.9 %collective-permute-done.21.refs_3_ = f32[16,2,16,128]{3,2,1,0:T(8,128)S(1)} collective-permute-done((f32[16,2,16,128]{3,2,1,0:T(8,128)S(1)}, f32[16,2,16,128]{3,2,1,0:T(8,128)S(1)}, u32[]{:S(2)}, u32[]{:S(2)}) %collective-permute-start.21) | collective-permute-done | bytes 262176 | tf_op jit(solution)/shard_map/ppermute | solution.py:273
  54.7 1.5 %shard_map.79 = (f32[16,2,2,64,128]{4,3,2,1,0:T(8,128)S(1)}, f32[16,2,16,128]{3,2,1,0:T(8,128)S(1)}) custom-call(s32[6,1,16]{2,1,0:T(1,128)S(4)} %get-tuple-element.67.refs_0_, bf16[16,6,2,128,128]{4,3,2,1,0:T(8,128)(2,1)S(1)} %get-tuple-element.68.refs_1_, f32[16,2,2,64,128]{4,3,2,1,0:T(8,128)S(1)} %get-tuple-element.113.refs_2_, ...), custom_call_target="tpu_custom_call", output_to_operand_aliasing={{0}: (2, {})} | custom-call | tf_op jit(solution)/shard_map/pallas_call | solution.py:255
  56.2 1.3 %collective-permute-start.24 = (f32[16,2,16,128]{3,2,1,0:T(8,128)S(1)}, f32[16,2,16,128]{3,2,1,0:T(8,128)S(1)}, u32[]{:S(2)}, u32[]{:S(2)}) collective-permute-start(f32[16,2,16,128]{3,2,1,0:T(8,128)S(1)} %get-tuple-element.119), channel_id=1, source_target_pairs={{24,28},{25,29},{26,30},{27,31}} | collective-permute-start | bytes 786440 | tf_op jit(solution)/shard_map/ppermute | solution.py:273
  57.5 0.8 collective-permute-done.22.refs_3_
  58.3 1.2 %shard_map.80 = (f32[16,2,2,64,128]{4,3,2,1,0:T(8,128)S(1)}, f32[16,2,16,128]{3,2,1,0:T(8,128)S(1)}) custom-call(s32[6,1,16]{2,1,0:T(1,128)S(4)} %get-tuple-element.67.refs_0_, bf16[16,6,2,128,128]{4,3,2,1,0:T(8,128)(2,1)S(1)} %get-tuple-element.68.refs_1_, f32[16,2,2,64,128]{4,3,2,1,0:T(8,128)S(1)} %get-tuple-element.115.refs_2_, ...), custom_call_target="tpu_custom_call", output_to_operand_aliasing={{0}: (2, {})} | custom-call | tf_op jit(solution)/shard_map/pallas_call | solution.py:255
  59.6 1.3 %collective-permute-start.25 = (f32[16,2,16,128]{3,2,1,0:T(8,128)S(1)}, f32[16,2,16,128]{3,2,1,0:T(8,128)S(1)}, u32[]{:S(2)}, u32[]{:S(2)}) collective-permute-start(f32[16,2,16,128]{3,2,1,0:T(8,128)S(1)} %get-tuple-element.122), channel_id=1, source_target_pairs={{24,28},{25,29},{26,30},{27,31}} | collective-permute-start | bytes 786440 | tf_op jit(solution)/shard_map/ppermute | solution.py:273
  60.9 0.0 collective-permute-done.23.refs_3_
  60.9 1.2 %shard_map.81.refs_2_ = f32[16,2,2,64,128]{4,3,2,1,0:T(8,128)S(1)} custom-call(s32[6,1,16]{2,1,0:T(1,128)S(4)} %get-tuple-element.67.refs_0_, bf16[16,6,2,128,128]{4,3,2,1,0:T(8,128)(2,1)S(1)} %get-tuple-element.68.refs_1_, f32[16,2,2,64,128]{4,3,2,1,0:T(8,128)S(1)} %get-tuple-element.117.refs_2_, ...), custom_call_target="tpu_custom_call", output_to_operand_aliasing={{}: (2, {})} | custom-call | tf_op jit(solution)/shard_map/pallas_call | solution.py:255
  62.1 1.6 %collective-permute-done.24.refs_3_ = f32[16,2,16,128]{3,2,1,0:T(8,128)S(1)} collective-permute-done((f32[16,2,16,128]{3,2,1,0:T(8,128)S(1)}, f32[16,2,16,128]{3,2,1,0:T(8,128)S(1)}, u32[]{:S(2)}, u32[]{:S(2)}) %collective-permute-start.24) | collective-permute-done | bytes 262176 | tf_op jit(solution)/shard_map/ppermute | solution.py:273
  63.7 1.2 %shard_map.82.kept_in = f32[16,2,2,64,128]{4,3,2,1,0:T(8,128)S(1)} custom-call(s32[6,1,16]{2,1,0:T(1,128)S(4)} %get-tuple-element.67.refs_0_, bf16[16,6,2,128,128]{4,3,2,1,0:T(8,128)(2,1)S(1)} %get-tuple-element.68.refs_1_, f32[16,2,2,64,128]{4,3,2,1,0:T(8,128)S(1)} %shard_map.81.refs_2_, ...), custom_call_target="tpu_custom_call", output_to_operand_aliasing={{}: (2, {})} | custom-call | tf_op jit(solution)/shard_map/pallas_call | solution.py:255
  64.9 0.4 shard_map.83
  65.4 1.3 %collective-permute-done.25.refs_3_ = f32[16,2,16,128]{3,2,1,0:T(8,128)S(1)} collective-permute-done((f32[16,2,16,128]{3,2,1,0:T(8,128)S(1)}, f32[16,2,16,128]{3,2,1,0:T(8,128)S(1)}, u32[]{:S(2)}, u32[]{:S(2)}) %collective-permute-start.25) | collective-permute-done | bytes 262176 | tf_op jit(solution)/shard_map/ppermute | solution.py:273
  66.6 1.2 %shard_map.84.kept = f32[16,2,2,64,128]{4,3,2,1,0:T(8,128)S(1)} custom-call(s32[6,1,16]{2,1,0:T(1,128)S(4)} %get-tuple-element.67.refs_0_, bf16[16,6,2,128,128]{4,3,2,1,0:T(8,128)(2,1)S(1)} %get-tuple-element.68.refs_1_, f32[16,2,2,64,128]{4,3,2,1,0:T(8,128)S(1)} %get-tuple-element.121.refs_2_, ...), custom_call_target="tpu_custom_call", output_to_operand_aliasing={{}: (2, {})} | custom-call | tf_op jit(solution)/shard_map/pallas_call | solution.py:255
  67.9 0.3 shard_map.85
  68.2 1.4 %collective-permute-start.26 = (f32[2,128,128]{2,1,0:T(8,128)S(1)}, f32[2,128,128]{2,1,0:T(8,128)S(1)}, u32[]{:S(2)}, u32[]{:S(2)}) collective-permute-start(f32[2,128,128]{2,1,0:T(8,128)S(1)} %get-tuple-element.124), channel_id=1, source_target_pairs={{0,1},{1,2},{2,3},{3,0},{4,5},{5,6},{6,7},{7,4},{8,9},{9,10},{10,1... | collective-permute-start | bytes 393224 | tf_op jit(solution)/shard_map/ppermute | solution.py:299
  69.5 1.1 %collective-permute-start.27 = (f32[2,128,128]{2,1,0:T(8,128)S(1)}, f32[2,128,128]{2,1,0:T(8,128)S(1)}, u32[]{:S(2)}, u32[]{:S(2)}) collective-permute-start(f32[2,128,128]{2,1,0:T(8,128)S(1)} %get-tuple-element.125), channel_id=1, source_target_pairs={{0,2},{1,3},{2,0},{3,1},{4,6},{5,7},{6,4},{7,5},{8,10},{9,11},{10,... | collective-permute-start | bytes 393224 | tf_op jit(solution)/shard_map/ppermute | solution.py:299
  70.6 1.4 %collective-permute-start.28 = (f32[2,128,128]{2,1,0:T(8,128)S(1)}, f32[2,128,128]{2,1,0:T(8,128)S(1)}, u32[]{:S(2)}, u32[]{:S(2)}) collective-permute-start(f32[2,128,128]{2,1,0:T(8,128)S(1)} %get-tuple-element.126), channel_id=1, source_target_pairs={{0,3},{1,0},{2,1},{3,2},{4,7},{5,4},{6,5},{7,6},{8,11},{9,8},{10,9... | collective-permute-start | bytes 393224 | tf_op jit(solution)/shard_map/ppermute | solution.py:299
  72.0 6.3 %collective-permute-done.26 = f32[2,128,128]{2,1,0:T(8,128)S(1)} collective-permute-done((f32[2,128,128]{2,1,0:T(8,128)S(1)}, f32[2,128,128]{2,1,0:T(8,128)S(1)}, u32[]{:S(2)}, u32[]{:S(2)}) %collective-permute-start.26) | collective-permute-done | bytes 131104 | tf_op jit(solution)/shard_map/ppermute | solution.py:299
  78.2 2.3 %collective-permute-done.27 = f32[2,128,128]{2,1,0:T(8,128)S(1)} collective-permute-done((f32[2,128,128]{2,1,0:T(8,128)S(1)}, f32[2,128,128]{2,1,0:T(8,128)S(1)}, u32[]{:S(2)}, u32[]{:S(2)}) %collective-permute-start.27) | collective-permute-done | bytes 131104 | tf_op jit(solution)/shard_map/ppermute | solution.py:299
  80.6 1.5 %collective-permute-done.28 = f32[2,128,128]{2,1,0:T(8,128)S(1)} collective-permute-done((f32[2,128,128]{2,1,0:T(8,128)S(1)}, f32[2,128,128]{2,1,0:T(8,128)S(1)}, u32[]{:S(2)}, u32[]{:S(2)}) %collective-permute-start.28) | collective-permute-done | bytes 131104 | tf_op jit(solution)/shard_map/ppermute | solution.py:299
  82.1 0.7 add_bitcast_fusion
  (26 shorter events, 0.6 us)
Async XLA Ops:
  2.9 2.2 %collective-permute-start = (f32[16,2,16,128]{3,2,1,0:T(8,128)S(1)}, f32[16,2,16,128]{3,2,1,0:T(8,128)S(1)}, u32[]{:S(2)}, u32[]{:S(2)}) collective-permute-start(f32[16,2,16,128]{3,2,1,0:T(8,128)S(1)} %get-tuple-element.72), channel_id=1, source_target_pairs={{0,4},{1,5},{2,6},{3,7}} | collective-permute-start | bytes 786440 | tf_op jit(solution)/shard_map/ppermute | solution.py:273
  3.6 2.2 %collective-permute-start.1 = (f32[16,2,16,128]{3,2,1,0:T(8,128)S(1)}, f32[16,2,16,128]{3,2,1,0:T(8,128)S(1)}, u32[]{:S(2)}, u32[]{:S(2)}) collective-permute-start(f32[16,2,16,128]{3,2,1,0:T(8,128)S(1)} %get-tuple-element.74), channel_id=1, source_target_pairs={{0,4},{1,5},{2,6},{3,7}} | collective-permute-start | bytes 786440 | tf_op jit(solution)/shard_map/ppermute | solution.py:273
  4.4 2.2 %collective-permute-start.2 = (f32[16,2,16,128]{3,2,1,0:T(8,128)S(1)}, f32[16,2,16,128]{3,2,1,0:T(8,128)S(1)}, u32[]{:S(2)}, u32[]{:S(2)}) collective-permute-start(f32[16,2,16,128]{3,2,1,0:T(8,128)S(1)} %get-tuple-element.76), channel_id=1, source_target_pairs={{0,4},{1,5},{2,6},{3,7}} | collective-permute-start | bytes 786440 | tf_op jit(solution)/shard_map/ppermute | solution.py:273
  5.1 2.2 %collective-permute-start.3 = (f32[16,2,16,128]{3,2,1,0:T(8,128)S(1)}, f32[16,2,16,128]{3,2,1,0:T(8,128)S(1)}, u32[]{:S(2)}, u32[]{:S(2)}) collective-permute-start(f32[16,2,16,128]{3,2,1,0:T(8,128)S(1)} %get-tuple-element.78), channel_id=1, source_target_pairs={{0,4},{4,8},{1,5},{5,9},{2,6},{6,10},{3,7},{7,11}} | collective-permute-start | bytes 786440 | tf_op jit(solution)/shard_map/ppermute | solution.py:273
  5.9 2.2 %collective-permute-start.4 = (f32[16,2,16,128]{3,2,1,0:T(8,128)S(1)}, f32[16,2,16,128]{3,2,1,0:T(8,128)S(1)}, u32[]{:S(2)}, u32[]{:S(2)}) collective-permute-start(f32[16,2,16,128]{3,2,1,0:T(8,128)S(1)} %get-tuple-element.80), channel_id=1, source_target_pairs={{0,4},{4,8},{1,5},{5,9},{2,6},{6,10},{3,7},{7,11}} | collective-permute-start | bytes 786440 | tf_op jit(solution)/shard_map/ppermute | solution.py:273
  6.6 2.2 %collective-permute-start.5 = (f32[16,2,16,128]{3,2,1,0:T(8,128)S(1)}, f32[16,2,16,128]{3,2,1,0:T(8,128)S(1)}, u32[]{:S(2)}, u32[]{:S(2)}) collective-permute-start(f32[16,2,16,128]{3,2,1,0:T(8,128)S(1)} %get-tuple-element.82), channel_id=1, source_target_pairs={{0,4},{4,8},{1,5},{5,9},{2,6},{6,10},{3,7},{7,11}} | collective-permute-start | bytes 786440 | tf_op jit(solution)/shard_map/ppermute | solution.py:273
  7.4 2.2 %collective-permute-start.6 = (f32[16,2,16,128]{3,2,1,0:T(8,128)S(1)}, f32[16,2,16,128]{3,2,1,0:T(8,128)S(1)}, u32[]{:S(2)}, u32[]{:S(2)}) collective-permute-start(f32[16,2,16,128]{3,2,1,0:T(8,128)S(1)} %get-tuple-element.84), channel_id=1, source_target_pairs={{0,4},{4,8},{8,12},{1,5},{5,9},{9,13},{2,6},{6,10},{10,14},{3,7},{... | collective-permute-start | bytes 786440 | tf_op jit(solution)/shard_map/ppermute | solution.py:273
  8.1 2.1 %collective-permute-start.7 = (f32[16,2,16,128]{3,2,1,0:T(8,128)S(1)}, f32[16,2,16,128]{3,2,1,0:T(8,128)S(1)}, u32[]{:S(2)}, u32[]{:S(2)}) collective-permute-start(f32[16,2,16,128]{3,2,1,0:T(8,128)S(1)} %get-tuple-element.86), channel_id=1, source_target_pairs={{0,4},{4,8},{8,12},{1,5},{5,9},{9,13},{2,6},{6,10},{10,14},{3,7},{... | collective-permute-start | bytes 786440 | tf_op jit(solution)/shard_map/ppermute | solution.py:273
  8.9 2.1 %collective-permute-start.8 = (f32[16,2,16,128]{3,2,1,0:T(8,128)S(1)}, f32[16,2,16,128]{3,2,1,0:T(8,128)S(1)}, u32[]{:S(2)}, u32[]{:S(2)}) collective-permute-start(f32[16,2,16,128]{3,2,1,0:T(8,128)S(1)} %get-tuple-element.88), channel_id=1, source_target_pairs={{4,8},{8,12},{5,9},{9,13},{6,10},{10,14},{7,11},{11,15}} | collective-permute-start | bytes 786440 | tf_op jit(solution)/shard_map/ppermute | solution.py:273
  9.6 2.3 %collective-permute-start.9 = (f32[16,2,16,128]{3,2,1,0:T(8,128)S(1)}, f32[16,2,16,128]{3,2,1,0:T(8,128)S(1)}, u32[]{:S(2)}, u32[]{:S(2)}) collective-permute-start(f32[16,2,16,128]{3,2,1,0:T(8,128)S(1)} %get-tuple-element.90), channel_id=1, source_target_pairs={{4,8},{8,12},{12,16},{5,9},{9,13},{13,17},{6,10},{10,14},{14,18},{... | collective-permute-start | bytes 786440 | tf_op jit(solution)/shard_map/ppermute | solution.py:273
  10.3 2.3 %collective-permute-start.10 = (f32[16,2,16,128]{3,2,1,0:T(8,128)S(1)}, f32[16,2,16,128]{3,2,1,0:T(8,128)S(1)}, u32[]{:S(2)}, u32[]{:S(2)}) collective-permute-start(f32[16,2,16,128]{3,2,1,0:T(8,128)S(1)} %get-tuple-element.92), channel_id=1, source_target_pairs={{4,8},{8,12},{12,16},{5,9},{9,13},{13,17},{6,10},{10,14},{14,18},{... | collective-permute-start | bytes 786440 | tf_op jit(solution)/shard_map/ppermute | solution.py:273
  11.2 2.1 %collective-permute-start.11 = (f32[16,2,16,128]{3,2,1,0:T(8,128)S(1)}, f32[16,2,16,128]{3,2,1,0:T(8,128)S(1)}, u32[]{:S(2)}, u32[]{:S(2)}) collective-permute-start(f32[16,2,16,128]{3,2,1,0:T(8,128)S(1)} %get-tuple-element.94), channel_id=1, source_target_pairs={{8,12},{12,16},{9,13},{13,17},{10,14},{14,18},{11,15},{15,19}} | collective-permute-start | bytes 786440 | tf_op jit(solution)/shard_map/ppermute | solution.py:273
  11.9 2.1 %collective-permute-start.12 = (f32[16,2,16,128]{3,2,1,0:T(8,128)S(1)}, f32[16,2,16,128]{3,2,1,0:T(8,128)S(1)}, u32[]{:S(2)}, u32[]{:S(2)}) collective-permute-start(f32[16,2,16,128]{3,2,1,0:T(8,128)S(1)} %get-tuple-element.96), channel_id=1, source_target_pairs={{8,12},{12,16},{16,20},{9,13},{13,17},{17,21},{10,14},{14,18},{18,... | collective-permute-start | bytes 786440 | tf_op jit(solution)/shard_map/ppermute | solution.py:273
  12.7 2.1 %collective-permute-start.13 = (f32[16,2,16,128]{3,2,1,0:T(8,128)S(1)}, f32[16,2,16,128]{3,2,1,0:T(8,128)S(1)}, u32[]{:S(2)}, u32[]{:S(2)}) collective-permute-start(f32[16,2,16,128]{3,2,1,0:T(8,128)S(1)} %get-tuple-element.98), channel_id=1, source_target_pairs={{8,12},{12,16},{16,20},{9,13},{13,17},{17,21},{10,14},{14,18},{18,... | collective-permute-start | bytes 786440 | tf_op jit(solution)/shard_map/ppermute | solution.py:273
  13.4 2.1 %collective-permute-start.14 = (f32[16,2,16,128]{3,2,1,0:T(8,128)S(1)}, f32[16,2,16,128]{3,2,1,0:T(8,128)S(1)}, u32[]{:S(2)}, u32[]{:S(2)}) collective-permute-start(f32[16,2,16,128]{3,2,1,0:T(8,128)S(1)} %get-tuple-element.100), channel_id=1, source_target_pairs={{12,16},{16,20},{13,17},{17,21},{14,18},{18,22},{15,19},{19,23}} | collective-permute-start | bytes 786440 | tf_op jit(solution)/shard_map/ppermute | solution.py:273
  14.1 2.1 %collective-permute-start.15 = (f32[16,2,16,128]{3,2,1,0:T(8,128)S(1)}, f32[16,2,16,128]{3,2,1,0:T(8,128)S(1)}, u32[]{:S(2)}, u32[]{:S(2)}) collective-permute-start(f32[16,2,16,128]{3,2,1,0:T(8,128)S(1)} %get-tuple-element.102), channel_id=1, source_target_pairs={{12,16},{16,20},{20,24},{13,17},{17,21},{21,25},{14,18},{18,22},{2... | collective-permute-start | bytes 786440 | tf_op jit(solution)/shard_map/ppermute | solution.py:273
  14.9 2.8 %collective-permute-start.16 = (f32[16,2,16,128]{3,2,1,0:T(8,128)S(1)}, f32[16,2,16,128]{3,2,1,0:T(8,128)S(1)}, u32[]{:S(2)}, u32[]{:S(2)}) collective-permute-start(f32[16,2,16,128]{3,2,1,0:T(8,128)S(1)} %get-tuple-element.104), channel_id=1, source_target_pairs={{12,16},{16,20},{20,24},{13,17},{17,21},{21,25},{14,18},{18,22},{2... | collective-permute-start | bytes 786440 | tf_op jit(solution)/shard_map/ppermute | solution.py:273
  15.6 3.4 %collective-permute-start.17 = (f32[16,2,16,128]{3,2,1,0:T(8,128)S(1)}, f32[16,2,16,128]{3,2,1,0:T(8,128)S(1)}, u32[]{:S(2)}, u32[]{:S(2)}) collective-permute-start(f32[16,2,16,128]{3,2,1,0:T(8,128)S(1)} %get-tuple-element.106), channel_id=1, source_target_pairs={{16,20},{20,24},{17,21},{21,25},{18,22},{22,26},{19,23},{23,27}} | collective-permute-start | bytes 786440 | tf_op jit(solution)/shard_map/ppermute | solution.py:273
  16.3 27.7 %collective-permute-start.18 = (f32[16,2,16,128]{3,2,1,0:T(8,128)S(1)}, f32[16,2,16,128]{3,2,1,0:T(8,128)S(1)}, u32[]{:S(2)}, u32[]{:S(2)}) collective-permute-start(f32[16,2,16,128]{3,2,1,0:T(8,128)S(1)} %get-tuple-element.108), channel_id=1, source_target_pairs={{16,20},{20,24},{24,28},{17,21},{21,25},{25,29},{18,22},{22,26},{2... | collective-permute-start | bytes 786440 | tf_op jit(solution)/shard_map/ppermute | solution.py:273
  17.6 30.0 %collective-permute-start.19 = (f32[16,2,16,128]{3,2,1,0:T(8,128)S(1)}, f32[16,2,16,128]{3,2,1,0:T(8,128)S(1)}, u32[]{:S(2)}, u32[]{:S(2)}) collective-permute-start(f32[16,2,16,128]{3,2,1,0:T(8,128)S(1)} %get-tuple-element.110), channel_id=1, source_target_pairs={{16,20},{20,24},{24,28},{17,21},{21,25},{25,29},{18,22},{22,26},{2... | collective-permute-start | bytes 786440 | tf_op jit(solution)/shard_map/ppermute | solution.py:273
  19.0 32.4 %collective-permute-start.20 = (f32[16,2,16,128]{3,2,1,0:T(8,128)S(1)}, f32[16,2,16,128]{3,2,1,0:T(8,128)S(1)}, u32[]{:S(2)}, u32[]{:S(2)}) collective-permute-start(f32[16,2,16,128]{3,2,1,0:T(8,128)S(1)} %get-tuple-element.112), channel_id=1, source_target_pairs={{20,24},{24,28},{21,25},{25,29},{22,26},{26,30},{23,27},{27,31}} | collective-permute-start | bytes 786440 | tf_op jit(solution)/shard_map/ppermute | solution.py:273
  45.3 9.4 %collective-permute-start.21 = (f32[16,2,16,128]{3,2,1,0:T(8,128)S(1)}, f32[16,2,16,128]{3,2,1,0:T(8,128)S(1)}, u32[]{:S(2)}, u32[]{:S(2)}) collective-permute-start(f32[16,2,16,128]{3,2,1,0:T(8,128)S(1)} %get-tuple-element.114), channel_id=1, source_target_pairs={{20,24},{24,28},{21,25},{25,29},{22,26},{26,30},{23,27},{27,31}} | collective-permute-start | bytes 786440 | tf_op jit(solution)/shard_map/ppermute | solution.py:273
  48.9 9.4 %collective-permute-start.22 = (f32[16,2,16,128]{3,2,1,0:T(8,128)S(1)}, f32[16,2,16,128]{3,2,1,0:T(8,128)S(1)}, u32[]{:S(2)}, u32[]{:S(2)}) collective-permute-start(f32[16,2,16,128]{3,2,1,0:T(8,128)S(1)} %get-tuple-element.116), channel_id=1, source_target_pairs={{20,24},{24,28},{21,25},{25,29},{22,26},{26,30},{23,27},{27,31}} | collective-permute-start | bytes 786440 | tf_op jit(solution)/shard_map/ppermute | solution.py:273
  52.6 8.3 %collective-permute-start.23 = (f32[16,2,16,128]{3,2,1,0:T(8,128)S(1)}, f32[16,2,16,128]{3,2,1,0:T(8,128)S(1)}, u32[]{:S(2)}, u32[]{:S(2)}) collective-permute-start(f32[16,2,16,128]{3,2,1,0:T(8,128)S(1)} %get-tuple-element.118), channel_id=1, source_target_pairs={{24,28},{25,29},{26,30},{27,31}} | collective-permute-start | bytes 786440 | tf_op jit(solution)/shard_map/ppermute | solution.py:273
  56.2 7.5 %collective-permute-start.24 = (f32[16,2,16,128]{3,2,1,0:T(8,128)S(1)}, f32[16,2,16,128]{3,2,1,0:T(8,128)S(1)}, u32[]{:S(2)}, u32[]{:S(2)}) collective-permute-start(f32[16,2,16,128]{3,2,1,0:T(8,128)S(1)} %get-tuple-element.119), channel_id=1, source_target_pairs={{24,28},{25,29},{26,30},{27,31}} | collective-permute-start | bytes 786440 | tf_op jit(solution)/shard_map/ppermute | solution.py:273
  59.6 7.1 %collective-permute-start.25 = (f32[16,2,16,128]{3,2,1,0:T(8,128)S(1)}, f32[16,2,16,128]{3,2,1,0:T(8,128)S(1)}, u32[]{:S(2)}, u32[]{:S(2)}) collective-permute-start(f32[16,2,16,128]{3,2,1,0:T(8,128)S(1)} %get-tuple-element.122), channel_id=1, source_target_pairs={{24,28},{25,29},{26,30},{27,31}} | collective-permute-start | bytes 786440 | tf_op jit(solution)/shard_map/ppermute | solution.py:273
  68.2 10.1 %collective-permute-start.26 = (f32[2,128,128]{2,1,0:T(8,128)S(1)}, f32[2,128,128]{2,1,0:T(8,128)S(1)}, u32[]{:S(2)}, u32[]{:S(2)}) collective-permute-start(f32[2,128,128]{2,1,0:T(8,128)S(1)} %get-tuple-element.124), channel_id=1, source_target_pairs={{0,1},{1,2},{2,3},{3,0},{4,5},{5,6},{6,7},{7,4},{8,9},{9,10},{10,1... | collective-permute-start | bytes 393224 | tf_op jit(solution)/shard_map/ppermute | solution.py:299
  69.5 11.1 %collective-permute-start.27 = (f32[2,128,128]{2,1,0:T(8,128)S(1)}, f32[2,128,128]{2,1,0:T(8,128)S(1)}, u32[]{:S(2)}, u32[]{:S(2)}) collective-permute-start(f32[2,128,128]{2,1,0:T(8,128)S(1)} %get-tuple-element.125), channel_id=1, source_target_pairs={{0,2},{1,3},{2,0},{3,1},{4,6},{5,7},{6,4},{7,5},{8,10},{9,11},{10,... | collective-permute-start | bytes 393224 | tf_op jit(solution)/shard_map/ppermute | solution.py:299
  70.6 11.5 %collective-permute-start.28 = (f32[2,128,128]{2,1,0:T(8,128)S(1)}, f32[2,128,128]{2,1,0:T(8,128)S(1)}, u32[]{:S(2)}, u32[]{:S(2)}) collective-permute-start(f32[2,128,128]{2,1,0:T(8,128)S(1)} %get-tuple-element.126), channel_id=1, source_target_pairs={{0,3},{1,0},{2,1},{3,2},{4,7},{5,4},{6,5},{7,6},{8,11},{9,8},{10,9... | collective-permute-start | bytes 393224 | tf_op jit(solution)/shard_map/ppermute | solution.py:299

commit v3 on v2

--- a/solution.py
+++ b/solution.py
@@ -51,46 +51,62 @@
         columns, operator, kept_in = refs[:3]
         del refs[:3]
     arrived = {c: refs.pop(0) for c in arrived}
-    surface = [refs.pop(0), refs.pop(0)] if turn < len(sizes) else None
+    drawn = refs.pop(0) if 0 < turn < len(sizes) else None
+    surface = [refs.pop(0), refs.pop(0)] if turn + 1 < len(sizes) else None
     if first:
         columns, pairs, operator = refs[:3]
         del refs[:3]
     kept = refs.pop(0)
+    upcoming = refs.pop(0) if surface else None
     outs = {c: refs.pop(0) for c in send}
     splits = {c: refs.pop(0) for c in classes}
     if surface:
-        drawn, surface_sems = refs[:2]
-        del refs[:2]
+        surface_sems = refs.pop(0)
+    if first:
+        drawn = refs.pop(0)
     block_rows, nnz = operator.shape[:2]
-    width = operator.shape[-1]
+    width = operator.shape[-1] // 2
     depth = lax.axis_index("depth")
     group = turn - entry_turn(depth)
 
     def chunk(k):
         rows = pl.ds(k * (block_rows // CHUNKS), block_rows // CHUNKS)
-        return pltpu.make_async_copy(
-            propagator.at[0, 0, rows], operator.at[rows], refs[0].at[k])
-
-    if surface:
-        draws = [
+        return [
             pltpu.make_async_copy(
-                surface[k].at[0, :, pl.ds(offsets[turn], sizes[turn]), :],
-                drawn.at[k], surface_sems.at[k])
+                propagator.at[0, 0, rows, :, part],
+                operator.at[rows, :, :, pl.ds(part * width, width)], refs[0].at[k, part])
+            for part in range(2)
+        ]
+
+    def draw(g, target, slot):
+        return [
+            pltpu.make_async_copy(
+                surface[k].at[0, :, pl.ds(offsets[g], sizes[g]), :],
+                target.at[k], surface_sems.at[slot, k])
             for k in range(2)
         ]
 
-        @pl.when(depth == 0)
-        def _():
-            for copy in draws:
-                copy.start()
-
-    if first:
-        for k in range(CHUNKS):
-            chunk(k).start()
+    if first:
         tables = [pltpu.make_async_copy(columns_in, columns, refs[1].at[0]),
                   pltpu.make_async_copy(pairs_in, pairs, refs[1].at[1])]
         for copy in tables:
             copy.start()
+
+        @pl.when(depth == 0)
+        def _():
+            for copy in draw(0, drawn, 0):
+                copy.start()
+
+    if upcoming is not None:
+        @pl.when(depth == 0)
+        def _():
+            for copy in draw(turn + 1, upcoming, 1):
+                copy.start()
+
+    if first:
+        for k in range(CHUNKS):
+            for copy in chunk(k):
+                copy.start()
         for copy in tables:
             copy.wait()
 
@@ -104,11 +120,12 @@
             split[block, part * rows:(part + 1) * rows, :] = high
             split[block, (2 + part) * rows:(3 + part) * rows, :] = low
 
-        if surface and sizes[turn] == shots:
+        if turn < len(sizes) and sizes[turn] == shots:
             @pl.when(depth == 0)
             def _():
-                for copy in draws:
-                    copy.wait()
+                if first:
+                    for copy in draw(0, drawn, 0):
+                        copy.wait()
                 for block in range(block_rows):
                     lanes = slice(block * width, (block + 1) * width)
                     for part in range(2):
@@ -133,13 +150,12 @@
 
         for r in range(block_rows):
             if first and r % (block_rows // CHUNKS) == 0:
-                chunk(r // (block_rows // CHUNKS)).wait()
+                for copy in chunk(r // (block_rows // CHUNKS)):
+                    copy.wait()
             picked = jnp.concatenate(
                 [split[columns[j, 0, r]] for j in range(nnz)], axis=1
             )
-            real = operator[r, :, 0].reshape(nnz * width, width)
-            imag = operator[r, :, 1].reshape(nnz * width, width)
-            weights = jnp.concatenate([real, imag], axis=1)
+            weights = operator[r].reshape(nnz * width, 2 * width)
             product = jnp.dot(picked, weights, preferred_element_type=jnp.float32)
             product = product[: 2 * rows] + product[2 * rows:]
             scale = taper_row(r, block_rows, width)
@@ -159,7 +175,14 @@
         @pl.when(depth > 0)
         def _():
             for k in range(CHUNKS):
-                chunk(k).wait()
+                for copy in chunk(k):
+                    copy.wait()
+
+    if upcoming is not None:
+        @pl.when(depth == 0)
+        def _():
+            for copy in draw(turn + 1, upcoming, 1):
+                copy.wait()
 
 
 def image_block(pairs, index, kept, shots, scale):
@@ -176,20 +199,25 @@
     )
 
 
-def early_kernel(pairs, kept_in, kept, out, *, shots, scale):
-    for index in range(out.shape[0]):
-        out[index] = image_block(pairs, index, kept_in, shots, scale)
-
-
-def last_kernel(pairs, early, kept, *outs, shots, scale):
+def owned(outs):
     share = outs[0].shape[0]
     parts = len(outs)
     own = lax.axis_index("freq")
     for step in range(parts):
         owner = lax.rem(own + step, parts)
         for index in range(share):
-            pair = owner * share + index
-            outs[step][index] = early[pair] + image_block(pairs, pair, kept, shots, scale)
+            yield step, index, owner * share + index
+
+
+def share_kernel(pairs, kept_in, kept, *outs, shots, scale):
+    for step, index, pair in owned(outs):
+        outs[step][index] = image_block(pairs, pair, kept_in, shots, scale)
+
+
+def last_kernel(pairs, kept, *refs, shots, scale):
+    early, outs = refs[:len(refs) // 2], refs[len(refs) // 2:]
+    for step, index, pair in owned(outs):
+        outs[step][index] = early[step][index] + image_block(pairs, pair, kept, shots, scale)
 
 
 def shards(source_field, receiver_data, propagator, block_columns, image_pairs):
@@ -217,6 +245,18 @@
         group = turn - entry_turn(d)
         return sizes[group] if 0 <= group < groups else None
 
+    share_type = pltpu.VMEM((pair_count // freq_count, width, width), jnp.float32)
+
+    def shares(kept, shots):
+        return pl.pallas_call(
+            functools.partial(share_kernel, shots=shots, scale=scale),
+            out_shape=(kept_type,) + (share_type,) * freq_count,
+            in_specs=[SMEM, VMEM],
+            out_specs=(VMEM,) * (1 + freq_count),
+            input_output_aliases={1: 0},
+            compiler_params=params,
+        )(pairs, kept)
+
     sent = {}
     for turn in range(turns):
         arrived = sent.pop(turn - DELAY, {})
@@ -230,7 +270,7 @@
             specs = [HBM, HBM, HBM]
             out_shape = [pltpu.SMEM(columns_in.shape, jnp.int32),
                          pltpu.SMEM(pairs_in.shape, jnp.int32),
-                         pltpu.VMEM(propagator.shape[2:], propagator.dtype),
+                         pltpu.VMEM((block_rows, nnz, width, 2 * width), propagator.dtype),
                          kept_type]
             out_specs = [SMEM, SMEM, VMEM, VMEM]
             aliases = {}
@@ -242,16 +282,22 @@
             aliases = {2: 0}
         operands += list(arrived.values())
         specs += [VMEM] * len(arrived)
+        if 0 < turn < groups:
+            operands.append(drawn)
+            specs.append(VMEM)
+        if turn + 1 < groups:
+            operands += [source_field, receiver_data]
+            specs += [HBM, HBM]
+            out_shape.append(pltpu.VMEM((2, 2, sizes[turn + 1], lateral), jnp.float32))
+            out_specs.append(VMEM)
         out_shape += [pltpu.VMEM((block_rows, 2, 2 * c, width), jnp.float32) for c in send]
         out_specs += [VMEM] * len(send)
         scratch = [pltpu.VMEM((block_rows, 8 * c, width), jnp.bfloat16) for c in classes]
-        if turn < groups:
-            operands += [source_field, receiver_data]
-            specs += [HBM, HBM]
-            scratch += [pltpu.VMEM((2, 2, sizes[turn], lateral), jnp.float32),
-                        pltpu.SemaphoreType.DMA((2,))]
+        if turn + 1 < groups:
+            scratch += [pltpu.SemaphoreType.DMA((2, 2))]
         if turn == 0:
-            scratch += [pltpu.SemaphoreType.DMA((CHUNKS,)), pltpu.SemaphoreType.DMA((2,))]
+            scratch += [pltpu.VMEM((2, 2, sizes[0], lateral), jnp.float32),
+                        pltpu.SemaphoreType.DMA((CHUNKS, 2)), pltpu.SemaphoreType.DMA((2,))]
         results = pl.pallas_call(
             functools.partial(
                 propagate_kernel, turn=turn, sizes=sizes, offsets=offsets, classes=classes,
@@ -268,36 +314,30 @@
             columns, pairs, operator = results[:3]
             results = results[3:]
         kept = results[0]
-        fields = dict(zip(send, results[1:]))
+        results = results[1:]
+        if turn + 1 < groups:
+            drawn = results[0]
+            results = results[1:]
+        fields = dict(zip(send, results))
         sent[turn] = {
             c: lax.ppermute(fields[c], "depth", [
                 (d, d + 1) for d in range(depth_count - 1) if size_of(d, turn) == c])
             for c in send
         }
         if turn == turns - 2:
-            image_type = pltpu.VMEM((pair_count, width, width), jnp.float32)
-            kept, early = pl.pallas_call(
-                functools.partial(early_kernel, shots=slice(0, offsets[-1]), scale=scale),
-                out_shape=(kept_type, image_type),
-                in_specs=[SMEM, VMEM],
-                out_specs=(VMEM, VMEM),
-                input_output_aliases={1: 0},
-                compiler_params=params,
-            )(pairs, kept)
-
-    share = pair_count // freq_count
-    share_type = pltpu.VMEM((share, width, width), jnp.float32)
-    shares = pl.pallas_call(
+            kept, *early = shares(kept, slice(0, offsets[-1]))
+
+    lasts = pl.pallas_call(
         functools.partial(last_kernel, shots=slice(offsets[-1], shots_all), scale=scale),
         out_shape=(share_type,) * freq_count,
-        in_specs=[SMEM, VMEM, VMEM],
+        in_specs=[SMEM] + [VMEM] * (1 + freq_count),
         out_specs=(VMEM,) * freq_count,
         compiler_params=params,
-    )(pairs, early, kept)
-    total = shares[0]
-    for step in range(1, freq_count):
+    )(pairs, kept, *early)
+    total = lasts[0]
+    for step in sorted(range(1, freq_count), key=lambda step: step % 2):
         total += lax.ppermute(
-            shares[step], "freq", [(f, (f + step) % freq_count) for f in range(freq_count)])
+            lasts[step], "freq", [(f, (f + step) % freq_count) for f in range(freq_count)])
     return total[None]
 
 

time: 83.3 us -> 82.2 us (0.987)
  waiting for transfers between devices: 40.6 us -> 38.8 us
    ppermute x26, waiting for transfers between devices: 30.6 us -> 29.3 us  [shards(): lax.ppermute(fields[c], 'depth', [(d, d + 1) for d in range(depth_count -...]
  transfers between devices with their start and end apart: 29 -> 29, of which waited for: 10 -> 9; matrix products, arithmetic and copies ran while one was open for 0% -> 0% of each run, Pallas kernels for 12% -> 12%
where the time goes in v3:
time: 82.2 us; the launch traced here: 81 us
  waiting for transfers between devices  38.8 us (47%)
  starting transfers between devices  26.4 us (32%)
  Pallas kernels  14.4 us (18%)
    ppermute x26, waiting for transfers between devices, shards(): lax.ppermute(fields[c], 'depth', [(d, d + 1) for d in range(depth_count -...  29.3 us
    ppermute x26, starting transfers between devices, shards(): lax.ppermute(fields[c], 'depth', [(d, d + 1) for d in range(depth_count -...  22.5 us
    pallas_call x29, Pallas kernels, shards(): pl.pallas_call(functools.partial(propagate_kernel, turn=turn, sizes=sizes...  13.7 us
    ppermute x3, waiting for transfers between devices, shards(): lax.ppermute(lasts[step], 'freq', [(f, (f + step) % freq_count) for f in...  9.57 us
    ppermute x3, starting transfers between devices, shards(): lax.ppermute(lasts[step], 'freq', [(f, (f + step) % freq_count) for f in...  3.84 us
  transfers between devices with their start and end apart: 29, of which 9 were waited for; matrix products, arithmetic and copies ran while one was open for 0% of the time, Pallas kernels for 12%

profile of v3, /device:TPU:15, one launch (start us, length us, event | category | flops | bytes accessed | tf_op | source)
XLA Modules:
  0.0 81.0 jit_solution(4129897728103927643)
XLA Ops:
  0.0 2.9 %shard_map.55 = (s32[6,1,16]{2,1,0:T(1,128)S(4)}, s32[1,2,8]{2,1,0:T(2,128)S(4)}, bf16[16,6,128,256]{3,2,1,0:T(8,128)(2,1)S(1)}, f32[16,2,2,64,128]{4,3,2,1,0:T(...) custom-call(s32[6,1,16]{2,1,0:T(1,128)} %bitcast.4, s32[1,2,8]{2,1,0:T(2,128)} %bitcast.5, ...), custom_call_target="tpu_custom_call" | custom-call | tf_op jit(solution)/shard_map/pallas_call | solution.py:301
  2.9 0.7 collective-permute-start
  3.6 0.1 shard_map.56
  3.7 0.7 collective-permute-start.1
  4.4 0.1 shard_map.57
  4.4 0.7 collective-permute-start.2
  5.1 0.0 collective-permute-done.refs_3_
  5.1 0.1 shard_map.58
  5.2 0.7 collective-permute-start.3
  5.9 0.0 collective-permute-done.1.refs_3_
  5.9 0.1 shard_map.59
  6.0 0.7 collective-permute-start.4
  6.7 0.0 collective-permute-done.2.refs_3_
  6.7 0.1 shard_map.60
  6.8 0.7 collective-permute-start.5
  7.4 0.1 shard_map.61
  7.5 0.7 collective-permute-start.6
  8.2 0.0 collective-permute-done.4.refs_3_
  8.2 0.7 collective-permute-start.7
  8.9 0.0 collective-permute-done.5.refs_3_
  9.0 0.7 collective-permute-start.8
  9.7 0.7 collective-permute-start.9
  10.4 0.0 collective-permute-done.7.refs_3_
  10.4 0.7 collective-permute-start.10
  11.1 0.0 collective-permute-done.8.refs_3_
  11.1 0.2 shard_map.66
  11.3 0.7 collective-permute-start.11
  12.1 0.7 collective-permute-start.12
  12.8 0.7 collective-permute-start.13
  13.5 0.7 collective-permute-start.14
  14.2 0.7 collective-permute-start.15
  15.0 0.7 collective-permute-start.16
  15.7 0.7 collective-permute-start.17
  16.4 1.3 %collective-permute-start.18 = (f32[16,2,16,128]{3,2,1,0:T(8,128)S(1)}, f32[16,2,16,128]{3,2,1,0:T(8,128)S(1)}, u32[]{:S(2)}, u32[]{:S(2)}) collective-permute-start(f32[16,2,16,128]{3,2,1,0:T(8,128)S(1)} %get-tuple-element.125), channel_id=1, source_target_pairs={{16,20},{20,24},{24,28},{17,21},{21,25},{25,29},{18,22},{22,26},{2... | collective-permute-start | bytes 786440 | tf_op jit(solution)/shard_map/ppermute | solution.py:323
  17.8 1.3 %collective-permute-start.19 = (f32[16,2,16,128]{3,2,1,0:T(8,128)S(1)}, f32[16,2,16,128]{3,2,1,0:T(8,128)S(1)}, u32[]{:S(2)}, u32[]{:S(2)}) collective-permute-start(f32[16,2,16,128]{3,2,1,0:T(8,128)S(1)} %get-tuple-element.127), channel_id=1, source_target_pairs={{16,20},{20,24},{24,28},{17,21},{21,25},{25,29},{18,22},{22,26},{2... | collective-permute-start | bytes 786440 | tf_op jit(solution)/shard_map/ppermute | solution.py:323
  19.1 1.3 %collective-permute-start.20 = (f32[16,2,16,128]{3,2,1,0:T(8,128)S(1)}, f32[16,2,16,128]{3,2,1,0:T(8,128)S(1)}, u32[]{:S(2)}, u32[]{:S(2)}) collective-permute-start(f32[16,2,16,128]{3,2,1,0:T(8,128)S(1)} %get-tuple-element.129), channel_id=1, source_target_pairs={{20,24},{24,28},{21,25},{25,29},{22,26},{26,30},{23,27},{27,31}} | collective-permute-start | bytes 786440 | tf_op jit(solution)/shard_map/ppermute | solution.py:323
  20.4 23.6 %collective-permute-done.18.refs_3_ = f32[16,2,16,128]{3,2,1,0:T(8,128)S(1)} collective-permute-done((f32[16,2,16,128]{3,2,1,0:T(8,128)S(1)}, f32[16,2,16,128]{3,2,1,0:T(8,128)S(1)}, u32[]{:S(2)}, u32[]{:S(2)}) %collective-permute-start.18) | collective-permute-done | bytes 262176 | tf_op jit(solution)/shard_map/ppermute | solution.py:323
  44.0 1.2 %shard_map.76 = (f32[16,2,2,64,128]{4,3,2,1,0:T(8,128)S(1)}, f32[16,2,16,128]{3,2,1,0:T(8,128)S(1)}) custom-call(s32[6,1,16]{2,1,0:T(1,128)S(4)} %get-tuple-element.77.refs_0_, bf16[16,6,128,256]{3,2,1,0:T(8,128)(2,1)S(1)} %get-tuple-element.78.refs_1_, f32[16,2,2,64,128]{4,3,2,1,0:T(8,128)S(1)} %get-tuple-element.124.refs_2_, ...), custom_call_target="tpu_custom_call", output_to_operand_aliasing={{0}: (2, {})} | custom-call | tf_op jit(solution)/shard_map/pallas_call | solution.py:301
  45.2 1.3 %collective-permute-start.21 = (f32[16,2,16,128]{3,2,1,0:T(8,128)S(1)}, f32[16,2,16,128]{3,2,1,0:T(8,128)S(1)}, u32[]{:S(2)}, u32[]{:S(2)}) collective-permute-start(f32[16,2,16,128]{3,2,1,0:T(8,128)S(1)} %get-tuple-element.131), channel_id=1, source_target_pairs={{20,24},{24,28},{21,25},{25,29},{22,26},{26,30},{23,27},{27,31}} | collective-permute-start | bytes 786440 | tf_op jit(solution)/shard_map/ppermute | solution.py:323
  46.5 0.7 collective-permute-done.19.refs_3_
  47.2 1.2 %shard_map.77 = (f32[16,2,2,64,128]{4,3,2,1,0:T(8,128)S(1)}, f32[16,2,16,128]{3,2,1,0:T(8,128)S(1)}) custom-call(s32[6,1,16]{2,1,0:T(1,128)S(4)} %get-tuple-element.77.refs_0_, bf16[16,6,128,256]{3,2,1,0:T(8,128)(2,1)S(1)} %get-tuple-element.78.refs_1_, f32[16,2,2,64,128]{4,3,2,1,0:T(8,128)S(1)} %get-tuple-element.126.refs_2_, ...), custom_call_target="tpu_custom_call", output_to_operand_aliasing={{0}: (2, {})} | custom-call | tf_op jit(solution)/shard_map/pallas_call | solution.py:301
  48.4 1.3 %collective-permute-start.22 = (f32[16,2,16,128]{3,2,1,0:T(8,128)S(1)}, f32[16,2,16,128]{3,2,1,0:T(8,128)S(1)}, u32[]{:S(2)}, u32[]{:S(2)}) collective-permute-start(f32[16,2,16,128]{3,2,1,0:T(8,128)S(1)} %get-tuple-element.133), channel_id=1, source_target_pairs={{20,24},{24,28},{21,25},{25,29},{22,26},{26,30},{23,27},{27,31}} | collective-permute-start | bytes 786440 | tf_op jit(solution)/shard_map/ppermute | solution.py:323
  49.7 0.8 %collective-permute-done.20.refs_3_ = f32[16,2,16,128]{3,2,1,0:T(8,128)S(1)} collective-permute-done((f32[16,2,16,128]{3,2,1,0:T(8,128)S(1)}, f32[16,2,16,128]{3,2,1,0:T(8,128)S(1)}, u32[]{:S(2)}, u32[]{:S(2)}) %collective-permute-start.20) | collective-permute-done | bytes 262176 | tf_op jit(solution)/shard_map/ppermute | solution.py:323
  50.6 1.2 %shard_map.78 = (f32[16,2,2,64,128]{4,3,2,1,0:T(8,128)S(1)}, f32[16,2,16,128]{3,2,1,0:T(8,128)S(1)}) custom-call(s32[6,1,16]{2,1,0:T(1,128)S(4)} %get-tuple-element.77.refs_0_, bf16[16,6,128,256]{3,2,1,0:T(8,128)(2,1)S(1)} %get-tuple-element.78.refs_1_, f32[16,2,2,64,128]{4,3,2,1,0:T(8,128)S(1)} %get-tuple-element.128.refs_2_, ...), custom_call_target="tpu_custom_call", output_to_operand_aliasing={{0}: (2, {})} | custom-call | tf_op jit(solution)/shard_map/pallas_call | solution.py:301
  51.8 1.3 %collective-permute-start.23 = (f32[16,2,16,128]{3,2,1,0:T(8,128)S(1)}, f32[16,2,16,128]{3,2,1,0:T(8,128)S(1)}, u32[]{:S(2)}, u32[]{:S(2)}) collective-permute-start(f32[16,2,16,128]{3,2,1,0:T(8,128)S(1)} %get-tuple-element.135), channel_id=1, source_target_pairs={{24,28},{25,29},{26,30},{27,31}} | collective-permute-start | bytes 786440 | tf_op jit(solution)/shard_map/ppermute | solution.py:323
  53.1 0.7 collective-permute-done.21.refs_3_
  53.8 1.4 %shard_map.79 = (f32[16,2,2,64,128]{4,3,2,1,0:T(8,128)S(1)}, f32[16,2,16,128]{3,2,1,0:T(8,128)S(1)}) custom-call(s32[6,1,16]{2,1,0:T(1,128)S(4)} %get-tuple-element.77.refs_0_, bf16[16,6,128,256]{3,2,1,0:T(8,128)(2,1)S(1)} %get-tuple-element.78.refs_1_, f32[16,2,2,64,128]{4,3,2,1,0:T(8,128)S(1)} %get-tuple-element.130.refs_2_, ...), custom_call_target="tpu_custom_call", output_to_operand_aliasing={{0}: (2, {})} | custom-call | tf_op jit(solution)/shard_map/pallas_call | solution.py:301
  55.2 1.3 %collective-permute-start.24 = (f32[16,2,16,128]{3,2,1,0:T(8,128)S(1)}, f32[16,2,16,128]{3,2,1,0:T(8,128)S(1)}, u32[]{:S(2)}, u32[]{:S(2)}) collective-permute-start(f32[16,2,16,128]{3,2,1,0:T(8,128)S(1)} %get-tuple-element.136), channel_id=1, source_target_pairs={{24,28},{25,29},{26,30},{27,31}} | collective-permute-start | bytes 786440 | tf_op jit(solution)/shard_map/ppermute | solution.py:323
  56.5 0.5 collective-permute-done.22.refs_3_
  57.0 1.2 %shard_map.80 = (f32[16,2,2,64,128]{4,3,2,1,0:T(8,128)S(1)}, f32[16,2,16,128]{3,2,1,0:T(8,128)S(1)}) custom-call(s32[6,1,16]{2,1,0:T(1,128)S(4)} %get-tuple-element.77.refs_0_, bf16[16,6,128,256]{3,2,1,0:T(8,128)(2,1)S(1)} %get-tuple-element.78.refs_1_, f32[16,2,2,64,128]{4,3,2,1,0:T(8,128)S(1)} %get-tuple-element.132.refs_2_, ...), custom_call_target="tpu_custom_call", output_to_operand_aliasing={{0}: (2, {})} | custom-call | tf_op jit(solution)/shard_map/pallas_call | solution.py:301
  58.3 1.3 %collective-permute-start.25 = (f32[16,2,16,128]{3,2,1,0:T(8,128)S(1)}, f32[16,2,16,128]{3,2,1,0:T(8,128)S(1)}, u32[]{:S(2)}, u32[]{:S(2)}) collective-permute-start(f32[16,2,16,128]{3,2,1,0:T(8,128)S(1)} %get-tuple-element.138), channel_id=1, source_target_pairs={{24,28},{25,29},{26,30},{27,31}} | collective-permute-start | bytes 786440 | tf_op jit(solution)/shard_map/ppermute | solution.py:323
  59.6 0.0 collective-permute-done.23.refs_3_
  59.6 1.2 %shard_map.81.refs_2_ = f32[16,2,2,64,128]{4,3,2,1,0:T(8,128)S(1)} custom-call(s32[6,1,16]{2,1,0:T(1,128)S(4)} %get-tuple-element.77.refs_0_, bf16[16,6,128,256]{3,2,1,0:T(8,128)(2,1)S(1)} %get-tuple-element.78.refs_1_, f32[16,2,2,64,128]{4,3,2,1,0:T(8,128)S(1)} %get-tuple-element.134.refs_2_, ...), custom_call_target="tpu_custom_call", output_to_operand_aliasing={{}: (2, {})} | custom-call | tf_op jit(solution)/shard_map/pallas_call | solution.py:301
  60.8 1.5 %collective-permute-done.24.refs_3_ = f32[16,2,16,128]{3,2,1,0:T(8,128)S(1)} collective-permute-done((f32[16,2,16,128]{3,2,1,0:T(8,128)S(1)}, f32[16,2,16,128]{3,2,1,0:T(8,128)S(1)}, u32[]{:S(2)}, u32[]{:S(2)}) %collective-permute-start.24) | collective-permute-done | bytes 262176 | tf_op jit(solution)/shard_map/ppermute | solution.py:323
  62.3 1.2 %shard_map.82.kept_in = f32[16,2,2,64,128]{4,3,2,1,0:T(8,128)S(1)} custom-call(s32[6,1,16]{2,1,0:T(1,128)S(4)} %get-tuple-element.77.refs_0_, bf16[16,6,128,256]{3,2,1,0:T(8,128)(2,1)S(1)} %get-tuple-element.78.refs_1_, f32[16,2,2,64,128]{4,3,2,1,0:T(8,128)S(1)} %shard_map.81.refs_2_, ...), custom_call_target="tpu_custom_call", output_to_operand_aliasing={{}: (2, {})} | custom-call | tf_op jit(solution)/shard_map/pallas_call | solution.py:301
  63.6 0.4 shard_map.83
  64.0 1.3 %collective-permute-done.25.refs_3_ = f32[16,2,16,128]{3,2,1,0:T(8,128)S(1)} collective-permute-done((f32[16,2,16,128]{3,2,1,0:T(8,128)S(1)}, f32[16,2,16,128]{3,2,1,0:T(8,128)S(1)}, u32[]{:S(2)}, u32[]{:S(2)}) %collective-permute-start.25) | collective-permute-done | bytes 262176 | tf_op jit(solution)/shard_map/ppermute | solution.py:323
  65.3 1.2 %shard_map.84.kept = f32[16,2,2,64,128]{4,3,2,1,0:T(8,128)S(1)} custom-call(s32[6,1,16]{2,1,0:T(1,128)S(4)} %get-tuple-element.77.refs_0_, bf16[16,6,128,256]{3,2,1,0:T(8,128)(2,1)S(1)} %get-tuple-element.78.refs_1_, f32[16,2,2,64,128]{4,3,2,1,0:T(8,128)S(1)} %get-tuple-element.137.refs_2_, ...), custom_call_target="tpu_custom_call", output_to_operand_aliasing={{}: (2, {})} | custom-call | tf_op jit(solution)/shard_map/pallas_call | solution.py:301
  66.5 0.3 shard_map.85
  66.8 2.4 %collective-permute-start.26 = (f32[2,128,128]{2,1,0:T(8,128)S(1)}, f32[2,128,128]{2,1,0:T(8,128)S(1)}, u32[]{:S(2)}, u32[]{:S(2)}) collective-permute-start(f32[2,128,128]{2,1,0:T(8,128)S(1)} %get-tuple-element.144), channel_id=1, source_target_pairs={{0,2},{1,3},{2,0},{3,1},{4,6},{5,7},{6,4},{7,5},{8,10},{9,11},{10,... | collective-permute-start | bytes 393224 | tf_op jit(solution)/shard_map/ppermute | solution.py:339
  69.2 1.5 %collective-permute-start.28 = (f32[2,128,128]{2,1,0:T(8,128)S(1)}, f32[2,128,128]{2,1,0:T(8,128)S(1)}, u32[]{:S(2)}, u32[]{:S(2)}) collective-permute-start(f32[2,128,128]{2,1,0:T(8,128)S(1)} %get-tuple-element.146), channel_id=1, source_target_pairs={{0,3},{1,0},{2,1},{3,2},{4,7},{5,4},{6,5},{7,6},{8,11},{9,8},{10,9... | collective-permute-start | bytes 393224 | tf_op jit(solution)/shard_map/ppermute | solution.py:339
  70.7 4.3 %collective-permute-done.26 = f32[2,128,128]{2,1,0:T(8,128)S(1)} collective-permute-done((f32[2,128,128]{2,1,0:T(8,128)S(1)}, f32[2,128,128]{2,1,0:T(8,128)S(1)}, u32[]{:S(2)}, u32[]{:S(2)}) %collective-permute-start.26) | collective-permute-done | bytes 131104 | tf_op jit(solution)/shard_map/ppermute | solution.py:339
  75.0 5.3 %collective-permute-done.27 = f32[2,128,128]{2,1,0:T(8,128)S(1)} collective-permute-done((f32[2,128,128]{2,1,0:T(8,128)S(1)}, f32[2,128,128]{2,1,0:T(8,128)S(1)}, u32[]{:S(2)}, u32[]{:S(2)}) %collective-permute-start.27) | collective-permute-done | bytes 131104 | tf_op jit(solution)/shard_map/ppermute | solution.py:339
  80.3 0.7 add_bitcast_fusion
  (26 shorter events, 0.3 us)
Async XLA Ops:
  2.9 2.2 %collective-permute-start = (f32[16,2,16,128]{3,2,1,0:T(8,128)S(1)}, f32[16,2,16,128]{3,2,1,0:T(8,128)S(1)}, u32[]{:S(2)}, u32[]{:S(2)}) collective-permute-start(f32[16,2,16,128]{3,2,1,0:T(8,128)S(1)} %get-tuple-element.84), channel_id=1, source_target_pairs={{0,4},{1,5},{2,6},{3,7}} | collective-permute-start | bytes 786440 | tf_op jit(solution)/shard_map/ppermute | solution.py:323
  3.7 2.2 %collective-permute-start.1 = (f32[16,2,16,128]{3,2,1,0:T(8,128)S(1)}, f32[16,2,16,128]{3,2,1,0:T(8,128)S(1)}, u32[]{:S(2)}, u32[]{:S(2)}) collective-permute-start(f32[16,2,16,128]{3,2,1,0:T(8,128)S(1)} %get-tuple-element.87), channel_id=1, source_target_pairs={{0,4},{1,5},{2,6},{3,7}} | collective-permute-start | bytes 786440 | tf_op jit(solution)/shard_map/ppermute | solution.py:323
  4.4 2.2 %collective-permute-start.2 = (f32[16,2,16,128]{3,2,1,0:T(8,128)S(1)}, f32[16,2,16,128]{3,2,1,0:T(8,128)S(1)}, u32[]{:S(2)}, u32[]{:S(2)}) collective-permute-start(f32[16,2,16,128]{3,2,1,0:T(8,128)S(1)} %get-tuple-element.90), channel_id=1, source_target_pairs={{0,4},{1,5},{2,6},{3,7}} | collective-permute-start | bytes 786440 | tf_op jit(solution)/shard_map/ppermute | solution.py:323
  5.2 2.2 %collective-permute-start.3 = (f32[16,2,16,128]{3,2,1,0:T(8,128)S(1)}, f32[16,2,16,128]{3,2,1,0:T(8,128)S(1)}, u32[]{:S(2)}, u32[]{:S(2)}) collective-permute-start(f32[16,2,16,128]{3,2,1,0:T(8,128)S(1)} %get-tuple-element.93), channel_id=1, source_target_pairs={{0,4},{4,8},{1,5},{5,9},{2,6},{6,10},{3,7},{7,11}} | collective-permute-start | bytes 786440 | tf_op jit(solution)/shard_map/ppermute | solution.py:323
  6.0 2.2 %collective-permute-start.4 = (f32[16,2,16,128]{3,2,1,0:T(8,128)S(1)}, f32[16,2,16,128]{3,2,1,0:T(8,128)S(1)}, u32[]{:S(2)}, u32[]{:S(2)}) collective-permute-start(f32[16,2,16,128]{3,2,1,0:T(8,128)S(1)} %get-tuple-element.96), channel_id=1, source_target_pairs={{0,4},{4,8},{1,5},{5,9},{2,6},{6,10},{3,7},{7,11}} | collective-permute-start | bytes 786440 | tf_op jit(solution)/shard_map/ppermute | solution.py:323
  6.8 2.2 %collective-permute-start.5 = (f32[16,2,16,128]{3,2,1,0:T(8,128)S(1)}, f32[16,2,16,128]{3,2,1,0:T(8,128)S(1)}, u32[]{:S(2)}, u32[]{:S(2)}) collective-permute-start(f32[16,2,16,128]{3,2,1,0:T(8,128)S(1)} %get-tuple-element.99), channel_id=1, source_target_pairs={{0,4},{4,8},{1,5},{5,9},{2,6},{6,10},{3,7},{7,11}} | collective-permute-start | bytes 786440 | tf_op jit(solution)/shard_map/ppermute | solution.py:323
  7.5 2.1 %collective-permute-start.6 = (f32[16,2,16,128]{3,2,1,0:T(8,128)S(1)}, f32[16,2,16,128]{3,2,1,0:T(8,128)S(1)}, u32[]{:S(2)}, u32[]{:S(2)}) collective-permute-start(f32[16,2,16,128]{3,2,1,0:T(8,128)S(1)} %get-tuple-element.101), channel_id=1, source_target_pairs={{0,4},{4,8},{8,12},{1,5},{5,9},{9,13},{2,6},{6,10},{10,14},{3,7},{... | collective-permute-start | bytes 786440 | tf_op jit(solution)/shard_map/ppermute | solution.py:323
  8.2 2.1 %collective-permute-start.7 = (f32[16,2,16,128]{3,2,1,0:T(8,128)S(1)}, f32[16,2,16,128]{3,2,1,0:T(8,128)S(1)}, u32[]{:S(2)}, u32[]{:S(2)}) collective-permute-start(f32[16,2,16,128]{3,2,1,0:T(8,128)S(1)} %get-tuple-element.103), channel_id=1, source_target_pairs={{0,4},{4,8},{8,12},{1,5},{5,9},{9,13},{2,6},{6,10},{10,14},{3,7},{... | collective-permute-start | bytes 786440 | tf_op jit(solution)/shard_map/ppermute | solution.py:323
  9.0 2.1 %collective-permute-start.8 = (f32[16,2,16,128]{3,2,1,0:T(8,128)S(1)}, f32[16,2,16,128]{3,2,1,0:T(8,128)S(1)}, u32[]{:S(2)}, u32[]{:S(2)}) collective-permute-start(f32[16,2,16,128]{3,2,1,0:T(8,128)S(1)} %get-tuple-element.105), channel_id=1, source_target_pairs={{4,8},{8,12},{5,9},{9,13},{6,10},{10,14},{7,11},{11,15}} | collective-permute-start | bytes 786440 | tf_op jit(solution)/shard_map/ppermute | solution.py:323
  9.7 2.3 %collective-permute-start.9 = (f32[16,2,16,128]{3,2,1,0:T(8,128)S(1)}, f32[16,2,16,128]{3,2,1,0:T(8,128)S(1)}, u32[]{:S(2)}, u32[]{:S(2)}) collective-permute-start(f32[16,2,16,128]{3,2,1,0:T(8,128)S(1)} %get-tuple-element.107), channel_id=1, source_target_pairs={{4,8},{8,12},{12,16},{5,9},{9,13},{13,17},{6,10},{10,14},{14,18},{... | collective-permute-start | bytes 786440 | tf_op jit(solution)/shard_map/ppermute | solution.py:323
  10.4 2.3 %collective-permute-start.10 = (f32[16,2,16,128]{3,2,1,0:T(8,128)S(1)}, f32[16,2,16,128]{3,2,1,0:T(8,128)S(1)}, u32[]{:S(2)}, u32[]{:S(2)}) collective-permute-start(f32[16,2,16,128]{3,2,1,0:T(8,128)S(1)} %get-tuple-element.109), channel_id=1, source_target_pairs={{4,8},{8,12},{12,16},{5,9},{9,13},{13,17},{6,10},{10,14},{14,18},{... | collective-permute-start | bytes 786440 | tf_op jit(solution)/shard_map/ppermute | solution.py:323
  11.3 2.1 %collective-permute-start.11 = (f32[16,2,16,128]{3,2,1,0:T(8,128)S(1)}, f32[16,2,16,128]{3,2,1,0:T(8,128)S(1)}, u32[]{:S(2)}, u32[]{:S(2)}) collective-permute-start(f32[16,2,16,128]{3,2,1,0:T(8,128)S(1)} %get-tuple-element.111), channel_id=1, source_target_pairs={{8,12},{12,16},{9,13},{13,17},{10,14},{14,18},{11,15},{15,19}} | collective-permute-start | bytes 786440 | tf_op jit(solution)/shard_map/ppermute | solution.py:323
  12.1 2.1 %collective-permute-start.12 = (f32[16,2,16,128]{3,2,1,0:T(8,128)S(1)}, f32[16,2,16,128]{3,2,1,0:T(8,128)S(1)}, u32[]{:S(2)}, u32[]{:S(2)}) collective-permute-start(f32[16,2,16,128]{3,2,1,0:T(8,128)S(1)} %get-tuple-element.113), channel_id=1, source_target_pairs={{8,12},{12,16},{16,20},{9,13},{13,17},{17,21},{10,14},{14,18},{18,... | collective-permute-start | bytes 786440 | tf_op jit(solution)/shard_map/ppermute | solution.py:323
  12.8 2.1 %collective-permute-start.13 = (f32[16,2,16,128]{3,2,1,0:T(8,128)S(1)}, f32[16,2,16,128]{3,2,1,0:T(8,128)S(1)}, u32[]{:S(2)}, u32[]{:S(2)}) collective-permute-start(f32[16,2,16,128]{3,2,1,0:T(8,128)S(1)} %get-tuple-element.115), channel_id=1, source_target_pairs={{8,12},{12,16},{16,20},{9,13},{13,17},{17,21},{10,14},{14,18},{18,... | collective-permute-start | bytes 786440 | tf_op jit(solution)/shard_map/ppermute | solution.py:323
  13.5 2.1 %collective-permute-start.14 = (f32[16,2,16,128]{3,2,1,0:T(8,128)S(1)}, f32[16,2,16,128]{3,2,1,0:T(8,128)S(1)}, u32[]{:S(2)}, u32[]{:S(2)}) collective-permute-start(f32[16,2,16,128]{3,2,1,0:T(8,128)S(1)} %get-tuple-element.117), channel_id=1, source_target_pairs={{12,16},{16,20},{13,17},{17,21},{14,18},{18,22},{15,19},{19,23}} | collective-permute-start | bytes 786440 | tf_op jit(solution)/shard_map/ppermute | solution.py:323
  14.2 2.1 %collective-permute-start.15 = (f32[16,2,16,128]{3,2,1,0:T(8,128)S(1)}, f32[16,2,16,128]{3,2,1,0:T(8,128)S(1)}, u32[]{:S(2)}, u32[]{:S(2)}) collective-permute-start(f32[16,2,16,128]{3,2,1,0:T(8,128)S(1)} %get-tuple-element.119), channel_id=1, source_target_pairs={{12,16},{16,20},{20,24},{13,17},{17,21},{21,25},{14,18},{18,22},{2... | collective-permute-start | bytes 786440 | tf_op jit(solution)/shard_map/ppermute | solution.py:323
  15.0 2.8 %collective-permute-start.16 = (f32[16,2,16,128]{3,2,1,0:T(8,128)S(1)}, f32[16,2,16,128]{3,2,1,0:T(8,128)S(1)}, u32[]{:S(2)}, u32[]{:S(2)}) collective-permute-start(f32[16,2,16,128]{3,2,1,0:T(8,128)S(1)} %get-tuple-element.121), channel_id=1, source_target_pairs={{12,16},{16,20},{20,24},{13,17},{17,21},{21,25},{14,18},{18,22},{2... | collective-permute-start | bytes 786440 | tf_op jit(solution)/shard_map/ppermute | solution.py:323
  15.7 3.4 %collective-permute-start.17 = (f32[16,2,16,128]{3,2,1,0:T(8,128)S(1)}, f32[16,2,16,128]{3,2,1,0:T(8,128)S(1)}, u32[]{:S(2)}, u32[]{:S(2)}) collective-permute-start(f32[16,2,16,128]{3,2,1,0:T(8,128)S(1)} %get-tuple-element.123), channel_id=1, source_target_pairs={{16,20},{20,24},{17,21},{21,25},{18,22},{22,26},{19,23},{23,27}} | collective-permute-start | bytes 786440 | tf_op jit(solution)/shard_map/ppermute | solution.py:323
  16.4 27.6 %collective-permute-start.18 = (f32[16,2,16,128]{3,2,1,0:T(8,128)S(1)}, f32[16,2,16,128]{3,2,1,0:T(8,128)S(1)}, u32[]{:S(2)}, u32[]{:S(2)}) collective-permute-start(f32[16,2,16,128]{3,2,1,0:T(8,128)S(1)} %get-tuple-element.125), channel_id=1, source_target_pairs={{16,20},{20,24},{24,28},{17,21},{21,25},{25,29},{18,22},{22,26},{2... | collective-permute-start | bytes 786440 | tf_op jit(solution)/shard_map/ppermute | solution.py:323
  17.8 29.4 %collective-permute-start.19 = (f32[16,2,16,128]{3,2,1,0:T(8,128)S(1)}, f32[16,2,16,128]{3,2,1,0:T(8,128)S(1)}, u32[]{:S(2)}, u32[]{:S(2)}) collective-permute-start(f32[16,2,16,128]{3,2,1,0:T(8,128)S(1)} %get-tuple-element.127), channel_id=1, source_target_pairs={{16,20},{20,24},{24,28},{17,21},{21,25},{25,29},{18,22},{22,26},{2... | collective-permute-start | bytes 786440 | tf_op jit(solution)/shard_map/ppermute | solution.py:323
  19.1 31.5 %collective-permute-start.20 = (f32[16,2,16,128]{3,2,1,0:T(8,128)S(1)}, f32[16,2,16,128]{3,2,1,0:T(8,128)S(1)}, u32[]{:S(2)}, u32[]{:S(2)}) collective-permute-start(f32[16,2,16,128]{3,2,1,0:T(8,128)S(1)} %get-tuple-element.129), channel_id=1, source_target_pairs={{20,24},{24,28},{21,25},{25,29},{22,26},{26,30},{23,27},{27,31}} | collective-permute-start | bytes 786440 | tf_op jit(solution)/shard_map/ppermute | solution.py:323
  45.2 8.6 %collective-permute-start.21 = (f32[16,2,16,128]{3,2,1,0:T(8,128)S(1)}, f32[16,2,16,128]{3,2,1,0:T(8,128)S(1)}, u32[]{:S(2)}, u32[]{:S(2)}) collective-permute-start(f32[16,2,16,128]{3,2,1,0:T(8,128)S(1)} %get-tuple-element.131), channel_id=1, source_target_pairs={{20,24},{24,28},{21,25},{25,29},{22,26},{26,30},{23,27},{27,31}} | collective-permute-start | bytes 786440 | tf_op jit(solution)/shard_map/ppermute | solution.py:323
  48.4 8.6 %collective-permute-start.22 = (f32[16,2,16,128]{3,2,1,0:T(8,128)S(1)}, f32[16,2,16,128]{3,2,1,0:T(8,128)S(1)}, u32[]{:S(2)}, u32[]{:S(2)}) collective-permute-start(f32[16,2,16,128]{3,2,1,0:T(8,128)S(1)} %get-tuple-element.133), channel_id=1, source_target_pairs={{20,24},{24,28},{21,25},{25,29},{22,26},{26,30},{23,27},{27,31}} | collective-permute-start | bytes 786440 | tf_op jit(solution)/shard_map/ppermute | solution.py:323
  51.8 7.8 %collective-permute-start.23 = (f32[16,2,16,128]{3,2,1,0:T(8,128)S(1)}, f32[16,2,16,128]{3,2,1,0:T(8,128)S(1)}, u32[]{:S(2)}, u32[]{:S(2)}) collective-permute-start(f32[16,2,16,128]{3,2,1,0:T(8,128)S(1)} %get-tuple-element.135), channel_id=1, source_target_pairs={{24,28},{25,29},{26,30},{27,31}} | collective-permute-start | bytes 786440 | tf_op jit(solution)/shard_map/ppermute | solution.py:323
  55.2 7.1 %collective-permute-start.24 = (f32[16,2,16,128]{3,2,1,0:T(8,128)S(1)}, f32[16,2,16,128]{3,2,1,0:T(8,128)S(1)}, u32[]{:S(2)}, u32[]{:S(2)}) collective-permute-start(f32[16,2,16,128]{3,2,1,0:T(8,128)S(1)} %get-tuple-element.136), channel_id=1, source_target_pairs={{24,28},{25,29},{26,30},{27,31}} | collective-permute-start | bytes 786440 | tf_op jit(solution)/shard_map/ppermute | solution.py:323
  58.3 7.1 %collective-permute-start.25 = (f32[16,2,16,128]{3,2,1,0:T(8,128)S(1)}, f32[16,2,16,128]{3,2,1,0:T(8,128)S(1)}, u32[]{:S(2)}, u32[]{:S(2)}) collective-permute-start(f32[16,2,16,128]{3,2,1,0:T(8,128)S(1)} %get-tuple-element.138), channel_id=1, source_target_pairs={{24,28},{25,29},{26,30},{27,31}} | collective-permute-start | bytes 786440 | tf_op jit(solution)/shard_map/ppermute | solution.py:323
  66.8 8.2 %collective-permute-start.26 = (f32[2,128,128]{2,1,0:T(8,128)S(1)}, f32[2,128,128]{2,1,0:T(8,128)S(1)}, u32[]{:S(2)}, u32[]{:S(2)}) collective-permute-start(f32[2,128,128]{2,1,0:T(8,128)S(1)} %get-tuple-element.144), channel_id=1, source_target_pairs={{0,2},{1,3},{2,0},{3,1},{4,6},{5,7},{6,4},{7,5},{8,10},{9,11},{10,... | collective-permute-start | bytes 393224 | tf_op jit(solution)/shard_map/ppermute | solution.py:339
  69.2 11.0 %collective-permute-start.27 = (f32[2,128,128]{2,1,0:T(8,128)S(1)}, f32[2,128,128]{2,1,0:T(8,128)S(1)}, u32[]{:S(2)}, u32[]{:S(2)}) collective-permute-start(f32[2,128,128]{2,1,0:T(8,128)S(1)} %get-tuple-element.145), channel_id=1, source_target_pairs={{0,1},{1,2},{2,3},{3,0},{4,5},{5,6},{6,7},{7,4},{8,9},{9,10},{10,1... | collective-permute-start | bytes 393224 | tf_op jit(solution)/shard_map/ppermute | solution.py:339
  69.2 11.0 %collective-permute-start.28 = (f32[2,128,128]{2,1,0:T(8,128)S(1)}, f32[2,128,128]{2,1,0:T(8,128)S(1)}, u32[]{:S(2)}, u32[]{:S(2)}) collective-permute-start(f32[2,128,128]{2,1,0:T(8,128)S(1)} %get-tuple-element.146), channel_id=1, source_target_pairs={{0,3},{1,0},{2,1},{3,2},{4,7},{5,4},{6,5},{7,6},{8,11},{9,8},{10,9... | collective-permute-start | bytes 393224 | tf_op jit(solution)/shard_map/ppermute | solution.py:339

commit v4 on v3

--- a/solution.py
+++ b/solution.py
@@ -335,7 +335,7 @@
         compiler_params=params,
     )(pairs, kept, *early)
     total = lasts[0]
-    for step in sorted(range(1, freq_count), key=lambda step: step % 2):
+    for step in range(1, freq_count):
         total += lax.ppermute(
             lasts[step], "freq", [(f, (f + step) % freq_count) for f in range(freq_count)])
     return total[None]

time: 82.2 us -> 81.9 us (level); the launches traced: 81 us -> 81.5 us
  transfers between devices with their start and end apart: 29 -> 29, of which waited for: 9 -> 10; matrix products, arithmetic and copies ran while one was open for 0% -> 0% of each run, Pallas kernels for 12% -> 12%
where the time goes in v4:
time: 81.9 us; the launch traced here: 81.5 us
  waiting for transfers between devices  39.4 us (48%)
  starting transfers between devices  26.3 us (32%)
  Pallas kernels  14.4 us (18%)
    ppermute x26, waiting for transfers between devices, shards(): lax.ppermute(fields[c], 'depth', [(d, d + 1) for d in range(depth_count -...  29.3 us
    ppermute x26, starting transfers between devices, shards(): lax.ppermute(fields[c], 'depth', [(d, d + 1) for d in range(depth_count -...  22.5 us
    pallas_call x29, Pallas kernels, shards(): pl.pallas_call(functools.partial(propagate_kernel, turn=turn, sizes=sizes...  13.7 us
    ppermute x3, waiting for transfers between devices, shards(): lax.ppermute(lasts[step], 'freq', [(f, (f + step) % freq_count) for f in...  10.1 us
    ppermute x3, starting transfers between devices, shards(): lax.ppermute(lasts[step], 'freq', [(f, (f + step) % freq_count) for f in...  3.82 us
  transfers between devices with their start and end apart: 29, of which 10 were waited for; matrix products, arithmetic and copies ran while one was open for 0% of the time, Pallas kernels for 12%

profile of v4, /device:TPU:15, one launch (start us, length us, event | category | flops | bytes accessed | tf_op | source)
XLA Modules:
  0.0 81.5 jit_solution(16397980820632735389)
XLA Ops:
  0.0 2.9 %shard_map.55 = (s32[6,1,16]{2,1,0:T(1,128)S(4)}, s32[1,2,8]{2,1,0:T(2,128)S(4)}, bf16[16,6,128,256]{3,2,1,0:T(8,128)(2,1)S(1)}, f32[16,2,2,64,128]{4,3,2,1,0:T(...) custom-call(s32[6,1,16]{2,1,0:T(1,128)} %bitcast.4, s32[1,2,8]{2,1,0:T(2,128)} %bitcast.5, ...), custom_call_target="tpu_custom_call" | custom-call | tf_op jit(solution)/shard_map/pallas_call | solution.py:301
  2.9 0.7 collective-permute-start
  3.6 0.1 shard_map.56
  3.7 0.7 collective-permute-start.1
  4.4 0.1 shard_map.57
  4.4 0.7 collective-permute-start.2
  5.1 0.1 shard_map.58
  5.2 0.7 collective-permute-start.3
  5.9 0.1 shard_map.59
  6.0 0.7 collective-permute-start.4
  6.7 0.0 collective-permute-done.2.refs_3_
  6.7 0.1 shard_map.60
  6.8 0.7 collective-permute-start.5
  7.4 0.0 collective-permute-done.3.refs_3_
  7.4 0.1 shard_map.61
  7.5 0.7 collective-permute-start.6
  8.2 0.7 collective-permute-start.7
  9.0 0.7 collective-permute-start.8
  9.7 0.0 collective-permute-done.6.refs_3_
  9.7 0.7 collective-permute-start.9
  10.4 0.0 collective-permute-done.7.refs_3_
  10.4 0.7 collective-permute-start.10
  11.1 0.2 shard_map.66
  11.3 0.7 collective-permute-start.11
  12.1 0.7 collective-permute-start.12
  12.7 0.0 collective-permute-done.10.refs_3_
  12.8 0.7 collective-permute-start.13
  13.5 0.7 collective-permute-start.14
  14.2 0.7 collective-permute-start.15
  15.0 0.7 collective-permute-start.16
  15.7 0.7 collective-permute-start.17
  16.4 1.3 %collective-permute-start.18 = (f32[16,2,16,128]{3,2,1,0:T(8,128)S(1)}, f32[16,2,16,128]{3,2,1,0:T(8,128)S(1)}, u32[]{:S(2)}, u32[]{:S(2)}) collective-permute-start(f32[16,2,16,128]{3,2,1,0:T(8,128)S(1)} %get-tuple-element.125), channel_id=1, source_target_pairs={{16,20},{20,24},{24,28},{17,21},{21,25},{25,29},{18,22},{22,26},{2... | collective-permute-start | bytes 786440 | tf_op jit(solution)/shard_map/ppermute | solution.py:323
  17.8 1.3 %collective-permute-start.19 = (f32[16,2,16,128]{3,2,1,0:T(8,128)S(1)}, f32[16,2,16,128]{3,2,1,0:T(8,128)S(1)}, u32[]{:S(2)}, u32[]{:S(2)}) collective-permute-start(f32[16,2,16,128]{3,2,1,0:T(8,128)S(1)} %get-tuple-element.127), channel_id=1, source_target_pairs={{16,20},{20,24},{24,28},{17,21},{21,25},{25,29},{18,22},{22,26},{2... | collective-permute-start | bytes 786440 | tf_op jit(solution)/shard_map/ppermute | solution.py:323
  19.1 1.3 %collective-permute-start.20 = (f32[16,2,16,128]{3,2,1,0:T(8,128)S(1)}, f32[16,2,16,128]{3,2,1,0:T(8,128)S(1)}, u32[]{:S(2)}, u32[]{:S(2)}) collective-permute-start(f32[16,2,16,128]{3,2,1,0:T(8,128)S(1)} %get-tuple-element.129), channel_id=1, source_target_pairs={{20,24},{24,28},{21,25},{25,29},{22,26},{26,30},{23,27},{27,31}} | collective-permute-start | bytes 786440 | tf_op jit(solution)/shard_map/ppermute | solution.py:323
  20.4 23.6 %collective-permute-done.18.refs_3_ = f32[16,2,16,128]{3,2,1,0:T(8,128)S(1)} collective-permute-done((f32[16,2,16,128]{3,2,1,0:T(8,128)S(1)}, f32[16,2,16,128]{3,2,1,0:T(8,128)S(1)}, u32[]{:S(2)}, u32[]{:S(2)}) %collective-permute-start.18) | collective-permute-done | bytes 262176 | tf_op jit(solution)/shard_map/ppermute | solution.py:323
  44.0 1.2 %shard_map.76 = (f32[16,2,2,64,128]{4,3,2,1,0:T(8,128)S(1)}, f32[16,2,16,128]{3,2,1,0:T(8,128)S(1)}) custom-call(s32[6,1,16]{2,1,0:T(1,128)S(4)} %get-tuple-element.77.refs_0_, bf16[16,6,128,256]{3,2,1,0:T(8,128)(2,1)S(1)} %get-tuple-element.78.refs_1_, f32[16,2,2,64,128]{4,3,2,1,0:T(8,128)S(1)} %get-tuple-element.124.refs_2_, ...), custom_call_target="tpu_custom_call", output_to_operand_aliasing={{0}: (2, {})} | custom-call | tf_op jit(solution)/shard_map/pallas_call | solution.py:301
  45.2 1.3 %collective-permute-start.21 = (f32[16,2,16,128]{3,2,1,0:T(8,128)S(1)}, f32[16,2,16,128]{3,2,1,0:T(8,128)S(1)}, u32[]{:S(2)}, u32[]{:S(2)}) collective-permute-start(f32[16,2,16,128]{3,2,1,0:T(8,128)S(1)} %get-tuple-element.131), channel_id=1, source_target_pairs={{20,24},{24,28},{21,25},{25,29},{22,26},{26,30},{23,27},{27,31}} | collective-permute-start | bytes 786440 | tf_op jit(solution)/shard_map/ppermute | solution.py:323
  46.5 0.7 collective-permute-done.19.refs_3_
  47.2 1.2 %shard_map.77 = (f32[16,2,2,64,128]{4,3,2,1,0:T(8,128)S(1)}, f32[16,2,16,128]{3,2,1,0:T(8,128)S(1)}) custom-call(s32[6,1,16]{2,1,0:T(1,128)S(4)} %get-tuple-element.77.refs_0_, bf16[16,6,128,256]{3,2,1,0:T(8,128)(2,1)S(1)} %get-tuple-element.78.refs_1_, f32[16,2,2,64,128]{4,3,2,1,0:T(8,128)S(1)} %get-tuple-element.126.refs_2_, ...), custom_call_target="tpu_custom_call", output_to_operand_aliasing={{0}: (2, {})} | custom-call | tf_op jit(solution)/shard_map/pallas_call | solution.py:301
  48.4 1.3 %collective-permute-start.22 = (f32[16,2,16,128]{3,2,1,0:T(8,128)S(1)}, f32[16,2,16,128]{3,2,1,0:T(8,128)S(1)}, u32[]{:S(2)}, u32[]{:S(2)}) collective-permute-start(f32[16,2,16,128]{3,2,1,0:T(8,128)S(1)} %get-tuple-element.133), channel_id=1, source_target_pairs={{20,24},{24,28},{21,25},{25,29},{22,26},{26,30},{23,27},{27,31}} | collective-permute-start | bytes 786440 | tf_op jit(solution)/shard_map/ppermute | solution.py:323
  49.7 0.8 %collective-permute-done.20.refs_3_ = f32[16,2,16,128]{3,2,1,0:T(8,128)S(1)} collective-permute-done((f32[16,2,16,128]{3,2,1,0:T(8,128)S(1)}, f32[16,2,16,128]{3,2,1,0:T(8,128)S(1)}, u32[]{:S(2)}, u32[]{:S(2)}) %collective-permute-start.20) | collective-permute-done | bytes 262176 | tf_op jit(solution)/shard_map/ppermute | solution.py:323
  50.6 1.2 %shard_map.78 = (f32[16,2,2,64,128]{4,3,2,1,0:T(8,128)S(1)}, f32[16,2,16,128]{3,2,1,0:T(8,128)S(1)}) custom-call(s32[6,1,16]{2,1,0:T(1,128)S(4)} %get-tuple-element.77.refs_0_, bf16[16,6,128,256]{3,2,1,0:T(8,128)(2,1)S(1)} %get-tuple-element.78.refs_1_, f32[16,2,2,64,128]{4,3,2,1,0:T(8,128)S(1)} %get-tuple-element.128.refs_2_, ...), custom_call_target="tpu_custom_call", output_to_operand_aliasing={{0}: (2, {})} | custom-call | tf_op jit(solution)/shard_map/pallas_call | solution.py:301
  51.8 1.3 %collective-permute-start.23 = (f32[16,2,16,128]{3,2,1,0:T(8,128)S(1)}, f32[16,2,16,128]{3,2,1,0:T(8,128)S(1)}, u32[]{:S(2)}, u32[]{:S(2)}) collective-permute-start(f32[16,2,16,128]{3,2,1,0:T(8,128)S(1)} %get-tuple-element.135), channel_id=1, source_target_pairs={{24,28},{25,29},{26,30},{27,31}} | collective-permute-start | bytes 786440 | tf_op jit(solution)/shard_map/ppermute | solution.py:323
  53.1 0.7 collective-permute-done.21.refs_3_
  53.8 1.4 %shard_map.79 = (f32[16,2,2,64,128]{4,3,2,1,0:T(8,128)S(1)}, f32[16,2,16,128]{3,2,1,0:T(8,128)S(1)}) custom-call(s32[6,1,16]{2,1,0:T(1,128)S(4)} %get-tuple-element.77.refs_0_, bf16[16,6,128,256]{3,2,1,0:T(8,128)(2,1)S(1)} %get-tuple-element.78.refs_1_, f32[16,2,2,64,128]{4,3,2,1,0:T(8,128)S(1)} %get-tuple-element.130.refs_2_, ...), custom_call_target="tpu_custom_call", output_to_operand_aliasing={{0}: (2, {})} | custom-call | tf_op jit(solution)/shard_map/pallas_call | solution.py:301
  55.2 1.3 %collective-permute-start.24 = (f32[16,2,16,128]{3,2,1,0:T(8,128)S(1)}, f32[16,2,16,128]{3,2,1,0:T(8,128)S(1)}, u32[]{:S(2)}, u32[]{:S(2)}) collective-permute-start(f32[16,2,16,128]{3,2,1,0:T(8,128)S(1)} %get-tuple-element.136), channel_id=1, source_target_pairs={{24,28},{25,29},{26,30},{27,31}} | collective-permute-start | bytes 786440 | tf_op jit(solution)/shard_map/ppermute | solution.py:323
  56.5 0.5 collective-permute-done.22.refs_3_
  57.0 1.2 %shard_map.80 = (f32[16,2,2,64,128]{4,3,2,1,0:T(8,128)S(1)}, f32[16,2,16,128]{3,2,1,0:T(8,128)S(1)}) custom-call(s32[6,1,16]{2,1,0:T(1,128)S(4)} %get-tuple-element.77.refs_0_, bf16[16,6,128,256]{3,2,1,0:T(8,128)(2,1)S(1)} %get-tuple-element.78.refs_1_, f32[16,2,2,64,128]{4,3,2,1,0:T(8,128)S(1)} %get-tuple-element.132.refs_2_, ...), custom_call_target="tpu_custom_call", output_to_operand_aliasing={{0}: (2, {})} | custom-call | tf_op jit(solution)/shard_map/pallas_call | solution.py:301
  58.3 1.3 %collective-permute-start.25 = (f32[16,2,16,128]{3,2,1,0:T(8,128)S(1)}, f32[16,2,16,128]{3,2,1,0:T(8,128)S(1)}, u32[]{:S(2)}, u32[]{:S(2)}) collective-permute-start(f32[16,2,16,128]{3,2,1,0:T(8,128)S(1)} %get-tuple-element.138), channel_id=1, source_target_pairs={{24,28},{25,29},{26,30},{27,31}} | collective-permute-start | bytes 786440 | tf_op jit(solution)/shard_map/ppermute | solution.py:323
  59.6 0.0 collective-permute-done.23.refs_3_
  59.6 1.2 %shard_map.81.refs_2_ = f32[16,2,2,64,128]{4,3,2,1,0:T(8,128)S(1)} custom-call(s32[6,1,16]{2,1,0:T(1,128)S(4)} %get-tuple-element.77.refs_0_, bf16[16,6,128,256]{3,2,1,0:T(8,128)(2,1)S(1)} %get-tuple-element.78.refs_1_, f32[16,2,2,64,128]{4,3,2,1,0:T(8,128)S(1)} %get-tuple-element.134.refs_2_, ...), custom_call_target="tpu_custom_call", output_to_operand_aliasing={{}: (2, {})} | custom-call | tf_op jit(solution)/shard_map/pallas_call | solution.py:301
  60.8 1.5 %collective-permute-done.24.refs_3_ = f32[16,2,16,128]{3,2,1,0:T(8,128)S(1)} collective-permute-done((f32[16,2,16,128]{3,2,1,0:T(8,128)S(1)}, f32[16,2,16,128]{3,2,1,0:T(8,128)S(1)}, u32[]{:S(2)}, u32[]{:S(2)}) %collective-permute-start.24) | collective-permute-done | bytes 262176 | tf_op jit(solution)/shard_map/ppermute | solution.py:323
  62.3 1.2 %shard_map.82.kept_in = f32[16,2,2,64,128]{4,3,2,1,0:T(8,128)S(1)} custom-call(s32[6,1,16]{2,1,0:T(1,128)S(4)} %get-tuple-element.77.refs_0_, bf16[16,6,128,256]{3,2,1,0:T(8,128)(2,1)S(1)} %get-tuple-element.78.refs_1_, f32[16,2,2,64,128]{4,3,2,1,0:T(8,128)S(1)} %shard_map.81.refs_2_, ...), custom_call_target="tpu_custom_call", output_to_operand_aliasing={{}: (2, {})} | custom-call | tf_op jit(solution)/shard_map/pallas_call | solution.py:301
  63.6 0.4 shard_map.83
  64.0 1.3 %collective-permute-done.25.refs_3_ = f32[16,2,16,128]{3,2,1,0:T(8,128)S(1)} collective-permute-done((f32[16,2,16,128]{3,2,1,0:T(8,128)S(1)}, f32[16,2,16,128]{3,2,1,0:T(8,128)S(1)}, u32[]{:S(2)}, u32[]{:S(2)}) %collective-permute-start.25) | collective-permute-done | bytes 262176 | tf_op jit(solution)/shard_map/ppermute | solution.py:323
  65.3 1.2 %shard_map.84.kept = f32[16,2,2,64,128]{4,3,2,1,0:T(8,128)S(1)} custom-call(s32[6,1,16]{2,1,0:T(1,128)S(4)} %get-tuple-element.77.refs_0_, bf16[16,6,128,256]{3,2,1,0:T(8,128)(2,1)S(1)} %get-tuple-element.78.refs_1_, f32[16,2,2,64,128]{4,3,2,1,0:T(8,128)S(1)} %get-tuple-element.137.refs_2_, ...), custom_call_target="tpu_custom_call", output_to_operand_aliasing={{}: (2, {})} | custom-call | tf_op jit(solution)/shard_map/pallas_call | solution.py:301
  66.5 0.3 shard_map.85
  66.8 1.3 %collective-permute-start.26 = (f32[2,128,128]{2,1,0:T(8,128)S(1)}, f32[2,128,128]{2,1,0:T(8,128)S(1)}, u32[]{:S(2)}, u32[]{:S(2)}) collective-permute-start(f32[2,128,128]{2,1,0:T(8,128)S(1)} %get-tuple-element.144), channel_id=1, source_target_pairs={{0,1},{1,2},{2,3},{3,0},{4,5},{5,6},{6,7},{7,4},{8,9},{9,10},{10,1... | collective-permute-start | bytes 393224 | tf_op jit(solution)/shard_map/ppermute | solution.py:339
  68.2 1.1 %collective-permute-start.27 = (f32[2,128,128]{2,1,0:T(8,128)S(1)}, f32[2,128,128]{2,1,0:T(8,128)S(1)}, u32[]{:S(2)}, u32[]{:S(2)}) collective-permute-start(f32[2,128,128]{2,1,0:T(8,128)S(1)} %get-tuple-element.145), channel_id=1, source_target_pairs={{0,2},{1,3},{2,0},{3,1},{4,6},{5,7},{6,4},{7,5},{8,10},{9,11},{10,... | collective-permute-start | bytes 393224 | tf_op jit(solution)/shard_map/ppermute | solution.py:339
  69.3 1.4 %collective-permute-start.28 = (f32[2,128,128]{2,1,0:T(8,128)S(1)}, f32[2,128,128]{2,1,0:T(8,128)S(1)}, u32[]{:S(2)}, u32[]{:S(2)}) collective-permute-start(f32[2,128,128]{2,1,0:T(8,128)S(1)} %get-tuple-element.146), channel_id=1, source_target_pairs={{0,3},{1,0},{2,1},{3,2},{4,7},{5,4},{6,5},{7,6},{8,11},{9,8},{10,9... | collective-permute-start | bytes 393224 | tf_op jit(solution)/shard_map/ppermute | solution.py:339
  70.7 6.3 %collective-permute-done.26 = f32[2,128,128]{2,1,0:T(8,128)S(1)} collective-permute-done((f32[2,128,128]{2,1,0:T(8,128)S(1)}, f32[2,128,128]{2,1,0:T(8,128)S(1)}, u32[]{:S(2)}, u32[]{:S(2)}) %collective-permute-start.26) | collective-permute-done | bytes 131104 | tf_op jit(solution)/shard_map/ppermute | solution.py:339
  76.9 2.4 %collective-permute-done.27 = f32[2,128,128]{2,1,0:T(8,128)S(1)} collective-permute-done((f32[2,128,128]{2,1,0:T(8,128)S(1)}, f32[2,128,128]{2,1,0:T(8,128)S(1)}, u32[]{:S(2)}, u32[]{:S(2)}) %collective-permute-start.27) | collective-permute-done | bytes 131104 | tf_op jit(solution)/shard_map/ppermute | solution.py:339
  79.3 1.5 %collective-permute-done.28 = f32[2,128,128]{2,1,0:T(8,128)S(1)} collective-permute-done((f32[2,128,128]{2,1,0:T(8,128)S(1)}, f32[2,128,128]{2,1,0:T(8,128)S(1)}, u32[]{:S(2)}, u32[]{:S(2)}) %collective-permute-start.28) | collective-permute-done | bytes 131104 | tf_op jit(solution)/shard_map/ppermute | solution.py:339
  80.8 0.7 add_bitcast_fusion
  (26 shorter events, 0.3 us)
Async XLA Ops:
  2.9 2.2 %collective-permute-start = (f32[16,2,16,128]{3,2,1,0:T(8,128)S(1)}, f32[16,2,16,128]{3,2,1,0:T(8,128)S(1)}, u32[]{:S(2)}, u32[]{:S(2)}) collective-permute-start(f32[16,2,16,128]{3,2,1,0:T(8,128)S(1)} %get-tuple-element.84), channel_id=1, source_target_pairs={{0,4},{1,5},{2,6},{3,7}} | collective-permute-start | bytes 786440 | tf_op jit(solution)/shard_map/ppermute | solution.py:323
  3.7 2.2 %collective-permute-start.1 = (f32[16,2,16,128]{3,2,1,0:T(8,128)S(1)}, f32[16,2,16,128]{3,2,1,0:T(8,128)S(1)}, u32[]{:S(2)}, u32[]{:S(2)}) collective-permute-start(f32[16,2,16,128]{3,2,1,0:T(8,128)S(1)} %get-tuple-element.87), channel_id=1, source_target_pairs={{0,4},{1,5},{2,6},{3,7}} | collective-permute-start | bytes 786440 | tf_op jit(solution)/shard_map/ppermute | solution.py:323
  4.4 2.2 %collective-permute-start.2 = (f32[16,2,16,128]{3,2,1,0:T(8,128)S(1)}, f32[16,2,16,128]{3,2,1,0:T(8,128)S(1)}, u32[]{:S(2)}, u32[]{:S(2)}) collective-permute-start(f32[16,2,16,128]{3,2,1,0:T(8,128)S(1)} %get-tuple-element.90), channel_id=1, source_target_pairs={{0,4},{1,5},{2,6},{3,7}} | collective-permute-start | bytes 786440 | tf_op jit(solution)/shard_map/ppermute | solution.py:323
  5.2 2.2 %collective-permute-start.3 = (f32[16,2,16,128]{3,2,1,0:T(8,128)S(1)}, f32[16,2,16,128]{3,2,1,0:T(8,128)S(1)}, u32[]{:S(2)}, u32[]{:S(2)}) collective-permute-start(f32[16,2,16,128]{3,2,1,0:T(8,128)S(1)} %get-tuple-element.93), channel_id=1, source_target_pairs={{0,4},{4,8},{1,5},{5,9},{2,6},{6,10},{3,7},{7,11}} | collective-permute-start | bytes 786440 | tf_op jit(solution)/shard_map/ppermute | solution.py:323
  6.0 2.2 %collective-permute-start.4 = (f32[16,2,16,128]{3,2,1,0:T(8,128)S(1)}, f32[16,2,16,128]{3,2,1,0:T(8,128)S(1)}, u32[]{:S(2)}, u32[]{:S(2)}) collective-permute-start(f32[16,2,16,128]{3,2,1,0:T(8,128)S(1)} %get-tuple-element.96), channel_id=1, source_target_pairs={{0,4},{4,8},{1,5},{5,9},{2,6},{6,10},{3,7},{7,11}} | collective-permute-start | bytes 786440 | tf_op jit(solution)/shard_map/ppermute | solution.py:323
  6.8 2.2 %collective-permute-start.5 = (f32[16,2,16,128]{3,2,1,0:T(8,128)S(1)}, f32[16,2,16,128]{3,2,1,0:T(8,128)S(1)}, u32[]{:S(2)}, u32[]{:S(2)}) collective-permute-start(f32[16,2,16,128]{3,2,1,0:T(8,128)S(1)} %get-tuple-element.99), channel_id=1, source_target_pairs={{0,4},{4,8},{1,5},{5,9},{2,6},{6,10},{3,7},{7,11}} | collective-permute-start | bytes 786440 | tf_op jit(solution)/shard_map/ppermute | solution.py:323
  7.5 2.1 %collective-permute-start.6 = (f32[16,2,16,128]{3,2,1,0:T(8,128)S(1)}, f32[16,2,16,128]{3,2,1,0:T(8,128)S(1)}, u32[]{:S(2)}, u32[]{:S(2)}) collective-permute-start(f32[16,2,16,128]{3,2,1,0:T(8,128)S(1)} %get-tuple-element.101), channel_id=1, source_target_pairs={{0,4},{4,8},{8,12},{1,5},{5,9},{9,13},{2,6},{6,10},{10,14},{3,7},{... | collective-permute-start | bytes 786440 | tf_op jit(solution)/shard_map/ppermute | solution.py:323
  8.2 2.1 %collective-permute-start.7 = (f32[16,2,16,128]{3,2,1,0:T(8,128)S(1)}, f32[16,2,16,128]{3,2,1,0:T(8,128)S(1)}, u32[]{:S(2)}, u32[]{:S(2)}) collective-permute-start(f32[16,2,16,128]{3,2,1,0:T(8,128)S(1)} %get-tuple-element.103), channel_id=1, source_target_pairs={{0,4},{4,8},{8,12},{1,5},{5,9},{9,13},{2,6},{6,10},{10,14},{3,7},{... | collective-permute-start | bytes 786440 | tf_op jit(solution)/shard_map/ppermute | solution.py:323
  9.0 2.1 %collective-permute-start.8 = (f32[16,2,16,128]{3,2,1,0:T(8,128)S(1)}, f32[16,2,16,128]{3,2,1,0:T(8,128)S(1)}, u32[]{:S(2)}, u32[]{:S(2)}) collective-permute-start(f32[16,2,16,128]{3,2,1,0:T(8,128)S(1)} %get-tuple-element.105), channel_id=1, source_target_pairs={{4,8},{8,12},{5,9},{9,13},{6,10},{10,14},{7,11},{11,15}} | collective-permute-start | bytes 786440 | tf_op jit(solution)/shard_map/ppermute | solution.py:323
  9.7 2.3 %collective-permute-start.9 = (f32[16,2,16,128]{3,2,1,0:T(8,128)S(1)}, f32[16,2,16,128]{3,2,1,0:T(8,128)S(1)}, u32[]{:S(2)}, u32[]{:S(2)}) collective-permute-start(f32[16,2,16,128]{3,2,1,0:T(8,128)S(1)} %get-tuple-element.107), channel_id=1, source_target_pairs={{4,8},{8,12},{12,16},{5,9},{9,13},{13,17},{6,10},{10,14},{14,18},{... | collective-permute-start | bytes 786440 | tf_op jit(solution)/shard_map/ppermute | solution.py:323
  10.4 2.3 %collective-permute-start.10 = (f32[16,2,16,128]{3,2,1,0:T(8,128)S(1)}, f32[16,2,16,128]{3,2,1,0:T(8,128)S(1)}, u32[]{:S(2)}, u32[]{:S(2)}) collective-permute-start(f32[16,2,16,128]{3,2,1,0:T(8,128)S(1)} %get-tuple-element.109), channel_id=1, source_target_pairs={{4,8},{8,12},{12,16},{5,9},{9,13},{13,17},{6,10},{10,14},{14,18},{... | collective-permute-start | bytes 786440 | tf_op jit(solution)/shard_map/ppermute | solution.py:323
  11.3 2.1 %collective-permute-start.11 = (f32[16,2,16,128]{3,2,1,0:T(8,128)S(1)}, f32[16,2,16,128]{3,2,1,0:T(8,128)S(1)}, u32[]{:S(2)}, u32[]{:S(2)}) collective-permute-start(f32[16,2,16,128]{3,2,1,0:T(8,128)S(1)} %get-tuple-element.111), channel_id=1, source_target_pairs={{8,12},{12,16},{9,13},{13,17},{10,14},{14,18},{11,15},{15,19}} | collective-permute-start | bytes 786440 | tf_op jit(solution)/shard_map/ppermute | solution.py:323
  12.1 2.1 %collective-permute-start.12 = (f32[16,2,16,128]{3,2,1,0:T(8,128)S(1)}, f32[16,2,16,128]{3,2,1,0:T(8,128)S(1)}, u32[]{:S(2)}, u32[]{:S(2)}) collective-permute-start(f32[16,2,16,128]{3,2,1,0:T(8,128)S(1)} %get-tuple-element.113), channel_id=1, source_target_pairs={{8,12},{12,16},{16,20},{9,13},{13,17},{17,21},{10,14},{14,18},{18,... | collective-permute-start | bytes 786440 | tf_op jit(solution)/shard_map/ppermute | solution.py:323
  12.8 2.1 %collective-permute-start.13 = (f32[16,2,16,128]{3,2,1,0:T(8,128)S(1)}, f32[16,2,16,128]{3,2,1,0:T(8,128)S(1)}, u32[]{:S(2)}, u32[]{:S(2)}) collective-permute-start(f32[16,2,16,128]{3,2,1,0:T(8,128)S(1)} %get-tuple-element.115), channel_id=1, source_target_pairs={{8,12},{12,16},{16,20},{9,13},{13,17},{17,21},{10,14},{14,18},{18,... | collective-permute-start | bytes 786440 | tf_op jit(solution)/shard_map/ppermute | solution.py:323
  13.5 2.1 %collective-permute-start.14 = (f32[16,2,16,128]{3,2,1,0:T(8,128)S(1)}, f32[16,2,16,128]{3,2,1,0:T(8,128)S(1)}, u32[]{:S(2)}, u32[]{:S(2)}) collective-permute-start(f32[16,2,16,128]{3,2,1,0:T(8,128)S(1)} %get-tuple-element.117), channel_id=1, source_target_pairs={{12,16},{16,20},{13,17},{17,21},{14,18},{18,22},{15,19},{19,23}} | collective-permute-start | bytes 786440 | tf_op jit(solution)/shard_map/ppermute | solution.py:323
  14.2 2.1 %collective-permute-start.15 = (f32[16,2,16,128]{3,2,1,0:T(8,128)S(1)}, f32[16,2,16,128]{3,2,1,0:T(8,128)S(1)}, u32[]{:S(2)}, u32[]{:S(2)}) collective-permute-start(f32[16,2,16,128]{3,2,1,0:T(8,128)S(1)} %get-tuple-element.119), channel_id=1, source_target_pairs={{12,16},{16,20},{20,24},{13,17},{17,21},{21,25},{14,18},{18,22},{2... | collective-permute-start | bytes 786440 | tf_op jit(solution)/shard_map/ppermute | solution.py:323
  15.0 2.8 %collective-permute-start.16 = (f32[16,2,16,128]{3,2,1,0:T(8,128)S(1)}, f32[16,2,16,128]{3,2,1,0:T(8,128)S(1)}, u32[]{:S(2)}, u32[]{:S(2)}) collective-permute-start(f32[16,2,16,128]{3,2,1,0:T(8,128)S(1)} %get-tuple-element.121), channel_id=1, source_target_pairs={{12,16},{16,20},{20,24},{13,17},{17,21},{21,25},{14,18},{18,22},{2... | collective-permute-start | bytes 786440 | tf_op jit(solution)/shard_map/ppermute | solution.py:323
  15.7 3.4 %collective-permute-start.17 = (f32[16,2,16,128]{3,2,1,0:T(8,128)S(1)}, f32[16,2,16,128]{3,2,1,0:T(8,128)S(1)}, u32[]{:S(2)}, u32[]{:S(2)}) collective-permute-start(f32[16,2,16,128]{3,2,1,0:T(8,128)S(1)} %get-tuple-element.123), channel_id=1, source_target_pairs={{16,20},{20,24},{17,21},{21,25},{18,22},{22,26},{19,23},{23,27}} | collective-permute-start | bytes 786440 | tf_op jit(solution)/shard_map/ppermute | solution.py:323
  16.4 27.6 %collective-permute-start.18 = (f32[16,2,16,128]{3,2,1,0:T(8,128)S(1)}, f32[16,2,16,128]{3,2,1,0:T(8,128)S(1)}, u32[]{:S(2)}, u32[]{:S(2)}) collective-permute-start(f32[16,2,16,128]{3,2,1,0:T(8,128)S(1)} %get-tuple-element.125), channel_id=1, source_target_pairs={{16,20},{20,24},{24,28},{17,21},{21,25},{25,29},{18,22},{22,26},{2... | collective-permute-start | bytes 786440 | tf_op jit(solution)/shard_map/ppermute | solution.py:323
  17.8 29.4 %collective-permute-start.19 = (f32[16,2,16,128]{3,2,1,0:T(8,128)S(1)}, f32[16,2,16,128]{3,2,1,0:T(8,128)S(1)}, u32[]{:S(2)}, u32[]{:S(2)}) collective-permute-start(f32[16,2,16,128]{3,2,1,0:T(8,128)S(1)} %get-tuple-element.127), channel_id=1, source_target_pairs={{16,20},{20,24},{24,28},{17,21},{21,25},{25,29},{18,22},{22,26},{2... | collective-permute-start | bytes 786440 | tf_op jit(solution)/shard_map/ppermute | solution.py:323
  19.1 31.5 %collective-permute-start.20 = (f32[16,2,16,128]{3,2,1,0:T(8,128)S(1)}, f32[16,2,16,128]{3,2,1,0:T(8,128)S(1)}, u32[]{:S(2)}, u32[]{:S(2)}) collective-permute-start(f32[16,2,16,128]{3,2,1,0:T(8,128)S(1)} %get-tuple-element.129), channel_id=1, source_target_pairs={{20,24},{24,28},{21,25},{25,29},{22,26},{26,30},{23,27},{27,31}} | collective-permute-start | bytes 786440 | tf_op jit(solution)/shard_map/ppermute | solution.py:323
  45.2 8.6 %collective-permute-start.21 = (f32[16,2,16,128]{3,2,1,0:T(8,128)S(1)}, f32[16,2,16,128]{3,2,1,0:T(8,128)S(1)}, u32[]{:S(2)}, u32[]{:S(2)}) collective-permute-start(f32[16,2,16,128]{3,2,1,0:T(8,128)S(1)} %get-tuple-element.131), channel_id=1, source_target_pairs={{20,24},{24,28},{21,25},{25,29},{22,26},{26,30},{23,27},{27,31}} | collective-permute-start | bytes 786440 | tf_op jit(solution)/shard_map/ppermute | solution.py:323
  48.4 8.6 %collective-permute-start.22 = (f32[16,2,16,128]{3,2,1,0:T(8,128)S(1)}, f32[16,2,16,128]{3,2,1,0:T(8,128)S(1)}, u32[]{:S(2)}, u32[]{:S(2)}) collective-permute-start(f32[16,2,16,128]{3,2,1,0:T(8,128)S(1)} %get-tuple-element.133), channel_id=1, source_target_pairs={{20,24},{24,28},{21,25},{25,29},{22,26},{26,30},{23,27},{27,31}} | collective-permute-start | bytes 786440 | tf_op jit(solution)/shard_map/ppermute | solution.py:323
  51.8 7.8 %collective-permute-start.23 = (f32[16,2,16,128]{3,2,1,0:T(8,128)S(1)}, f32[16,2,16,128]{3,2,1,0:T(8,128)S(1)}, u32[]{:S(2)}, u32[]{:S(2)}) collective-permute-start(f32[16,2,16,128]{3,2,1,0:T(8,128)S(1)} %get-tuple-element.135), channel_id=1, source_target_pairs={{24,28},{25,29},{26,30},{27,31}} | collective-permute-start | bytes 786440 | tf_op jit(solution)/shard_map/ppermute | solution.py:323
  55.2 7.1 %collective-permute-start.24 = (f32[16,2,16,128]{3,2,1,0:T(8,128)S(1)}, f32[16,2,16,128]{3,2,1,0:T(8,128)S(1)}, u32[]{:S(2)}, u32[]{:S(2)}) collective-permute-start(f32[16,2,16,128]{3,2,1,0:T(8,128)S(1)} %get-tuple-element.136), channel_id=1, source_target_pairs={{24,28},{25,29},{26,30},{27,31}} | collective-permute-start | bytes 786440 | tf_op jit(solution)/shard_map/ppermute | solution.py:323
  58.3 7.1 %collective-permute-start.25 = (f32[16,2,16,128]{3,2,1,0:T(8,128)S(1)}, f32[16,2,16,128]{3,2,1,0:T(8,128)S(1)}, u32[]{:S(2)}, u32[]{:S(2)}) collective-permute-start(f32[16,2,16,128]{3,2,1,0:T(8,128)S(1)} %get-tuple-element.138), channel_id=1, source_target_pairs={{24,28},{25,29},{26,30},{27,31}} | collective-permute-start | bytes 786440 | tf_op jit(solution)/shard_map/ppermute | solution.py:323
  66.8 10.1 %collective-permute-start.26 = (f32[2,128,128]{2,1,0:T(8,128)S(1)}, f32[2,128,128]{2,1,0:T(8,128)S(1)}, u32[]{:S(2)}, u32[]{:S(2)}) collective-permute-start(f32[2,128,128]{2,1,0:T(8,128)S(1)} %get-tuple-element.144), channel_id=1, source_target_pairs={{0,1},{1,2},{2,3},{3,0},{4,5},{5,6},{6,7},{7,4},{8,9},{9,10},{10,1... | collective-permute-start | bytes 393224 | tf_op jit(solution)/shard_map/ppermute | solution.py:339
  68.2 11.1 %collective-permute-start.27 = (f32[2,128,128]{2,1,0:T(8,128)S(1)}, f32[2,128,128]{2,1,0:T(8,128)S(1)}, u32[]{:S(2)}, u32[]{:S(2)}) collective-permute-start(f32[2,128,128]{2,1,0:T(8,128)S(1)} %get-tuple-element.145), channel_id=1, source_target_pairs={{0,2},{1,3},{2,0},{3,1},{4,6},{5,7},{6,4},{7,5},{8,10},{9,11},{10,... | collective-permute-start | bytes 393224 | tf_op jit(solution)/shard_map/ppermute | solution.py:339
  69.3 11.5 %collective-permute-start.28 = (f32[2,128,128]{2,1,0:T(8,128)S(1)}, f32[2,128,128]{2,1,0:T(8,128)S(1)}, u32[]{:S(2)}, u32[]{:S(2)}) collective-permute-start(f32[2,128,128]{2,1,0:T(8,128)S(1)} %get-tuple-element.146), channel_id=1, source_target_pairs={{0,3},{1,0},{2,1},{3,2},{4,7},{5,4},{6,5},{7,6},{8,11},{9,8},{10,9... | collective-permute-start | bytes 393224 | tf_op jit(solution)/shard_map/ppermute | solution.py:339

commit v5 on v4

--- a/solution.py
+++ b/solution.py
@@ -97,6 +97,11 @@
             for copy in draw(0, drawn, 0):
                 copy.start()
 
+    if first:
+        for k in range(CHUNKS):
+            for part, copy in enumerate(chunk(k)):
+                copy.start(priority=part)
+
     if upcoming is not None:
         @pl.when(depth == 0)
         def _():
@@ -104,9 +109,6 @@
                 copy.start()
 
     if first:
-        for k in range(CHUNKS):
-            for copy in chunk(k):
-                copy.start()
         for copy in tables:
             copy.wait()
 

time: 81.9 us -> 81.9 us (level)
  no operation moved by 1% of the time
where the time goes in v5:
time: 81.9 us; the launch traced here: 81.5 us
  waiting for transfers between devices  39.4 us (48%)
  starting transfers between devices  26.4 us (32%)
  Pallas kernels  14.4 us (18%)
    ppermute x26, waiting for transfers between devices, shards(): lax.ppermute(fields[c], 'depth', [(d, d + 1) for d in range(depth_count -...  29.3 us
    ppermute x26, starting transfers between devices, shards(): lax.ppermute(fields[c], 'depth', [(d, d + 1) for d in range(depth_count -...  22.5 us
    pallas_call x29, Pallas kernels, shards(): pl.pallas_call(functools.partial(propagate_kernel, turn=turn, sizes=sizes...  13.7 us
    ppermute x3, waiting for transfers between devices, shards(): lax.ppermute(lasts[step], 'freq', [(f, (f + step) % freq_count) for f in...  10.1 us
    ppermute x3, starting transfers between devices, shards(): lax.ppermute(lasts[step], 'freq', [(f, (f + step) % freq_count) for f in...  3.83 us
  transfers between devices with their start and end apart: 29, of which 10 were waited for; matrix products, arithmetic and copies ran while one was open for 0% of the time, Pallas kernels for 12%

profile of v5, /device:TPU:15, one launch (start us, length us, event | category | flops | bytes accessed | tf_op | source)
XLA Modules:
  0.0 81.5 jit_solution(17511000179643522502)
XLA Ops:
  0.0 2.9 %shard_map.55 = (s32[6,1,16]{2,1,0:T(1,128)S(4)}, s32[1,2,8]{2,1,0:T(2,128)S(4)}, bf16[16,6,128,256]{3,2,1,0:T(8,128)(2,1)S(1)}, f32[16,2,2,64,128]{4,3,2,1,0:T(...) custom-call(s32[6,1,16]{2,1,0:T(1,128)} %bitcast.4, s32[1,2,8]{2,1,0:T(2,128)} %bitcast.5, ...), custom_call_target="tpu_custom_call" | custom-call | tf_op jit(solution)/shard_map/pallas_call | solution.py:303
  2.9 0.7 collective-permute-start
  3.6 0.1 shard_map.56
  3.7 0.7 collective-permute-start.1
  4.4 0.1 shard_map.57
  4.4 0.7 collective-permute-start.2
  5.1 0.0 collective-permute-done.refs_3_
  5.1 0.1 shard_map.58
  5.2 0.7 collective-permute-start.3
  5.9 0.0 collective-permute-done.1.refs_3_
  5.9 0.1 shard_map.59
  6.0 0.7 collective-permute-start.4
  6.7 0.0 collective-permute-done.2.refs_3_
  6.7 0.1 shard_map.60
  6.8 0.7 collective-permute-start.5
  7.4 0.1 shard_map.61
  7.5 0.7 collective-permute-start.6
  8.2 0.0 collective-permute-done.4.refs_3_
  8.2 0.7 collective-permute-start.7
  8.9 0.0 collective-permute-done.5.refs_3_
  9.0 0.7 collective-permute-start.8
  9.7 0.7 collective-permute-start.9
  10.4 0.7 collective-permute-start.10
  11.1 0.2 shard_map.66
  11.3 0.7 collective-permute-start.11
  12.1 0.7 collective-permute-start.12
  12.8 0.7 collective-permute-start.13
  13.5 0.7 collective-permute-start.14
  14.2 0.7 collective-permute-start.15
  15.0 0.7 collective-permute-start.16
  15.7 0.7 collective-permute-start.17
  16.4 1.3 %collective-permute-start.18 = (f32[16,2,16,128]{3,2,1,0:T(8,128)S(1)}, f32[16,2,16,128]{3,2,1,0:T(8,128)S(1)}, u32[]{:S(2)}, u32[]{:S(2)}) collective-permute-start(f32[16,2,16,128]{3,2,1,0:T(8,128)S(1)} %get-tuple-element.125), channel_id=1, source_target_pairs={{16,20},{20,24},{24,28},{17,21},{21,25},{25,29},{18,22},{22,26},{2... | collective-permute-start | bytes 786440 | tf_op jit(solution)/shard_map/ppermute | solution.py:325
  17.8 1.3 %collective-permute-start.19 = (f32[16,2,16,128]{3,2,1,0:T(8,128)S(1)}, f32[16,2,16,128]{3,2,1,0:T(8,128)S(1)}, u32[]{:S(2)}, u32[]{:S(2)}) collective-permute-start(f32[16,2,16,128]{3,2,1,0:T(8,128)S(1)} %get-tuple-element.127), channel_id=1, source_target_pairs={{16,20},{20,24},{24,28},{17,21},{21,25},{25,29},{18,22},{22,26},{2... | collective-permute-start | bytes 786440 | tf_op jit(solution)/shard_map/ppermute | solution.py:325
  19.1 1.3 %collective-permute-start.20 = (f32[16,2,16,128]{3,2,1,0:T(8,128)S(1)}, f32[16,2,16,128]{3,2,1,0:T(8,128)S(1)}, u32[]{:S(2)}, u32[]{:S(2)}) collective-permute-start(f32[16,2,16,128]{3,2,1,0:T(8,128)S(1)} %get-tuple-element.129), channel_id=1, source_target_pairs={{20,24},{24,28},{21,25},{25,29},{22,26},{26,30},{23,27},{27,31}} | collective-permute-start | bytes 786440 | tf_op jit(solution)/shard_map/ppermute | solution.py:325
  20.4 23.6 %collective-permute-done.18.refs_3_ = f32[16,2,16,128]{3,2,1,0:T(8,128)S(1)} collective-permute-done((f32[16,2,16,128]{3,2,1,0:T(8,128)S(1)}, f32[16,2,16,128]{3,2,1,0:T(8,128)S(1)}, u32[]{:S(2)}, u32[]{:S(2)}) %collective-permute-start.18) | collective-permute-done | bytes 262176 | tf_op jit(solution)/shard_map/ppermute | solution.py:325
  44.0 1.2 %shard_map.76 = (f32[16,2,2,64,128]{4,3,2,1,0:T(8,128)S(1)}, f32[16,2,16,128]{3,2,1,0:T(8,128)S(1)}) custom-call(s32[6,1,16]{2,1,0:T(1,128)S(4)} %get-tuple-element.77.refs_0_, bf16[16,6,128,256]{3,2,1,0:T(8,128)(2,1)S(1)} %get-tuple-element.78.refs_1_, f32[16,2,2,64,128]{4,3,2,1,0:T(8,128)S(1)} %get-tuple-element.124.refs_2_, ...), custom_call_target="tpu_custom_call", output_to_operand_aliasing={{0}: (2, {})} | custom-call | tf_op jit(solution)/shard_map/pallas_call | solution.py:303
  45.2 1.3 %collective-permute-start.21 = (f32[16,2,16,128]{3,2,1,0:T(8,128)S(1)}, f32[16,2,16,128]{3,2,1,0:T(8,128)S(1)}, u32[]{:S(2)}, u32[]{:S(2)}) collective-permute-start(f32[16,2,16,128]{3,2,1,0:T(8,128)S(1)} %get-tuple-element.131), channel_id=1, source_target_pairs={{20,24},{24,28},{21,25},{25,29},{22,26},{26,30},{23,27},{27,31}} | collective-permute-start | bytes 786440 | tf_op jit(solution)/shard_map/ppermute | solution.py:325
  46.5 0.7 collective-permute-done.19.refs_3_
  47.2 1.2 %shard_map.77 = (f32[16,2,2,64,128]{4,3,2,1,0:T(8,128)S(1)}, f32[16,2,16,128]{3,2,1,0:T(8,128)S(1)}) custom-call(s32[6,1,16]{2,1,0:T(1,128)S(4)} %get-tuple-element.77.refs_0_, bf16[16,6,128,256]{3,2,1,0:T(8,128)(2,1)S(1)} %get-tuple-element.78.refs_1_, f32[16,2,2,64,128]{4,3,2,1,0:T(8,128)S(1)} %get-tuple-element.126.refs_2_, ...), custom_call_target="tpu_custom_call", output_to_operand_aliasing={{0}: (2, {})} | custom-call | tf_op jit(solution)/shard_map/pallas_call | solution.py:303
  48.4 1.3 %collective-permute-start.22 = (f32[16,2,16,128]{3,2,1,0:T(8,128)S(1)}, f32[16,2,16,128]{3,2,1,0:T(8,128)S(1)}, u32[]{:S(2)}, u32[]{:S(2)}) collective-permute-start(f32[16,2,16,128]{3,2,1,0:T(8,128)S(1)} %get-tuple-element.133), channel_id=1, source_target_pairs={{20,24},{24,28},{21,25},{25,29},{22,26},{26,30},{23,27},{27,31}} | collective-permute-start | bytes 786440 | tf_op jit(solution)/shard_map/ppermute | solution.py:325
  49.7 0.8 %collective-permute-done.20.refs_3_ = f32[16,2,16,128]{3,2,1,0:T(8,128)S(1)} collective-permute-done((f32[16,2,16,128]{3,2,1,0:T(8,128)S(1)}, f32[16,2,16,128]{3,2,1,0:T(8,128)S(1)}, u32[]{:S(2)}, u32[]{:S(2)}) %collective-permute-start.20) | collective-permute-done | bytes 262176 | tf_op jit(solution)/shard_map/ppermute | solution.py:325
  50.6 1.2 %shard_map.78 = (f32[16,2,2,64,128]{4,3,2,1,0:T(8,128)S(1)}, f32[16,2,16,128]{3,2,1,0:T(8,128)S(1)}) custom-call(s32[6,1,16]{2,1,0:T(1,128)S(4)} %get-tuple-element.77.refs_0_, bf16[16,6,128,256]{3,2,1,0:T(8,128)(2,1)S(1)} %get-tuple-element.78.refs_1_, f32[16,2,2,64,128]{4,3,2,1,0:T(8,128)S(1)} %get-tuple-element.128.refs_2_, ...), custom_call_target="tpu_custom_call", output_to_operand_aliasing={{0}: (2, {})} | custom-call | tf_op jit(solution)/shard_map/pallas_call | solution.py:303
  51.8 1.3 %collective-permute-start.23 = (f32[16,2,16,128]{3,2,1,0:T(8,128)S(1)}, f32[16,2,16,128]{3,2,1,0:T(8,128)S(1)}, u32[]{:S(2)}, u32[]{:S(2)}) collective-permute-start(f32[16,2,16,128]{3,2,1,0:T(8,128)S(1)} %get-tuple-element.135), channel_id=1, source_target_pairs={{24,28},{25,29},{26,30},{27,31}} | collective-permute-start | bytes 786440 | tf_op jit(solution)/shard_map/ppermute | solution.py:325
  53.1 0.7 collective-permute-done.21.refs_3_
  53.8 1.4 %shard_map.79 = (f32[16,2,2,64,128]{4,3,2,1,0:T(8,128)S(1)}, f32[16,2,16,128]{3,2,1,0:T(8,128)S(1)}) custom-call(s32[6,1,16]{2,1,0:T(1,128)S(4)} %get-tuple-element.77.refs_0_, bf16[16,6,128,256]{3,2,1,0:T(8,128)(2,1)S(1)} %get-tuple-element.78.refs_1_, f32[16,2,2,64,128]{4,3,2,1,0:T(8,128)S(1)} %get-tuple-element.130.refs_2_, ...), custom_call_target="tpu_custom_call", output_to_operand_aliasing={{0}: (2, {})} | custom-call | tf_op jit(solution)/shard_map/pallas_call | solution.py:303
  55.2 1.3 %collective-permute-start.24 = (f32[16,2,16,128]{3,2,1,0:T(8,128)S(1)}, f32[16,2,16,128]{3,2,1,0:T(8,128)S(1)}, u32[]{:S(2)}, u32[]{:S(2)}) collective-permute-start(f32[16,2,16,128]{3,2,1,0:T(8,128)S(1)} %get-tuple-element.136), channel_id=1, source_target_pairs={{24,28},{25,29},{26,30},{27,31}} | collective-permute-start | bytes 786440 | tf_op jit(solution)/shard_map/ppermute | solution.py:325
  56.5 0.5 collective-permute-done.22.refs_3_
  57.0 1.2 %shard_map.80 = (f32[16,2,2,64,128]{4,3,2,1,0:T(8,128)S(1)}, f32[16,2,16,128]{3,2,1,0:T(8,128)S(1)}) custom-call(s32[6,1,16]{2,1,0:T(1,128)S(4)} %get-tuple-element.77.refs_0_, bf16[16,6,128,256]{3,2,1,0:T(8,128)(2,1)S(1)} %get-tuple-element.78.refs_1_, f32[16,2,2,64,128]{4,3,2,1,0:T(8,128)S(1)} %get-tuple-element.132.refs_2_, ...), custom_call_target="tpu_custom_call", output_to_operand_aliasing={{0}: (2, {})} | custom-call | tf_op jit(solution)/shard_map/pallas_call | solution.py:303
  58.3 1.3 %collective-permute-start.25 = (f32[16,2,16,128]{3,2,1,0:T(8,128)S(1)}, f32[16,2,16,128]{3,2,1,0:T(8,128)S(1)}, u32[]{:S(2)}, u32[]{:S(2)}) collective-permute-start(f32[16,2,16,128]{3,2,1,0:T(8,128)S(1)} %get-tuple-element.138), channel_id=1, source_target_pairs={{24,28},{25,29},{26,30},{27,31}} | collective-permute-start | bytes 786440 | tf_op jit(solution)/shard_map/ppermute | solution.py:325
  59.6 0.0 collective-permute-done.23.refs_3_
  59.6 1.2 %shard_map.81.refs_2_ = f32[16,2,2,64,128]{4,3,2,1,0:T(8,128)S(1)} custom-call(s32[6,1,16]{2,1,0:T(1,128)S(4)} %get-tuple-element.77.refs_0_, bf16[16,6,128,256]{3,2,1,0:T(8,128)(2,1)S(1)} %get-tuple-element.78.refs_1_, f32[16,2,2,64,128]{4,3,2,1,0:T(8,128)S(1)} %get-tuple-element.134.refs_2_, ...), custom_call_target="tpu_custom_call", output_to_operand_aliasing={{}: (2, {})} | custom-call | tf_op jit(solution)/shard_map/pallas_call | solution.py:303
  60.8 1.5 %collective-permute-done.24.refs_3_ = f32[16,2,16,128]{3,2,1,0:T(8,128)S(1)} collective-permute-done((f32[16,2,16,128]{3,2,1,0:T(8,128)S(1)}, f32[16,2,16,128]{3,2,1,0:T(8,128)S(1)}, u32[]{:S(2)}, u32[]{:S(2)}) %collective-permute-start.24) | collective-permute-done | bytes 262176 | tf_op jit(solution)/shard_map/ppermute | solution.py:325
  62.3 1.2 %shard_map.82.kept_in = f32[16,2,2,64,128]{4,3,2,1,0:T(8,128)S(1)} custom-call(s32[6,1,16]{2,1,0:T(1,128)S(4)} %get-tuple-element.77.refs_0_, bf16[16,6,128,256]{3,2,1,0:T(8,128)(2,1)S(1)} %get-tuple-element.78.refs_1_, f32[16,2,2,64,128]{4,3,2,1,0:T(8,128)S(1)} %shard_map.81.refs_2_, ...), custom_call_target="tpu_custom_call", output_to_operand_aliasing={{}: (2, {})} | custom-call | tf_op jit(solution)/shard_map/pallas_call | solution.py:303
  63.6 0.4 shard_map.83
  64.0 1.3 %collective-permute-done.25.refs_3_ = f32[16,2,16,128]{3,2,1,0:T(8,128)S(1)} collective-permute-done((f32[16,2,16,128]{3,2,1,0:T(8,128)S(1)}, f32[16,2,16,128]{3,2,1,0:T(8,128)S(1)}, u32[]{:S(2)}, u32[]{:S(2)}) %collective-permute-start.25) | collective-permute-done | bytes 262176 | tf_op jit(solution)/shard_map/ppermute | solution.py:325
  65.3 1.2 %shard_map.84.kept = f32[16,2,2,64,128]{4,3,2,1,0:T(8,128)S(1)} custom-call(s32[6,1,16]{2,1,0:T(1,128)S(4)} %get-tuple-element.77.refs_0_, bf16[16,6,128,256]{3,2,1,0:T(8,128)(2,1)S(1)} %get-tuple-element.78.refs_1_, f32[16,2,2,64,128]{4,3,2,1,0:T(8,128)S(1)} %get-tuple-element.137.refs_2_, ...), custom_call_target="tpu_custom_call", output_to_operand_aliasing={{}: (2, {})} | custom-call | tf_op jit(solution)/shard_map/pallas_call | solution.py:303
  66.5 0.3 shard_map.85
  66.8 1.4 %collective-permute-start.26 = (f32[2,128,128]{2,1,0:T(8,128)S(1)}, f32[2,128,128]{2,1,0:T(8,128)S(1)}, u32[]{:S(2)}, u32[]{:S(2)}) collective-permute-start(f32[2,128,128]{2,1,0:T(8,128)S(1)} %get-tuple-element.144), channel_id=1, source_target_pairs={{0,1},{1,2},{2,3},{3,0},{4,5},{5,6},{6,7},{7,4},{8,9},{9,10},{10,1... | collective-permute-start | bytes 393224 | tf_op jit(solution)/shard_map/ppermute | solution.py:341
  68.2 1.1 %collective-permute-start.27 = (f32[2,128,128]{2,1,0:T(8,128)S(1)}, f32[2,128,128]{2,1,0:T(8,128)S(1)}, u32[]{:S(2)}, u32[]{:S(2)}) collective-permute-start(f32[2,128,128]{2,1,0:T(8,128)S(1)} %get-tuple-element.145), channel_id=1, source_target_pairs={{0,2},{1,3},{2,0},{3,1},{4,6},{5,7},{6,4},{7,5},{8,10},{9,11},{10,... | collective-permute-start | bytes 393224 | tf_op jit(solution)/shard_map/ppermute | solution.py:341
  69.3 1.4 %collective-permute-start.28 = (f32[2,128,128]{2,1,0:T(8,128)S(1)}, f32[2,128,128]{2,1,0:T(8,128)S(1)}, u32[]{:S(2)}, u32[]{:S(2)}) collective-permute-start(f32[2,128,128]{2,1,0:T(8,128)S(1)} %get-tuple-element.146), channel_id=1, source_target_pairs={{0,3},{1,0},{2,1},{3,2},{4,7},{5,4},{6,5},{7,6},{8,11},{9,8},{10,9... | collective-permute-start | bytes 393224 | tf_op jit(solution)/shard_map/ppermute | solution.py:341
  70.7 6.3 %collective-permute-done.26 = f32[2,128,128]{2,1,0:T(8,128)S(1)} collective-permute-done((f32[2,128,128]{2,1,0:T(8,128)S(1)}, f32[2,128,128]{2,1,0:T(8,128)S(1)}, u32[]{:S(2)}, u32[]{:S(2)}) %collective-permute-start.26) | collective-permute-done | bytes 131104 | tf_op jit(solution)/shard_map/ppermute | solution.py:341
  76.9 2.4 %collective-permute-done.27 = f32[2,128,128]{2,1,0:T(8,128)S(1)} collective-permute-done((f32[2,128,128]{2,1,0:T(8,128)S(1)}, f32[2,128,128]{2,1,0:T(8,128)S(1)}, u32[]{:S(2)}, u32[]{:S(2)}) %collective-permute-start.27) | collective-permute-done | bytes 131104 | tf_op jit(solution)/shard_map/ppermute | solution.py:341
  79.3 1.5 %collective-permute-done.28 = f32[2,128,128]{2,1,0:T(8,128)S(1)} collective-permute-done((f32[2,128,128]{2,1,0:T(8,128)S(1)}, f32[2,128,128]{2,1,0:T(8,128)S(1)}, u32[]{:S(2)}, u32[]{:S(2)}) %collective-permute-start.28) | collective-permute-done | bytes 131104 | tf_op jit(solution)/shard_map/ppermute | solution.py:341
  80.8 0.7 add_bitcast_fusion
  (26 shorter events, 0.3 us)
Async XLA Ops:
  2.9 2.2 %collective-permute-start = (f32[16,2,16,128]{3,2,1,0:T(8,128)S(1)}, f32[16,2,16,128]{3,2,1,0:T(8,128)S(1)}, u32[]{:S(2)}, u32[]{:S(2)}) collective-permute-start(f32[16,2,16,128]{3,2,1,0:T(8,128)S(1)} %get-tuple-element.84), channel_id=1, source_target_pairs={{0,4},{1,5},{2,6},{3,7}} | collective-permute-start | bytes 786440 | tf_op jit(solution)/shard_map/ppermute | solution.py:325
  3.7 2.2 %collective-permute-start.1 = (f32[16,2,16,128]{3,2,1,0:T(8,128)S(1)}, f32[16,2,16,128]{3,2,1,0:T(8,128)S(1)}, u32[]{:S(2)}, u32[]{:S(2)}) collective-permute-start(f32[16,2,16,128]{3,2,1,0:T(8,128)S(1)} %get-tuple-element.87), channel_id=1, source_target_pairs={{0,4},{1,5},{2,6},{3,7}} | collective-permute-start | bytes 786440 | tf_op jit(solution)/shard_map/ppermute | solution.py:325
  4.4 2.2 %collective-permute-start.2 = (f32[16,2,16,128]{3,2,1,0:T(8,128)S(1)}, f32[16,2,16,128]{3,2,1,0:T(8,128)S(1)}, u32[]{:S(2)}, u32[]{:S(2)}) collective-permute-start(f32[16,2,16,128]{3,2,1,0:T(8,128)S(1)} %get-tuple-element.90), channel_id=1, source_target_pairs={{0,4},{1,5},{2,6},{3,7}} | collective-permute-start | bytes 786440 | tf_op jit(solution)/shard_map/ppermute | solution.py:325
  5.2 2.2 %collective-permute-start.3 = (f32[16,2,16,128]{3,2,1,0:T(8,128)S(1)}, f32[16,2,16,128]{3,2,1,0:T(8,128)S(1)}, u32[]{:S(2)}, u32[]{:S(2)}) collective-permute-start(f32[16,2,16,128]{3,2,1,0:T(8,128)S(1)} %get-tuple-element.93), channel_id=1, source_target_pairs={{0,4},{4,8},{1,5},{5,9},{2,6},{6,10},{3,7},{7,11}} | collective-permute-start | bytes 786440 | tf_op jit(solution)/shard_map/ppermute | solution.py:325
  6.0 2.2 %collective-permute-start.4 = (f32[16,2,16,128]{3,2,1,0:T(8,128)S(1)}, f32[16,2,16,128]{3,2,1,0:T(8,128)S(1)}, u32[]{:S(2)}, u32[]{:S(2)}) collective-permute-start(f32[16,2,16,128]{3,2,1,0:T(8,128)S(1)} %get-tuple-element.96), channel_id=1, source_target_pairs={{0,4},{4,8},{1,5},{5,9},{2,6},{6,10},{3,7},{7,11}} | collective-permute-start | bytes 786440 | tf_op jit(solution)/shard_map/ppermute | solution.py:325
  6.8 2.2 %collective-permute-start.5 = (f32[16,2,16,128]{3,2,1,0:T(8,128)S(1)}, f32[16,2,16,128]{3,2,1,0:T(8,128)S(1)}, u32[]{:S(2)}, u32[]{:S(2)}) collective-permute-start(f32[16,2,16,128]{3,2,1,0:T(8,128)S(1)} %get-tuple-element.99), channel_id=1, source_target_pairs={{0,4},{4,8},{1,5},{5,9},{2,6},{6,10},{3,7},{7,11}} | collective-permute-start | bytes 786440 | tf_op jit(solution)/shard_map/ppermute | solution.py:325
  7.5 2.1 %collective-permute-start.6 = (f32[16,2,16,128]{3,2,1,0:T(8,128)S(1)}, f32[16,2,16,128]{3,2,1,0:T(8,128)S(1)}, u32[]{:S(2)}, u32[]{:S(2)}) collective-permute-start(f32[16,2,16,128]{3,2,1,0:T(8,128)S(1)} %get-tuple-element.101), channel_id=1, source_target_pairs={{0,4},{4,8},{8,12},{1,5},{5,9},{9,13},{2,6},{6,10},{10,14},{3,7},{... | collective-permute-start | bytes 786440 | tf_op jit(solution)/shard_map/ppermute | solution.py:325
  8.2 2.1 %collective-permute-start.7 = (f32[16,2,16,128]{3,2,1,0:T(8,128)S(1)}, f32[16,2,16,128]{3,2,1,0:T(8,128)S(1)}, u32[]{:S(2)}, u32[]{:S(2)}) collective-permute-start(f32[16,2,16,128]{3,2,1,0:T(8,128)S(1)} %get-tuple-element.103), channel_id=1, source_target_pairs={{0,4},{4,8},{8,12},{1,5},{5,9},{9,13},{2,6},{6,10},{10,14},{3,7},{... | collective-permute-start | bytes 786440 | tf_op jit(solution)/shard_map/ppermute | solution.py:325
  9.0 2.1 %collective-permute-start.8 = (f32[16,2,16,128]{3,2,1,0:T(8,128)S(1)}, f32[16,2,16,128]{3,2,1,0:T(8,128)S(1)}, u32[]{:S(2)}, u32[]{:S(2)}) collective-permute-start(f32[16,2,16,128]{3,2,1,0:T(8,128)S(1)} %get-tuple-element.105), channel_id=1, source_target_pairs={{4,8},{8,12},{5,9},{9,13},{6,10},{10,14},{7,11},{11,15}} | collective-permute-start | bytes 786440 | tf_op jit(solution)/shard_map/ppermute | solution.py:325
  9.7 2.3 %collective-permute-start.9 = (f32[16,2,16,128]{3,2,1,0:T(8,128)S(1)}, f32[16,2,16,128]{3,2,1,0:T(8,128)S(1)}, u32[]{:S(2)}, u32[]{:S(2)}) collective-permute-start(f32[16,2,16,128]{3,2,1,0:T(8,128)S(1)} %get-tuple-element.107), channel_id=1, source_target_pairs={{4,8},{8,12},{12,16},{5,9},{9,13},{13,17},{6,10},{10,14},{14,18},{... | collective-permute-start | bytes 786440 | tf_op jit(solution)/shard_map/ppermute | solution.py:325
  10.4 2.3 %collective-permute-start.10 = (f32[16,2,16,128]{3,2,1,0:T(8,128)S(1)}, f32[16,2,16,128]{3,2,1,0:T(8,128)S(1)}, u32[]{:S(2)}, u32[]{:S(2)}) collective-permute-start(f32[16,2,16,128]{3,2,1,0:T(8,128)S(1)} %get-tuple-element.109), channel_id=1, source_target_pairs={{4,8},{8,12},{12,16},{5,9},{9,13},{13,17},{6,10},{10,14},{14,18},{... | collective-permute-start | bytes 786440 | tf_op jit(solution)/shard_map/ppermute | solution.py:325
  11.3 2.1 %collective-permute-start.11 = (f32[16,2,16,128]{3,2,1,0:T(8,128)S(1)}, f32[16,2,16,128]{3,2,1,0:T(8,128)S(1)}, u32[]{:S(2)}, u32[]{:S(2)}) collective-permute-start(f32[16,2,16,128]{3,2,1,0:T(8,128)S(1)} %get-tuple-element.111), channel_id=1, source_target_pairs={{8,12},{12,16},{9,13},{13,17},{10,14},{14,18},{11,15},{15,19}} | collective-permute-start | bytes 786440 | tf_op jit(solution)/shard_map/ppermute | solution.py:325
  12.1 2.1 %collective-permute-start.12 = (f32[16,2,16,128]{3,2,1,0:T(8,128)S(1)}, f32[16,2,16,128]{3,2,1,0:T(8,128)S(1)}, u32[]{:S(2)}, u32[]{:S(2)}) collective-permute-start(f32[16,2,16,128]{3,2,1,0:T(8,128)S(1)} %get-tuple-element.113), channel_id=1, source_target_pairs={{8,12},{12,16},{16,20},{9,13},{13,17},{17,21},{10,14},{14,18},{18,... | collective-permute-start | bytes 786440 | tf_op jit(solution)/shard_map/ppermute | solution.py:325
  12.8 2.1 %collective-permute-start.13 = (f32[16,2,16,128]{3,2,1,0:T(8,128)S(1)}, f32[16,2,16,128]{3,2,1,0:T(8,128)S(1)}, u32[]{:S(2)}, u32[]{:S(2)}) collective-permute-start(f32[16,2,16,128]{3,2,1,0:T(8,128)S(1)} %get-tuple-element.115), channel_id=1, source_target_pairs={{8,12},{12,16},{16,20},{9,13},{13,17},{17,21},{10,14},{14,18},{18,... | collective-permute-start | bytes 786440 | tf_op jit(solution)/shard_map/ppermute | solution.py:325
  13.5 2.1 %collective-permute-start.14 = (f32[16,2,16,128]{3,2,1,0:T(8,128)S(1)}, f32[16,2,16,128]{3,2,1,0:T(8,128)S(1)}, u32[]{:S(2)}, u32[]{:S(2)}) collective-permute-start(f32[16,2,16,128]{3,2,1,0:T(8,128)S(1)} %get-tuple-element.117), channel_id=1, source_target_pairs={{12,16},{16,20},{13,17},{17,21},{14,18},{18,22},{15,19},{19,23}} | collective-permute-start | bytes 786440 | tf_op jit(solution)/shard_map/ppermute | solution.py:325
  14.2 2.1 %collective-permute-start.15 = (f32[16,2,16,128]{3,2,1,0:T(8,128)S(1)}, f32[16,2,16,128]{3,2,1,0:T(8,128)S(1)}, u32[]{:S(2)}, u32[]{:S(2)}) collective-permute-start(f32[16,2,16,128]{3,2,1,0:T(8,128)S(1)} %get-tuple-element.119), channel_id=1, source_target_pairs={{12,16},{16,20},{20,24},{13,17},{17,21},{21,25},{14,18},{18,22},{2... | collective-permute-start | bytes 786440 | tf_op jit(solution)/shard_map/ppermute | solution.py:325
  15.0 2.8 %collective-permute-start.16 = (f32[16,2,16,128]{3,2,1,0:T(8,128)S(1)}, f32[16,2,16,128]{3,2,1,0:T(8,128)S(1)}, u32[]{:S(2)}, u32[]{:S(2)}) collective-permute-start(f32[16,2,16,128]{3,2,1,0:T(8,128)S(1)} %get-tuple-element.121), channel_id=1, source_target_pairs={{12,16},{16,20},{20,24},{13,17},{17,21},{21,25},{14,18},{18,22},{2... | collective-permute-start | bytes 786440 | tf_op jit(solution)/shard_map/ppermute | solution.py:325
  15.7 3.4 %collective-permute-start.17 = (f32[16,2,16,128]{3,2,1,0:T(8,128)S(1)}, f32[16,2,16,128]{3,2,1,0:T(8,128)S(1)}, u32[]{:S(2)}, u32[]{:S(2)}) collective-permute-start(f32[16,2,16,128]{3,2,1,0:T(8,128)S(1)} %get-tuple-element.123), channel_id=1, source_target_pairs={{16,20},{20,24},{17,21},{21,25},{18,22},{22,26},{19,23},{23,27}} | collective-permute-start | bytes 786440 | tf_op jit(solution)/shard_map/ppermute | solution.py:325
  16.4 27.6 %collective-permute-start.18 = (f32[16,2,16,128]{3,2,1,0:T(8,128)S(1)}, f32[16,2,16,128]{3,2,1,0:T(8,128)S(1)}, u32[]{:S(2)}, u32[]{:S(2)}) collective-permute-start(f32[16,2,16,128]{3,2,1,0:T(8,128)S(1)} %get-tuple-element.125), channel_id=1, source_target_pairs={{16,20},{20,24},{24,28},{17,21},{21,25},{25,29},{18,22},{22,26},{2... | collective-permute-start | bytes 786440 | tf_op jit(solution)/shard_map/ppermute | solution.py:325
  17.8 29.4 %collective-permute-start.19 = (f32[16,2,16,128]{3,2,1,0:T(8,128)S(1)}, f32[16,2,16,128]{3,2,1,0:T(8,128)S(1)}, u32[]{:S(2)}, u32[]{:S(2)}) collective-permute-start(f32[16,2,16,128]{3,2,1,0:T(8,128)S(1)} %get-tuple-element.127), channel_id=1, source_target_pairs={{16,20},{20,24},{24,28},{17,21},{21,25},{25,29},{18,22},{22,26},{2... | collective-permute-start | bytes 786440 | tf_op jit(solution)/shard_map/ppermute | solution.py:325
  19.1 31.5 %collective-permute-start.20 = (f32[16,2,16,128]{3,2,1,0:T(8,128)S(1)}, f32[16,2,16,128]{3,2,1,0:T(8,128)S(1)}, u32[]{:S(2)}, u32[]{:S(2)}) collective-permute-start(f32[16,2,16,128]{3,2,1,0:T(8,128)S(1)} %get-tuple-element.129), channel_id=1, source_target_pairs={{20,24},{24,28},{21,25},{25,29},{22,26},{26,30},{23,27},{27,31}} | collective-permute-start | bytes 786440 | tf_op jit(solution)/shard_map/ppermute | solution.py:325
  45.2 8.6 %collective-permute-start.21 = (f32[16,2,16,128]{3,2,1,0:T(8,128)S(1)}, f32[16,2,16,128]{3,2,1,0:T(8,128)S(1)}, u32[]{:S(2)}, u32[]{:S(2)}) collective-permute-start(f32[16,2,16,128]{3,2,1,0:T(8,128)S(1)} %get-tuple-element.131), channel_id=1, source_target_pairs={{20,24},{24,28},{21,25},{25,29},{22,26},{26,30},{23,27},{27,31}} | collective-permute-start | bytes 786440 | tf_op jit(solution)/shard_map/ppermute | solution.py:325
  48.4 8.6 %collective-permute-start.22 = (f32[16,2,16,128]{3,2,1,0:T(8,128)S(1)}, f32[16,2,16,128]{3,2,1,0:T(8,128)S(1)}, u32[]{:S(2)}, u32[]{:S(2)}) collective-permute-start(f32[16,2,16,128]{3,2,1,0:T(8,128)S(1)} %get-tuple-element.133), channel_id=1, source_target_pairs={{20,24},{24,28},{21,25},{25,29},{22,26},{26,30},{23,27},{27,31}} | collective-permute-start | bytes 786440 | tf_op jit(solution)/shard_map/ppermute | solution.py:325
  51.8 7.8 %collective-permute-start.23 = (f32[16,2,16,128]{3,2,1,0:T(8,128)S(1)}, f32[16,2,16,128]{3,2,1,0:T(8,128)S(1)}, u32[]{:S(2)}, u32[]{:S(2)}) collective-permute-start(f32[16,2,16,128]{3,2,1,0:T(8,128)S(1)} %get-tuple-element.135), channel_id=1, source_target_pairs={{24,28},{25,29},{26,30},{27,31}} | collective-permute-start | bytes 786440 | tf_op jit(solution)/shard_map/ppermute | solution.py:325
  55.2 7.1 %collective-permute-start.24 = (f32[16,2,16,128]{3,2,1,0:T(8,128)S(1)}, f32[16,2,16,128]{3,2,1,0:T(8,128)S(1)}, u32[]{:S(2)}, u32[]{:S(2)}) collective-permute-start(f32[16,2,16,128]{3,2,1,0:T(8,128)S(1)} %get-tuple-element.136), channel_id=1, source_target_pairs={{24,28},{25,29},{26,30},{27,31}} | collective-permute-start | bytes 786440 | tf_op jit(solution)/shard_map/ppermute | solution.py:325
  58.3 7.1 %collective-permute-start.25 = (f32[16,2,16,128]{3,2,1,0:T(8,128)S(1)}, f32[16,2,16,128]{3,2,1,0:T(8,128)S(1)}, u32[]{:S(2)}, u32[]{:S(2)}) collective-permute-start(f32[16,2,16,128]{3,2,1,0:T(8,128)S(1)} %get-tuple-element.138), channel_id=1, source_target_pairs={{24,28},{25,29},{26,30},{27,31}} | collective-permute-start | bytes 786440 | tf_op jit(solution)/shard_map/ppermute | solution.py:325
  66.8 10.1 %collective-permute-start.26 = (f32[2,128,128]{2,1,0:T(8,128)S(1)}, f32[2,128,128]{2,1,0:T(8,128)S(1)}, u32[]{:S(2)}, u32[]{:S(2)}) collective-permute-start(f32[2,128,128]{2,1,0:T(8,128)S(1)} %get-tuple-element.144), channel_id=1, source_target_pairs={{0,1},{1,2},{2,3},{3,0},{4,5},{5,6},{6,7},{7,4},{8,9},{9,10},{10,1... | collective-permute-start | bytes 393224 | tf_op jit(solution)/shard_map/ppermute | solution.py:341
  68.2 11.1 %collective-permute-start.27 = (f32[2,128,128]{2,1,0:T(8,128)S(1)}, f32[2,128,128]{2,1,0:T(8,128)S(1)}, u32[]{:S(2)}, u32[]{:S(2)}) collective-permute-start(f32[2,128,128]{2,1,0:T(8,128)S(1)} %get-tuple-element.145), channel_id=1, source_target_pairs={{0,2},{1,3},{2,0},{3,1},{4,6},{5,7},{6,4},{7,5},{8,10},{9,11},{10,... | collective-permute-start | bytes 393224 | tf_op jit(solution)/shard_map/ppermute | solution.py:341
  69.3 11.5 %collective-permute-start.28 = (f32[2,128,128]{2,1,0:T(8,128)S(1)}, f32[2,128,128]{2,1,0:T(8,128)S(1)}, u32[]{:S(2)}, u32[]{:S(2)}) collective-permute-start(f32[2,128,128]{2,1,0:T(8,128)S(1)} %get-tuple-element.146), channel_id=1, source_target_pairs={{0,3},{1,0},{2,1},{3,2},{4,7},{5,4},{6,5},{7,6},{8,11},{9,8},{10,9... | collective-permute-start | bytes 393224 | tf_op jit(solution)/shard_map/ppermute | solution.py:341
